TPU v7x, 256 devices: a whole 4x4x8 slice. The times are simulated.
256 devices in a mesh: gz: 4 (over x), gx: 16 (over z, core), gy: 4 (over y).
Axes of the slice: x: 4, y: 4, z: 8, core: 2. Of those that a mesh axis runs over, the one named last changes fastest.
Arguments:
- initial_heat_state: float32 [32, 512, 1024], P('gz', 'gx', 'gy'), may hold values from -6 to 6
- flow_speed_components: bfloat16 [3, 32, 512, 1024], P(None, 'gz', 'gx', 'gy'), may hold values from -4 to 4
- heat_spread_rate: float32 [32, 512, 1024], P('gz', 'gx', 'gy'), may hold values from 0.001 to 4
Outputs:
- advanced: float32 [32, 512, 1024], P('gz', 'gx', 'gy')
All inputs are finite; a program needn't handle non-finite values.
Results may differ from a plain program's by a relative error of at most 0.0003.
Values sent between devices are 32-bit elements; how exact they have to be, the bound alone decides.
No kernel may reach another device: no remote copies, remote signals or barrier semaphores. Data moves between devices by JAX's collectives and lax.ppermute only.
A program may use at most 192 MiB of HBM per device.

v0:
```python
import functools
import jax
import jax.numpy as jnp
from jax import lax
from jax.experimental import pallas as pl
from jax.experimental.pallas import tpu as pltpu
from jax.sharding import PartitionSpec as P


QUARTER = 0.25
VERTICAL = 0.06
VMEM_BYTES = 24 * 2**20


def call(kernel, outs, *ins, name, flops=0):
    shapes = [jax.ShapeDtypeStruct(s, jnp.float32) for s in outs]
    vm = pl.BlockSpec(memory_space=pltpu.VMEM)
    size = 4 * (sum(x.size for x in ins) + sum(x.size for x in shapes))
    return pl.pallas_call(
        kernel,
        out_shape=shapes,
        in_specs=[vm] * len(ins),
        out_specs=[vm] * len(outs),
        compiler_params=pltpu.CompilerParams(vmem_limit_bytes=VMEM_BYTES),
        cost_estimate=pl.CostEstimate(flops=flops, bytes_accessed=size, transcendentals=0),
        name=name,
    )(*ins)


def merge(a, b):
    a0, a1, aL, aC, aR = a
    b0, b1, bL, bC, bR = b
    inv = 1.0 / (1.0 - aR * bL)
    x = aC * inv
    y = bC * inv
    return (
        a0 + x * (b0 + bL * a1),
        b1 + y * (a1 + aR * b0),
        aL + x * bL * aC,
        x * bC,
        bR + y * aR * bC,
    )


def close_left(p, g, block):
    b0, b1, bL, bC, bR = block
    f = bC / (1.0 - bL * g)
    return b1 + bC * p + f * g * (b0 + bL * p), bR + f * g * bC


def close_right(p, g, block):
    b0, b1, bL, bC, bR = block
    f = bC / (1.0 - bR * g)
    return b0 + bC * p + f * g * (b1 + bR * p), bL + f * g * bC


def chain_ends(blocks, index):
    zero = jnp.zeros_like(blocks[0][0])
    p, g = zero, zero
    lp, lg = zero, zero
    for m in range(len(blocks) - 1):
        p, g = close_left(p, g, blocks[m])
        here = index == m + 1
        lp, lg = jnp.where(here, p, lp), jnp.where(here, g, lg)
    p, g = zero, zero
    rp, rg = zero, zero
    for m in range(len(blocks) - 1, 0, -1):
        p, g = close_right(p, g, blocks[m])
        here = index == m - 1
        rp, rg = jnp.where(here, p, rp), jnp.where(here, g, rg)
    return lp, lg, rp, rg


def factor(d_ref, w_ref, l_ref, r_ref, count):
    delta = 1.0 + d_ref[0]
    w = 1.0 / (1.0 + delta)
    w_ref[0] = w
    y = jnp.ones_like(w)
    l_ref[0] = y
    for i in range(1, count):
        y = y * w
        l_ref[i] = y
        delta = d_ref[i] + delta * w
        w = 1.0 / (1.0 + delta)
        w_ref[i] = w
    r = w
    s = w * y
    r_ref[count - 1] = r
    l_ref[count - 1] = s
    for i in range(count - 2, -1, -1):
        w = w_ref[i]
        r = w * r
        s = w * (l_ref[i] + s)
        r_ref[i] = r
        l_ref[i] = s


def sweep(q, w_ref, out_ref, count):
    y = q(0)
    out_ref[0] = y
    for i in range(1, count):
        y = q(i) + w_ref[i - 1] * y
        out_ref[i] = y
    s = w_ref[count - 1] * y
    out_ref[count - 1] = s
    for i in range(count - 2, -1, -1):
        s = w_ref[i] * (out_ref[i] + s)
        out_ref[i] = s


def pack(v, half, h):
    piece = v[h * half : (h + 1) * half]
    mid = v.shape[1] // 2
    return jnp.concatenate([piece[:, :mid], piece[:, mid:]], axis=0)


def unpack(v):
    half = v.shape[0] // 2
    return jnp.concatenate([v[:half], v[half:]], axis=1)


def stencil(z, f, below, above, west, east, ydiff, wind_ref, k):
    count = f.shape[0]
    row = lax.broadcasted_iota(jnp.int32, f.shape, 0)
    e = jnp.where(row == count - 1, east, pltpu.roll(f, count - 1, 0))
    w = jnp.where(row == 0, west, pltpu.roll(f, 1, 0))
    wz = wind_ref[0, z].astype(jnp.float32)
    wx = wind_ref[1, z].astype(jnp.float32)
    wy = wind_ref[2, z].astype(jnp.float32)
    return (
        f
        - QUARTER * (wz * (above - below) + wx * (e - w) + wy * ydiff)
        + VERTICAL * k * (above + below - 2.0 * f)
    )


def body(field, wind, rate):
    nz, nx, ny = field.shape
    lines = nz * nx
    members = lax.axis_size("gx")
    chips = members // 2
    levels = lax.axis_size("gz")
    columns = lax.axis_size("gy")
    reach = nx * members / 8.0
    c = reach * reach
    subs = 8
    steps = ny // subs
    half = nz // 2
    face = (2 * half, ny // 2)

    def core():
        return lax.rem(lax.axis_index("gx"), 2)

    def faces_kernel(f_ref, zlo, zhi, ylo, yhi, xc, xi):
        zlo[...] = f_ref[0]
        zhi[...] = f_ref[nz - 1]
        flat = f_ref[...].reshape(lines, ny)
        ylo[...] = flat[:, :128].T[:8]
        yhi[...] = flat[:, ny - 128 :].T[120:]
        first, last = f_ref[:, 0, :], f_ref[:, nx - 1, :]
        odd = core() == 1
        xc[...] = jnp.where(odd, last, first)
        xi[...] = jnp.where(odd, first, last)

    def up(a, axis):
        n = lax.axis_size(axis)
        return lax.ppermute(a, axis, [(i, (i + 1) % n) for i in range(n)])

    def down(a, axis):
        n = lax.axis_size(axis)
        return lax.ppermute(a, axis, [((i + 1) % n, i) for i in range(n)])

    def across(a):
        return lax.ppermute(a, "gx", [(i, (i + 1 if i % 2 else i - 1) % members) for i in range(members)])

    def sibling(a):
        return lax.ppermute(a, "gx", [(i, i ^ 1) for i in range(members)])

    def x_rows(cross, inner):
        index = lax.axis_index("gx")
        odd = core() == 1
        west = jnp.where(index == 0, 0.0, jnp.where(odd, inner, cross))
        east = jnp.where(index == members - 1, 0.0, jnp.where(odd, cross, inner))
        return west, east

    def z_planes(below, above):
        index = lax.axis_index("gz")
        return jnp.where(index == 0, 0.0, below), jnp.where(index == levels - 1, 0.0, above)

    def x_matrix_kernel(k_ref, d_ref, w_ref, l_ref, r_ref):
        d_ref[...] = 1.0 / (c * jnp.swapaxes(k_ref[...], 0, 1))
        factor(d_ref, w_ref, l_ref, r_ref, nx)

    def y_matrix_kernel(dx_ref, d_ref, w_ref, l_ref, r_ref, c_ref):
        d_ref[...] = jnp.swapaxes(dx_ref[...].reshape(lines, ny).T.reshape(subs, steps, lines), 0, 1)
        factor(d_ref, w_ref, l_ref, r_ref, steps)
        L, C, R = l_ref[0], r_ref[0], r_ref[steps - 1]
        for level in range(3):
            shift = subs - (1 << level)
            bL, bC, bR = pltpu.roll(L, shift, 0), pltpu.roll(C, shift, 0), pltpu.roll(R, shift, 0)
            inv = 1.0 / (1.0 - R * bL)
            x, y = C * inv, bC * inv
            for n, value in enumerate((x, y, bL, R, bC, inv, R * y)):
                c_ref[level, n] = value
            L, C, R = L + x * bL * C, x * bC, bR + y * R * bC
        c_ref[3, 0], c_ref[3, 1], c_ref[3, 2] = L, C, R

    def explicit_kernel(
        f_ref, wind_ref, k_ref, below, above, south, north, xc, xi, d_ref, w_ref, l_ref, r_ref,
        base_ref, mine_ref, send_ref, e_ref,
    ):
        west, east = x_rows(xc[...], xi[...])
        low, high = z_planes(below[...], above[...])
        gy = lax.axis_index("gy")
        left = jnp.where(gy == 0, 0.0, south[7:8])
        right = jnp.where(gy == columns - 1, 0.0, north[0:1])
        left = jnp.broadcast_to(left, (128, lines)).T
        right = jnp.broadcast_to(right, (128, lines)).T
        lane = lax.broadcasted_iota(jnp.int32, (nx, 128), 1)
        for z in range(nz):
            f = f_ref[z]
            rows = slice(z * nx, (z + 1) * nx)
            no = pltpu.roll(f, ny - 1, 1)
            so = pltpu.roll(f, 1, 1)
            no = jnp.concatenate([no[:, : ny - 128], jnp.where(lane == 127, right[rows], no[:, ny - 128 :])], axis=1)
            so = jnp.concatenate([jnp.where(lane == 0, left[rows], so[:, :128]), so[:, 128:]], axis=1)
            e_ref[z] = stencil(
                z, f,
                f_ref[z - 1] if z else low,
                f_ref[z + 1] if z < nz - 1 else high,
                west[z : z + 1], east[z : z + 1], no - so, wind_ref, k_ref[z],
            )
        e = jnp.swapaxes(e_ref[...], 0, 1)
        sweep(lambda i: e[i] * d_ref[i], w_ref, base_ref, nx)
        odd = core() == 1
        ends = (base_ref[0], base_ref[nx - 1], l_ref[0], r_ref[0], r_ref[nx - 1])
        for n, v in enumerate(ends):
            lo, hi = pack(v, half, 0), pack(v, half, 1)
            mine_ref[n] = jnp.where(odd, hi, lo)
            send_ref[n] = jnp.where(odd, lo, hi)

    def pair(mine_ref, got_ref):
        odd = core() == 1
        a = tuple(jnp.where(odd, got_ref[n], mine_ref[n]) for n in range(5))
        b = tuple(jnp.where(odd, mine_ref[n], got_ref[n]) for n in range(5))
        return a, b

    def chip_kernel(mine_ref, got_ref, out_ref):
        whole = merge(*pair(mine_ref, got_ref))
        for n in range(5):
            for m in range(chips):
                out_ref[m, n] = whole[n]

    def x_chain_kernel(all_ref, mine_ref, got_ref, own_ref, send_ref):
        a, b = pair(mine_ref, got_ref)
        blocks = [tuple(all_ref[m, n] for n in range(5)) for m in range(chips)]
        lp, lg, rp, rg = chain_ends(blocks, lax.axis_index("gx") // 2)
        ap, ag = close_left(lp, lg, a)
        bp, bg = close_right(rp, rg, b)
        last_a = (ap + ag * bp) / (1.0 - ag * bg)
        first_b = bp + bg * last_a
        first_a = (a[0] + a[2] * lp + a[3] * first_b) / (1.0 - a[2] * lg)
        last_b = (b[1] + b[4] * rp + b[3] * last_a) / (1.0 - b[4] * rg)
        outer_l = lp + lg * first_a
        outer_r = rp + rg * last_b
        odd = core() == 1
        own_ref[0] = jnp.where(odd, last_a, outer_l)
        own_ref[1] = jnp.where(odd, outer_r, first_b)
        send_ref[0] = jnp.where(odd, outer_l, last_a)
        send_ref[1] = jnp.where(odd, first_b, outer_r)

    def x_finish_kernel(
        own_ref, got_ref, base_ref, l_ref, r_ref, d_ref, w_ref, c_ref,
        ybase_ref, up_ref, send_ref, s_ref,
    ):
        odd = core() == 1
        sides = []
        for n in range(2):
            own, got = unpack(own_ref[n]), unpack(got_ref[n])
            sides.append(jnp.concatenate([jnp.where(odd, got, own), jnp.where(odd, own, got)], axis=0))
        for i in range(nx):
            s_ref[i] = base_ref[i] + l_ref[i] * sides[0] + r_ref[i] * sides[1]
        t = s_ref[...].reshape(lines, ny).T
        q = jnp.swapaxes(t.reshape(subs, steps, lines), 0, 1)
        sweep(lambda i: q[i] * d_ref[i], w_ref, ybase_ref, steps)
        b0, b1 = ybase_ref[0], ybase_ref[steps - 1]
        for level in range(3):
            shift = subs - (1 << level)
            o0, o1 = pltpu.roll(b0, shift, 0), pltpu.roll(b1, shift, 0)
            x, y, bL, aR, _, inv, _ = (c_ref[level, n] for n in range(7))
            inner = b1 + aR * o0
            up_ref[level, 0] = inner * inv
            up_ref[level, 1] = o0
            b0, b1 = b0 + x * (o0 + bL * b1), o1 + y * inner
        for n, v in enumerate((b0, b1, c_ref[3, 0], c_ref[3, 1], c_ref[3, 2])):
            send_ref[n : n + 1] = v[0:1]
        send_ref[5:8] = jnp.zeros((3, lines), jnp.float32)

    def y_finish_kernel(
        own_ref, *refs,
    ):
        got, (ybase_ref, up_ref, l_ref, r_ref, c_ref), (s_ref, yd_ref, xc, xi, zlo, zhi) = (
            refs[: columns - 1], refs[columns - 1 : columns + 4], refs[columns + 4 :],
        )
        index = lax.axis_index("gy")
        messages = [own_ref[...]] + [ref[...] for ref in got]
        blocks = []
        for m in range(columns):
            v = messages[0]
            for back in range(1, columns):
                v = jnp.where(lax.rem(index - m + columns, columns) == back, messages[back], v)
            blocks.append(tuple(v[n : n + 1] for n in range(5)))
        mine = tuple(messages[0][n : n + 1] for n in range(5))
        lp, lg, rp, rg = chain_ends(blocks, index)
        p, g = close_left(lp, lg, mine)
        last = (p + g * rp) / (1.0 - g * rg)
        right = rp + rg * last
        first = (mine[0] + mine[2] * lp + mine[3] * right) / (1.0 - mine[2] * lg)
        left = lp + lg * first
        sub = lax.broadcasted_iota(jnp.int32, (subs, lines), 0)
        L = jnp.broadcast_to(left, (subs, lines))
        R = jnp.broadcast_to(right, (subs, lines))
        for level in (2, 1, 0):
            step = 1 << level
            x, _, bL, _, bC, _, z = (c_ref[level, n] for n in range(7))
            a = up_ref[level, 0] + x * L + z * R
            b = up_ref[level, 1] + bL * a + bC * R
            upper = (sub & step) != 0
            L, R = (
                jnp.where(upper, pltpu.roll(a, step, 0), L),
                jnp.where(upper, pltpu.roll(R, step, 0), b),
            )
        for i in range(steps):
            ybase_ref_i = ybase_ref[i] + l_ref[i] * L + r_ref[i] * R
            yd_ref[i] = ybase_ref_i
        s = jnp.swapaxes(yd_ref[...].reshape(steps, subs, lines), 0, 1).reshape(ny, lines)
        row = lax.broadcasted_iota(jnp.int32, s.shape, 0)
        north = jnp.where(row == ny - 1, right, pltpu.roll(s, ny - 1, 0))
        south = jnp.where(row == 0, left, pltpu.roll(s, 1, 0))
        yd_ref[...] = (north - south).reshape(yd_ref.shape)
        t = s.T
        odd = core() == 1
        low, high = t[:nz], t[lines - nz :]
        xc[...] = jnp.where(odd, high, low)
        xi[...] = jnp.where(odd, low, high)
        s_ref[...] = jnp.swapaxes(t.reshape(nx, nz, ny), 0, 1)
        zlo[...] = s_ref[0]
        zhi[...] = s_ref[nz - 1]

    def turn_kernel(yd_ref, out_ref):
        out_ref[...] = jnp.swapaxes(yd_ref[...].reshape(ny, lines).T.reshape(nx, nz, ny), 0, 1)

    def final_kernel(s_ref, yd_ref, wind_ref, k_ref, below, above, xc, xi, out_ref):
        west, east = x_rows(xc[...], xi[...])
        low, high = z_planes(below[...], above[...])
        for z in range(nz):
            out_ref[z] = stencil(
                z, s_ref[z],
                s_ref[z - 1] if z else low,
                s_ref[z + 1] if z < nz - 1 else high,
                west[z : z + 1], east[z : z + 1], yd_ref[z], wind_ref, k_ref[z],
            )

    box, xbox, ybox = (nz, nx, ny), (nx, nz, ny), (steps, subs, lines)
    five = (5,) + face

    zlo, zhi, ylo, yhi, xc, xi = call(
        faces_kernel, [(nx, ny), (nx, ny), (8, lines), (8, lines), (nz, ny), (nz, ny)], field, name="faces"
    )
    xc, xi = across(xc), sibling(xi)
    below, above = up(zhi, "gz"), down(zlo, "gz")
    south, north = up(yhi, "gy"), down(ylo, "gy")
    dx, wx, lx, rx = call(x_matrix_kernel, [xbox] * 4, rate, name="x_matrix", flops=10**6)
    dy, wy, ly, ry, cy = call(y_matrix_kernel, [ybox] * 4 + [(4, 7, subs, lines)], dx, name="y_matrix", flops=10**6)
    base, mine, send, _ = call(
        explicit_kernel, [xbox, five, five, box],
        field, wind, rate, below, above, south, north, xc, xi, dx, wx, lx, rx, name="explicit",
    )
    got = sibling(send)
    (spread,) = call(chip_kernel, [(chips,) + five], mine, got, name="chip")
    groups = [[2 * m + k for m in range(chips)] for k in range(2)]
    everyone = lax.all_to_all(spread, "gx", 0, 0, axis_index_groups=groups, tiled=True)
    own, send = call(x_chain_kernel, [(2,) + face] * 2, everyone, mine, got, name="x_chain")
    got = sibling(send)
    ybase, ups, send, _ = call(
        x_finish_kernel, [ybox, (3, 2, subs, lines), (8, lines), xbox],
        own, got, base, lx, rx, dy, wy, cy, name="x_finish",
    )
    ring = [
        lax.ppermute(send, "gy", [(i, (i + back) % columns) for i in range(columns)])
        for back in range(1, columns)
    ]
    swept, yd, xc, xi, zlo, zhi = call(
        y_finish_kernel, [box, ybox, (nz, ny), (nz, ny), (nx, ny), (nx, ny)],
        send, *ring, ybase, ups, ly, ry, cy, name="y_finish",
    )
    xc, xi = across(xc), sibling(xi)
    below, above = up(zhi, "gz"), down(zlo, "gz")
    (ydiff,) = call(turn_kernel, [box], yd, name="turn", flops=10**6)
    (out,) = call(final_kernel, [box], swept, ydiff, wind, rate, below, above, xc, xi, name="final")
    return out


def solution(mesh):
    in_specs = (P("gz", "gx", "gy"), P(None, "gz", "gx", "gy"), P("gz", "gx", "gy"))
    out_specs = P("gz", "gx", "gy")
    return jax.shard_map(body, mesh=mesh, in_specs=in_specs, out_specs=out_specs, check_vma=False)
```

profile of v0, /device:TPU:1, one launch (start us, length us, event | category | flops | bytes accessed | tf_op | source)
XLA Modules:
  0.0 50.9 jit_solution(16286443377432555311)
XLA Ops:
  0.0 0.0 copy-start
  0.0 0.0 copy-start.3
  0.0 1.0 %copy-done.3 = f32[8,32,256]{2,1,0:T(8,128)S(1)} copy-done((f32[8,32,256]{2,1,0:T(8,128)S(1)}, f32[8,32,256]{2,1,0:T(8,128)}, u32[]{:S(2)}) %copy-start.3) | copy-done | bytes 262168
  1.0 0.1 faces.1
  1.1 2.1 %collective-permute-start = (f32[32,256]{1,0:T(8,128)S(1)}, f32[32,256]{1,0:T(8,128)S(1)}, u32[]{:S(2)}, u32[]{:S(2)}) collective-permute-start(f32[32,256]{1,0:T(8,128)S(1)} %get-tuple-element.34), channel_id=1, source_target_pairs={{0,64},{64,128},{128,192},{192,0},{1,65},{65,129},{129,193},{193,1... | collective-permute-start | bytes 98312 | tf_op jit(solution)/shard_map/ppermute | solution.py:167
  3.2 1.4 %collective-permute-start.1 = (f32[32,256]{1,0:T(8,128)S(1)}, f32[32,256]{1,0:T(8,128)S(1)}, u32[]{:S(2)}, u32[]{:S(2)}) collective-permute-start(f32[32,256]{1,0:T(8,128)S(1)} %get-tuple-element.35), channel_id=1, source_target_pairs={{64,0},{128,64},{192,128},{0,192},{65,1},{129,65},{193,129},{1,193... | collective-permute-start | bytes 98312 | tf_op jit(solution)/shard_map/ppermute | solution.py:171
  4.6 1.4 %collective-permute-start.2 = (f32[8,256]{1,0:T(8,128)S(1)}, f32[8,256]{1,0:T(8,128)S(1)}, u32[]{:S(2)}, u32[]{:S(2)}) collective-permute-start(f32[8,256]{1,0:T(8,128)S(1)} %get-tuple-element.36), channel_id=1, source_target_pairs={{0,1},{1,2},{2,3},{3,0},{4,5},{5,6},{6,7},{7,4},{8,9},{9,10},{10,1... | collective-permute-start | bytes 24584 | tf_op jit(solution)/shard_map/ppermute | solution.py:167
  6.0 1.4 %collective-permute-start.3 = (f32[8,256]{1,0:T(8,128)S(1)}, f32[8,256]{1,0:T(8,128)S(1)}, u32[]{:S(2)}, u32[]{:S(2)}) collective-permute-start(f32[8,256]{1,0:T(8,128)S(1)} %get-tuple-element.37), channel_id=1, source_target_pairs={{1,0},{2,1},{3,2},{0,3},{5,4},{6,5},{7,6},{4,7},{9,8},{10,9},{11,1... | collective-permute-start | bytes 24584 | tf_op jit(solution)/shard_map/ppermute | solution.py:171
  7.4 3.3 %collective-permute-start.4 = (f32[8,256]{1,0:T(8,128)S(1)}, f32[8,256]{1,0:T(8,128)S(1)}, u32[]{:S(2)}, u32[]{:S(2)}) collective-permute-start(f32[8,256]{1,0:T(8,128)S(1)} %get-tuple-element.38), channel_id=1, source_target_pairs={{0,60},{4,8},{8,4},{12,16},{16,12},{20,24},{24,20},{28,32},{32,28}... | collective-permute-start | bytes 24584 | tf_op jit(solution)/shard_map/ppermute | solution.py:174
  10.7 0.0 collective-permute-done.2.south
  10.7 2.7 %collective-permute-start.5 = (f32[8,256]{1,0:T(8,128)S(1)}, f32[8,256]{1,0:T(8,128)S(1)}, u32[]{:S(2)}, u32[]{:S(2)}) collective-permute-start(f32[8,256]{1,0:T(8,128)S(1)} %get-tuple-element.39), channel_id=1, source_target_pairs={{0,4},{4,0},{8,12},{12,8},{16,20},{20,16},{24,28},{28,24},{32,36},... | collective-permute-start | bytes 24584 | tf_op jit(solution)/shard_map/ppermute | solution.py:177
  13.4 0.0 copy-done
  13.4 0.4 x_matrix.1
  13.8 0.0 collective-permute-done.3.north
  13.9 0.0 collective-permute-done.4.xc
  13.9 0.4 collective-permute-done.5.xi
  14.3 0.0 collective-permute-done.below
  14.3 0.0 collective-permute-done.1.above
  14.3 0.0 copy-start.1
  14.3 1.0 %copy-done.1 = bf16[3,8,32,256]{3,2,1,0:T(8,128)(2,1)S(1)} copy-done((bf16[3,8,32,256]{3,2,1,0:T(8,128)(2,1)S(1)}, bf16[3,8,32,256]{3,2,1,0:T(8,128)(2,1)}, u32[]{:S(2)}) %copy-start.1) | copy-done | bytes 393240
  15.3 1.1 %explicit.1 = (f32[32,8,256]{2,1,0:T(8,128)S(1)}, f32[5,8,128]{2,1,0:T(8,128)S(1)}, f32[5,8,128]{2,1,0:T(8,128)S(1)}, f32[8,32,256]{2,1,0:T(8,128)}) custom-call(f32[8,32,256]{2,1,0:T(8,128)S(1)} %copy-done.3, bf16[3,8,32,256]{3,2,1,0:T(8,128)(2,1)S(1)} %copy-done.1, f32[8,32,256]{2,1,0:T(8,128)S(1)} %copy-done, f32[32,256]{1,0:T(8,128)S(1)} %collective-permute-done.below, ...), custom_call_target="tpu_custom_call" | custom-call | bytes 3022848 | tf_op jit(solution)/shard_map/explicit/pallas_call | solution.py:19
  16.4 1.0 %collective-permute-start.6 = (f32[5,8,128]{2,1,0:T(8,128)S(1)}, f32[5,8,128]{2,1,0:T(8,128)S(1)}, u32[]{:S(2)}, u32[]{:S(2)}) collective-permute-start(f32[5,8,128]{2,1,0:T(8,128)S(1)} %get-tuple-element.45), channel_id=1, source_target_pairs={{0,4},{4,0},{8,12},{12,8},{16,20},{20,16},{24,28},{28,24},{32,36},... | collective-permute-start | bytes 61448 | tf_op jit(solution)/shard_map/ppermute | solution.py:177
  17.3 0.8 %collective-permute-done.6.got_ref = f32[5,8,128]{2,1,0:T(8,128)S(1)} collective-permute-done((f32[5,8,128]{2,1,0:T(8,128)S(1)}, f32[5,8,128]{2,1,0:T(8,128)S(1)}, u32[]{:S(2)}, u32[]{:S(2)}) %collective-permute-start.6) | collective-permute-done | bytes 20512 | tf_op jit(solution)/shard_map/ppermute | solution.py:177
  18.2 14.9 %all_to_all.5.all_ref = f32[8,5,8,128]{3,2,1,0:T(8,128)S(1)} all-to-all(f32[8,5,8,128]{3,2,1,0:T(8,128)S(1)} %chip.1), channel_id=1, replica_groups={{0,8,16,24,32,40,48,56},{4,12,20,28,36,44,52,60},{1,9,17,25,33,41,49,57..., dimensions={0} | all-to-all | bytes 327680 | tf_op jit(solution)/shard_map/all_to_all | solution.py:382
  33.1 0.1 x_chain.1
  33.2 2.2 %collective-permute-start.7 = (f32[2,8,128]{2,1,0:T(8,128)S(1)}, f32[2,8,128]{2,1,0:T(8,128)S(1)}, u32[]{:S(2)}, u32[]{:S(2)}) collective-permute-start(f32[2,8,128]{2,1,0:T(8,128)S(1)} %get-tuple-element.47), channel_id=1, source_target_pairs={{0,4},{4,0},{8,12},{12,8},{16,20},{20,16},{24,28},{28,24},{32,36},... | collective-permute-start | bytes 24584 | tf_op jit(solution)/shard_map/ppermute | solution.py:177
  35.4 0.5 %y_matrix.1 = (f32[32,8,256]{2,1,0:T(8,128)S(1)}, f32[32,8,256]{2,1,0:T(8,128)S(1)}, f32[32,8,256]{2,1,0:T(8,128)S(1)}, f32[32,8,256]{2,1,0:T(8,128)S(1)}, f32[4,7,8,256]{3,2,1,0:T(8,128)S(1)}) custom-call(f32[32,8,256]{2,1,0:T(8,128)S(1)} %get-tuple-element.40.d_ref.dx_ref), custom_call_target="tpu_custom_call" | custom-call | flops 1000000 | bytes 1540096 | tf_op jit(solution)/shard_map/y_matrix/pallas_call | solution.py:19
  35.9 0.3 collective-permute-done.7.got_ref
  36.2 0.9 %x_finish.1 = (f32[32,8,256]{2,1,0:T(8,128)S(1)}, f32[3,2,8,256]{3,2,1,0:T(8,128)S(1)}, f32[8,256]{1,0:T(8,128)S(1)}, f32[32,8,256]{2,1,0:T(8,128)}) custom-call(f32[2,8,128]{2,1,0:T(8,128)S(1)} %get-tuple-element.46.own_ref, f32[2,8,128]{2,1,0:T(8,128)S(1)} %collective-permute-done.7.got_ref, f32[32,8,256]{2,1,0:T(8,128)S(1)} %get-tuple-element.48.base_ref, ...), custom_call_target="tpu_custom_call" | custom-call | bytes 2138112 | tf_op jit(solution)/shard_map/x_finish/pallas_call | solution.py:19
  37.1 1.5 %collective-permute-start.10 = (f32[8,256]{1,0:T(8,128)S(1)}, f32[8,256]{1,0:T(8,128)S(1)}, u32[]{:S(2)}, u32[]{:S(2)}) collective-permute-start(f32[8,256]{1,0:T(8,128)S(1)} %get-tuple-element.52.own_ref), channel_id=1, source_target_pairs={{0,3},{1,0},{2,1},{3,2},{4,7},{5,4},{6,5},{7,6},{8,11},{9,8},{10,9... | collective-permute-start | bytes 24584 | tf_op jit(solution)/shard_map/ppermute | solution.py:390
  38.7 0.3 collective-permute-start.9
  39.0 0.7 %collective-permute-start.8 = (f32[8,256]{1,0:T(8,128)S(1)}, f32[8,256]{1,0:T(8,128)S(1)}, u32[]{:S(2)}, u32[]{:S(2)}) collective-permute-start(f32[8,256]{1,0:T(8,128)S(1)} %get-tuple-element.52.own_ref), channel_id=1, source_target_pairs={{0,1},{1,2},{2,3},{3,0},{4,5},{5,6},{6,7},{7,4},{8,9},{9,10},{10,1... | collective-permute-start | bytes 24584 | tf_op jit(solution)/shard_map/ppermute | solution.py:390
  39.7 0.0 collective-permute-done.10.refs_2_
  39.7 3.0 %collective-permute-done.9.refs_1_ = f32[8,256]{1,0:T(8,128)S(1)} collective-permute-done((f32[8,256]{1,0:T(8,128)S(1)}, f32[8,256]{1,0:T(8,128)S(1)}, u32[]{:S(2)}, u32[]{:S(2)}) %collective-permute-start.9) | collective-permute-done | bytes 8224 | tf_op jit(solution)/shard_map/ppermute | solution.py:390
  42.7 0.1 collective-permute-done.8.refs_0_
  42.8 0.3 y_finish.1
  43.1 0.0 copy-start.2
  43.1 0.1 collective-permute-start.11
  43.2 2.7 %collective-permute-start.12 = (f32[32,256]{1,0:T(8,128)S(1)}, f32[32,256]{1,0:T(8,128)S(1)}, u32[]{:S(2)}, u32[]{:S(2)}) collective-permute-start(f32[32,256]{1,0:T(8,128)S(1)} %get-tuple-element.60), channel_id=1, source_target_pairs={{64,0},{128,64},{192,128},{0,192},{65,1},{129,65},{193,129},{1,193... | collective-permute-start | bytes 98312 | tf_op jit(solution)/shard_map/ppermute | solution.py:171
  45.9 2.6 %collective-permute-start.13 = (f32[8,256]{1,0:T(8,128)S(1)}, f32[8,256]{1,0:T(8,128)S(1)}, u32[]{:S(2)}, u32[]{:S(2)}) collective-permute-start(f32[8,256]{1,0:T(8,128)S(1)} %get-tuple-element.61), channel_id=1, source_target_pairs={{0,60},{4,8},{8,4},{12,16},{16,12},{20,24},{24,20},{28,32},{32,28}... | collective-permute-start | bytes 24584 | tf_op jit(solution)/shard_map/ppermute | solution.py:174
  48.5 0.0 collective-permute-start.14
  48.5 0.1 turn.1.yd_ref
  48.7 1.3 %collective-permute-done.13.xc = f32[8,256]{1,0:T(8,128)S(1)} collective-permute-done((f32[8,256]{1,0:T(8,128)S(1)}, f32[8,256]{1,0:T(8,128)S(1)}, u32[]{:S(2)}, u32[]{:S(2)}) %collective-permute-start.13) | collective-permute-done | bytes 8224 | tf_op jit(solution)/shard_map/ppermute | solution.py:174
  49.9 0.0 collective-permute-done.14.xi
  49.9 0.0 collective-permute-done.11.below
  49.9 0.0 collective-permute-done.12.above
  49.9 0.0 copy-done.2
  50.0 0.9 %final.1 = f32[8,32,256]{2,1,0:T(8,128)} custom-call(f32[8,32,256]{2,1,0:T(8,128)S(1)} %get-tuple-element.57.s_ref, f32[8,32,256]{2,1,0:T(8,128)S(1)} %turn.1.yd_ref, bf16[3,8,32,256]{3,2,1,0:T(8,128)(2,1)S(1)} %copy-done.2, f32[8,32,256]{2,1,0:T(8,128)S(1)} %copy-done, f32[32,256]{1,0:T(8,128)S(1)} %collective-permute-done.11.below, ...), custom_call_target="tpu_custom_call" | custom-call | bytes 1916928 | tf_op jit(solution)/shard_map/final/pallas_call | solution.py:19
  (1 shorter events, 0.0 us)
Async XLA Ops:
  0.0 13.4 %copy-start = (f32[8,32,256]{2,1,0:T(8,128)S(1)}, f32[8,32,256]{2,1,0:T(8,128)}, u32[]{:S(2)}) copy-start(f32[8,32,256]{2,1,0:T(8,128)} %k_ref.5) | copy-start | bytes 786436
  0.0 1.0 %copy-start.3 = (f32[8,32,256]{2,1,0:T(8,128)S(1)}, f32[8,32,256]{2,1,0:T(8,128)}, u32[]{:S(2)}) copy-start(f32[8,32,256]{2,1,0:T(8,128)} %f_ref.3) | copy-start | bytes 786436
  1.1 13.1 %collective-permute-start = (f32[32,256]{1,0:T(8,128)S(1)}, f32[32,256]{1,0:T(8,128)S(1)}, u32[]{:S(2)}, u32[]{:S(2)}) collective-permute-start(f32[32,256]{1,0:T(8,128)S(1)} %get-tuple-element.34), channel_id=1, source_target_pairs={{0,64},{64,128},{128,192},{192,0},{1,65},{65,129},{129,193},{193,1... | collective-permute-start | bytes 98312 | tf_op jit(solution)/shard_map/ppermute | solution.py:167
  3.2 11.0 %collective-permute-start.1 = (f32[32,256]{1,0:T(8,128)S(1)}, f32[32,256]{1,0:T(8,128)S(1)}, u32[]{:S(2)}, u32[]{:S(2)}) collective-permute-start(f32[32,256]{1,0:T(8,128)S(1)} %get-tuple-element.35), channel_id=1, source_target_pairs={{64,0},{128,64},{192,128},{0,192},{65,1},{129,65},{193,129},{1,193... | collective-permute-start | bytes 98312 | tf_op jit(solution)/shard_map/ppermute | solution.py:171
  4.6 6.1 %collective-permute-start.2 = (f32[8,256]{1,0:T(8,128)S(1)}, f32[8,256]{1,0:T(8,128)S(1)}, u32[]{:S(2)}, u32[]{:S(2)}) collective-permute-start(f32[8,256]{1,0:T(8,128)S(1)} %get-tuple-element.36), channel_id=1, source_target_pairs={{0,1},{1,2},{2,3},{3,0},{4,5},{5,6},{6,7},{7,4},{8,9},{9,10},{10,1... | collective-permute-start | bytes 24584 | tf_op jit(solution)/shard_map/ppermute | solution.py:167
  6.0 7.8 %collective-permute-start.3 = (f32[8,256]{1,0:T(8,128)S(1)}, f32[8,256]{1,0:T(8,128)S(1)}, u32[]{:S(2)}, u32[]{:S(2)}) collective-permute-start(f32[8,256]{1,0:T(8,128)S(1)} %get-tuple-element.37), channel_id=1, source_target_pairs={{1,0},{2,1},{3,2},{0,3},{5,4},{6,5},{7,6},{4,7},{9,8},{10,9},{11,1... | collective-permute-start | bytes 24584 | tf_op jit(solution)/shard_map/ppermute | solution.py:171
  7.4 6.4 %collective-permute-start.4 = (f32[8,256]{1,0:T(8,128)S(1)}, f32[8,256]{1,0:T(8,128)S(1)}, u32[]{:S(2)}, u32[]{:S(2)}) collective-permute-start(f32[8,256]{1,0:T(8,128)S(1)} %get-tuple-element.38), channel_id=1, source_target_pairs={{0,60},{4,8},{8,4},{12,16},{16,12},{20,24},{24,20},{28,32},{32,28}... | collective-permute-start | bytes 24584 | tf_op jit(solution)/shard_map/ppermute | solution.py:174
  10.7 3.5 %collective-permute-start.5 = (f32[8,256]{1,0:T(8,128)S(1)}, f32[8,256]{1,0:T(8,128)S(1)}, u32[]{:S(2)}, u32[]{:S(2)}) collective-permute-start(f32[8,256]{1,0:T(8,128)S(1)} %get-tuple-element.39), channel_id=1, source_target_pairs={{0,4},{4,0},{8,12},{12,8},{16,20},{20,16},{24,28},{28,24},{32,36},... | collective-permute-start | bytes 24584 | tf_op jit(solution)/shard_map/ppermute | solution.py:177
  14.3 1.0 %copy-start.1 = (bf16[3,8,32,256]{3,2,1,0:T(8,128)(2,1)S(1)}, bf16[3,8,32,256]{3,2,1,0:T(8,128)(2,1)}, u32[]{:S(2)}) copy-start(bf16[3,8,32,256]{3,2,1,0:T(8,128)(2,1)} %wind_ref.3) | copy-start | bytes 1179652
  16.4 1.8 %collective-permute-start.6 = (f32[5,8,128]{2,1,0:T(8,128)S(1)}, f32[5,8,128]{2,1,0:T(8,128)S(1)}, u32[]{:S(2)}, u32[]{:S(2)}) collective-permute-start(f32[5,8,128]{2,1,0:T(8,128)S(1)} %get-tuple-element.45), channel_id=1, source_target_pairs={{0,4},{4,0},{8,12},{12,8},{16,20},{20,16},{24,28},{28,24},{32,36},... | collective-permute-start | bytes 61448 | tf_op jit(solution)/shard_map/ppermute | solution.py:177
  33.2 3.0 %collective-permute-start.7 = (f32[2,8,128]{2,1,0:T(8,128)S(1)}, f32[2,8,128]{2,1,0:T(8,128)S(1)}, u32[]{:S(2)}, u32[]{:S(2)}) collective-permute-start(f32[2,8,128]{2,1,0:T(8,128)S(1)} %get-tuple-element.47), channel_id=1, source_target_pairs={{0,4},{4,0},{8,12},{12,8},{16,20},{20,16},{24,28},{28,24},{32,36},... | collective-permute-start | bytes 24584 | tf_op jit(solution)/shard_map/ppermute | solution.py:177
  37.1 2.6 %collective-permute-start.10 = (f32[8,256]{1,0:T(8,128)S(1)}, f32[8,256]{1,0:T(8,128)S(1)}, u32[]{:S(2)}, u32[]{:S(2)}) collective-permute-start(f32[8,256]{1,0:T(8,128)S(1)} %get-tuple-element.52.own_ref), channel_id=1, source_target_pairs={{0,3},{1,0},{2,1},{3,2},{4,7},{5,4},{6,5},{7,6},{8,11},{9,8},{10,9... | collective-permute-start | bytes 24584 | tf_op jit(solution)/shard_map/ppermute | solution.py:390
  38.7 4.0 %collective-permute-start.9 = (f32[8,256]{1,0:T(8,128)S(1)}, f32[8,256]{1,0:T(8,128)S(1)}, u32[]{:S(2)}, u32[]{:S(2)}) collective-permute-start(f32[8,256]{1,0:T(8,128)S(1)} %get-tuple-element.52.own_ref), channel_id=1, source_target_pairs={{0,2},{1,3},{2,0},{3,1},{4,6},{5,7},{6,4},{7,5},{8,10},{9,11},{10,... | collective-permute-start | bytes 24584 | tf_op jit(solution)/shard_map/ppermute | solution.py:390
  39.0 3.7 %collective-permute-start.8 = (f32[8,256]{1,0:T(8,128)S(1)}, f32[8,256]{1,0:T(8,128)S(1)}, u32[]{:S(2)}, u32[]{:S(2)}) collective-permute-start(f32[8,256]{1,0:T(8,128)S(1)} %get-tuple-element.52.own_ref), channel_id=1, source_target_pairs={{0,1},{1,2},{2,3},{3,0},{4,5},{5,6},{6,7},{7,4},{8,9},{9,10},{10,1... | collective-permute-start | bytes 24584 | tf_op jit(solution)/shard_map/ppermute | solution.py:390
  43.1 6.9 %copy-start.2 = (bf16[3,8,32,256]{3,2,1,0:T(8,128)(2,1)S(1)}, bf16[3,8,32,256]{3,2,1,0:T(8,128)(2,1)}, u32[]{:S(2)}) copy-start(bf16[3,8,32,256]{3,2,1,0:T(8,128)(2,1)} %wind_ref.3) | copy-start | bytes 1179652
  43.1 6.8 %collective-permute-start.11 = (f32[32,256]{1,0:T(8,128)S(1)}, f32[32,256]{1,0:T(8,128)S(1)}, u32[]{:S(2)}, u32[]{:S(2)}) collective-permute-start(f32[32,256]{1,0:T(8,128)S(1)} %get-tuple-element.59), channel_id=1, source_target_pairs={{0,64},{64,128},{128,192},{192,0},{1,65},{65,129},{129,193},{193,1... | collective-permute-start | bytes 98312 | tf_op jit(solution)/shard_map/ppermute | solution.py:167
  43.2 6.7 %collective-permute-start.12 = (f32[32,256]{1,0:T(8,128)S(1)}, f32[32,256]{1,0:T(8,128)S(1)}, u32[]{:S(2)}, u32[]{:S(2)}) collective-permute-start(f32[32,256]{1,0:T(8,128)S(1)} %get-tuple-element.60), channel_id=1, source_target_pairs={{64,0},{128,64},{192,128},{0,192},{65,1},{129,65},{193,129},{1,193... | collective-permute-start | bytes 98312 | tf_op jit(solution)/shard_map/ppermute | solution.py:171
  45.9 4.1 %collective-permute-start.13 = (f32[8,256]{1,0:T(8,128)S(1)}, f32[8,256]{1,0:T(8,128)S(1)}, u32[]{:S(2)}, u32[]{:S(2)}) collective-permute-start(f32[8,256]{1,0:T(8,128)S(1)} %get-tuple-element.61), channel_id=1, source_target_pairs={{0,60},{4,8},{8,4},{12,16},{16,12},{20,24},{24,20},{28,32},{32,28}... | collective-permute-start | bytes 24584 | tf_op jit(solution)/shard_map/ppermute | solution.py:174
  48.5 1.4 %collective-permute-start.14 = (f32[8,256]{1,0:T(8,128)S(1)}, f32[8,256]{1,0:T(8,128)S(1)}, u32[]{:S(2)}, u32[]{:S(2)}) collective-permute-start(f32[8,256]{1,0:T(8,128)S(1)} %get-tuple-element.62), channel_id=1, source_target_pairs={{0,4},{4,0},{8,12},{12,8},{16,20},{20,16},{24,28},{28,24},{32,36},... | collective-permute-start | bytes 24584 | tf_op jit(solution)/shard_map/ppermute | solution.py:177
where the time goes:
time: 51 us; the launch traced here: 50.9 us
  starting transfers between devices  23.4 us (46%)
  blocking collectives  14.9 us (29%)
  waiting for transfers between devices  5.89 us (12%)
  Pallas kernels  4.61 us (9%)
  local copies, waits for them, and re-layouts  2 us (4%)
    all_to_all x1, blocking collectives, body(): lax.all_to_all(spread, 'gx', 0, 0, axis_index_groups=groups, tiled=True)  14.9 us
    ppermute x2, starting transfers between devices, across(): lax.ppermute(a, 'gx', [(i, (i + 1 if i % 2 else i - 1) % members) for i i...  5.9 us
    ppermute x4, starting transfers between devices, sibling(): return lax.ppermute(a, 'gx', [(i, i ^ 1) for i in range(members)])  5.85 us
    ppermute x3, starting transfers between devices, down(): return lax.ppermute(a, axis, [((i + 1) % n, i) for i in range(n)])  5.46 us
    pallas_call x10, Pallas kernels, call(): pl.pallas_call(kernel, out_shape=shapes, in_specs=[vm] * len(ins), out_sp...  4.61 us
    ppermute x3, starting transfers between devices, up(): return lax.ppermute(a, axis, [(i, (i + 1) % n) for i in range(n)])  3.6 us
    ppermute x3, waiting for transfers between devices, body(): lax.ppermute(send, 'gy', [(i, (i + back) % columns) for i in range(column...  3.05 us
    ppermute x3, starting transfers between devices, body(): lax.ppermute(send, 'gy', [(i, (i + back) % columns) for i in range(column...  2.56 us
  transfers between devices with their start and end apart: 15, of which 6 were waited for; matrix products, arithmetic and copies ran while one was open for 0% of the time, Pallas kernels for 2%

commit v1 on v0

--- a/solution.py
+++ b/solution.py
@@ -12,15 +12,17 @@
 VMEM_BYTES = 24 * 2**20
 
 
-def call(kernel, outs, *ins, name, flops=0):
-    shapes = [jax.ShapeDtypeStruct(s, jnp.float32) for s in outs]
+def call(kernel, outs, *ins, name, flops=0, far=(), scratch=()):
+    shapes = [jax.ShapeDtypeStruct(s, jnp.float32) if isinstance(s, tuple) else s for s in outs]
     vm = pl.BlockSpec(memory_space=pltpu.VMEM)
+    any_space = pl.BlockSpec(memory_space=pltpu.HBM)
     size = 4 * (sum(x.size for x in ins) + sum(x.size for x in shapes))
     return pl.pallas_call(
         kernel,
         out_shape=shapes,
-        in_specs=[vm] * len(ins),
+        in_specs=[any_space if n in far else vm for n in range(len(ins))],
         out_specs=[vm] * len(outs),
+        scratch_shapes=list(scratch),
         compiler_params=pltpu.CompilerParams(vmem_limit_bytes=VMEM_BYTES),
         cost_estimate=pl.CostEstimate(flops=flops, bytes_accessed=size, transcendentals=0),
         name=name,
@@ -108,17 +110,6 @@
         out_ref[i] = s
 
 
-def pack(v, half, h):
-    piece = v[h * half : (h + 1) * half]
-    mid = v.shape[1] // 2
-    return jnp.concatenate([piece[:, :mid], piece[:, mid:]], axis=0)
-
-
-def unpack(v):
-    half = v.shape[0] // 2
-    return jnp.concatenate([v[:half], v[half:]], axis=1)
-
-
 def stencil(z, f, below, above, west, east, ydiff, wind_ref, k):
     count = f.shape[0]
     row = lax.broadcasted_iota(jnp.int32, f.shape, 0)
@@ -145,8 +136,6 @@
     c = reach * reach
     subs = 8
     steps = ny // subs
-    half = nz // 2
-    face = (2 * half, ny // 2)
 
     def core():
         return lax.rem(lax.axis_index("gx"), 2)
@@ -187,14 +176,16 @@
         index = lax.axis_index("gz")
         return jnp.where(index == 0, 0.0, below), jnp.where(index == levels - 1, 0.0, above)
 
-    def x_matrix_kernel(k_ref, d_ref, w_ref, l_ref, r_ref):
+    def matrix_kernel(
+        k_ref, far_wind, d_ref, w_ref, l_ref, r_ref, yd_ref, yw_ref, yl_ref, yr_ref, c_ref, wind_ref, sem
+    ):
+        fetch = pltpu.make_async_copy(far_wind, wind_ref, sem)
+        fetch.start()
         d_ref[...] = 1.0 / (c * jnp.swapaxes(k_ref[...], 0, 1))
         factor(d_ref, w_ref, l_ref, r_ref, nx)
-
-    def y_matrix_kernel(dx_ref, d_ref, w_ref, l_ref, r_ref, c_ref):
-        d_ref[...] = jnp.swapaxes(dx_ref[...].reshape(lines, ny).T.reshape(subs, steps, lines), 0, 1)
-        factor(d_ref, w_ref, l_ref, r_ref, steps)
-        L, C, R = l_ref[0], r_ref[0], r_ref[steps - 1]
+        yd_ref[...] = jnp.swapaxes(d_ref[...].reshape(lines, ny).T.reshape(subs, steps, lines), 0, 1)
+        factor(yd_ref, yw_ref, yl_ref, yr_ref, steps)
+        L, C, R = yl_ref[0], yr_ref[0], yr_ref[steps - 1]
         for level in range(3):
             shift = subs - (1 << level)
             bL, bC, bR = pltpu.roll(L, shift, 0), pltpu.roll(C, shift, 0), pltpu.roll(R, shift, 0)
@@ -203,11 +194,15 @@
             for n, value in enumerate((x, y, bL, R, bC, inv, R * y)):
                 c_ref[level, n] = value
             L, C, R = L + x * bL * C, x * bC, bR + y * R * bC
-        c_ref[3, 0], c_ref[3, 1], c_ref[3, 2] = L, C, R
+        for n, value in enumerate((L, C, R)):
+            c_ref[3, n] = value
+        for n in range(3, 7):
+            c_ref[3, n] = jnp.zeros_like(L)
+        fetch.wait()
 
     def explicit_kernel(
         f_ref, wind_ref, k_ref, below, above, south, north, xc, xi, d_ref, w_ref, l_ref, r_ref,
-        base_ref, mine_ref, send_ref, e_ref,
+        base_ref, ends_ref, e_ref,
     ):
         west, east = x_rows(xc[...], xi[...])
         low, high = z_planes(below[...], above[...])
@@ -232,54 +227,66 @@
             )
         e = jnp.swapaxes(e_ref[...], 0, 1)
         sweep(lambda i: e[i] * d_ref[i], w_ref, base_ref, nx)
-        odd = core() == 1
         ends = (base_ref[0], base_ref[nx - 1], l_ref[0], r_ref[0], r_ref[nx - 1])
         for n, v in enumerate(ends):
-            lo, hi = pack(v, half, 0), pack(v, half, 1)
-            mine_ref[n] = jnp.where(odd, hi, lo)
-            send_ref[n] = jnp.where(odd, lo, hi)
-
-    def pair(mine_ref, got_ref):
+            ends_ref[n] = v
+
+    def read(ref):
+        return tuple(ref[n] for n in range(5))
+
+    def choose(test, a, b):
+        return tuple(jnp.where(test, x, y) for x, y in zip(a, b))
+
+    def ordered(own_ref, got_ref, own_first):
+        own, got = read(own_ref), read(got_ref)
+        return choose(own_first, own, got), choose(own_first, got, own)
+
+    def chip_kernel(own_ref, got_ref, out_ref):
+        b0, b1, L, C, R = merge(*ordered(own_ref, got_ref, core() == 0))
+        chip = lax.axis_index("gx") // 2
+        first, last = chip == 0, chip == chips - 1
+        L, R = jnp.where(first, 0.0, L), jnp.where(last, 0.0, R)
+        C = jnp.where(jnp.logical_or(first, last), 0.0, C)
+        for n, v in enumerate((b0, b1, L, C, R)):
+            out_ref[n] = v
+
+    def pair_kernel(own_ref, got_ref, out_ref):
+        for n, v in enumerate(merge(*ordered(own_ref, got_ref, core() == 1))):
+            out_ref[n] = v
+
+    def side_kernel(near_ref, far_ref, opposite_ref, out_ref):
+        three = merge(*ordered(near_ref, far_ref, core() == 1))
+        four = merge(read(opposite_ref), three)
+        for n, v in enumerate(choose(core() == 0, four, three)):
+            out_ref[n] = v
+
+    def x_finish_kernel(
+        ends_ref, other_ref, side_ref, got_ref, base_ref, l_ref, r_ref, d_ref, w_ref, c_ref,
+        ybase_ref, up_ref, send_ref, s_ref,
+    ):
         odd = core() == 1
-        a = tuple(jnp.where(odd, got_ref[n], mine_ref[n]) for n in range(5))
-        b = tuple(jnp.where(odd, mine_ref[n], got_ref[n]) for n in range(5))
-        return a, b
-
-    def chip_kernel(mine_ref, got_ref, out_ref):
-        whole = merge(*pair(mine_ref, got_ref))
-        for n in range(5):
-            for m in range(chips):
-                out_ref[m, n] = whole[n]
-
-    def x_chain_kernel(all_ref, mine_ref, got_ref, own_ref, send_ref):
-        a, b = pair(mine_ref, got_ref)
-        blocks = [tuple(all_ref[m, n] for n in range(5)) for m in range(chips)]
-        lp, lg, rp, rg = chain_ends(blocks, lax.axis_index("gx") // 2)
+        chip = lax.axis_index("gx") // 2
+        a, b = ordered(ends_ref, other_ref, core() == 0)
+        left, right = ordered(side_ref, got_ref, core() == 0)
+        zero = jnp.zeros_like(a[0])
+        lp, lg = zero, zero
+        for block in (right, left):
+            lp, lg = close_left(lp, lg, block)
+        rp, rg = zero, zero
+        for block in (left, right):
+            rp, rg = close_right(rp, rg, block)
+        lp, lg = jnp.where(chip == 0, 0.0, lp), jnp.where(chip == 0, 0.0, lg)
+        rp, rg = jnp.where(chip == chips - 1, 0.0, rp), jnp.where(chip == chips - 1, 0.0, rg)
         ap, ag = close_left(lp, lg, a)
         bp, bg = close_right(rp, rg, b)
         last_a = (ap + ag * bp) / (1.0 - ag * bg)
         first_b = bp + bg * last_a
         first_a = (a[0] + a[2] * lp + a[3] * first_b) / (1.0 - a[2] * lg)
         last_b = (b[1] + b[4] * rp + b[3] * last_a) / (1.0 - b[4] * rg)
-        outer_l = lp + lg * first_a
-        outer_r = rp + rg * last_b
-        odd = core() == 1
-        own_ref[0] = jnp.where(odd, last_a, outer_l)
-        own_ref[1] = jnp.where(odd, outer_r, first_b)
-        send_ref[0] = jnp.where(odd, outer_l, last_a)
-        send_ref[1] = jnp.where(odd, first_b, outer_r)
-
-    def x_finish_kernel(
-        own_ref, got_ref, base_ref, l_ref, r_ref, d_ref, w_ref, c_ref,
-        ybase_ref, up_ref, send_ref, s_ref,
-    ):
-        odd = core() == 1
-        sides = []
-        for n in range(2):
-            own, got = unpack(own_ref[n]), unpack(got_ref[n])
-            sides.append(jnp.concatenate([jnp.where(odd, got, own), jnp.where(odd, own, got)], axis=0))
+        before = jnp.where(odd, last_a, lp + lg * first_a)
+        after = jnp.where(odd, rp + rg * last_b, first_b)
         for i in range(nx):
-            s_ref[i] = base_ref[i] + l_ref[i] * sides[0] + r_ref[i] * sides[1]
+            s_ref[i] = base_ref[i] + l_ref[i] * before + r_ref[i] * after
         t = s_ref[...].reshape(lines, ny).T
         q = jnp.swapaxes(t.reshape(subs, steps, lines), 0, 1)
         sweep(lambda i: q[i] * d_ref[i], w_ref, ybase_ref, steps)
@@ -362,7 +369,11 @@
             )
 
     box, xbox, ybox = (nz, nx, ny), (nx, nz, ny), (steps, subs, lines)
-    five = (5,) + face
+    five = (5, nz, ny)
+
+    def outward(a, distance):
+        move = lambda i: ((i // 2 + (-distance if i % 2 else distance)) % chips) * 2 + i % 2
+        return lax.ppermute(a, "gx", [(i, move(i)) for i in range(members)])
 
     zlo, zhi, ylo, yhi, xc, xi = call(
         faces_kernel, [(nx, ny), (nx, ny), (8, lines), (8, lines), (nz, ny), (nz, ny)], field, name="faces"
@@ -370,21 +381,26 @@
     xc, xi = across(xc), sibling(xi)
     below, above = up(zhi, "gz"), down(zlo, "gz")
     south, north = up(yhi, "gy"), down(ylo, "gy")
-    dx, wx, lx, rx = call(x_matrix_kernel, [xbox] * 4, rate, name="x_matrix", flops=10**6)
-    dy, wy, ly, ry, cy = call(y_matrix_kernel, [ybox] * 4 + [(4, 7, subs, lines)], dx, name="y_matrix", flops=10**6)
-    base, mine, send, _ = call(
-        explicit_kernel, [xbox, five, five, box],
-        field, wind, rate, below, above, south, north, xc, xi, dx, wx, lx, rx, name="explicit",
-    )
-    got = sibling(send)
-    (spread,) = call(chip_kernel, [(chips,) + five], mine, got, name="chip")
-    groups = [[2 * m + k for m in range(chips)] for k in range(2)]
-    everyone = lax.all_to_all(spread, "gx", 0, 0, axis_index_groups=groups, tiled=True)
-    own, send = call(x_chain_kernel, [(2,) + face] * 2, everyone, mine, got, name="x_chain")
-    got = sibling(send)
+    dx, wx, lx, rx, dy, wy, ly, ry, cy, near_wind = call(
+        matrix_kernel,
+        [xbox] * 4 + [ybox] * 4 + [(4, 7, subs, lines), jax.ShapeDtypeStruct(wind.shape, wind.dtype)],
+        rate, wind, name="matrix", flops=10**6, far=(1,), scratch=[pltpu.SemaphoreType.DMA],
+    )
+    base, ends, _ = call(
+        explicit_kernel, [xbox, five, box],
+        field, near_wind, rate, below, above, south, north, xc, xi, dx, wx, lx, rx, name="explicit",
+    )
+    other = sibling(ends)
+    (chip,) = call(chip_kernel, [five], ends, other, name="chip")
+    opposite = outward(chip, chips // 2)
+    near = outward(chip, 1)
+    (pair,) = call(pair_kernel, [five], chip, near, name="pair")
+    distant = outward(pair, 2)
+    (side,) = call(side_kernel, [five], near, distant, opposite, name="side")
+    facing = sibling(side)
     ybase, ups, send, _ = call(
         x_finish_kernel, [ybox, (3, 2, subs, lines), (8, lines), xbox],
-        own, got, base, lx, rx, dy, wy, cy, name="x_finish",
+        ends, other, side, facing, base, lx, rx, dy, wy, cy, name="x_finish",
     )
     ring = [
         lax.ppermute(send, "gy", [(i, (i + back) % columns) for i in range(columns)])
@@ -397,7 +413,7 @@
     xc, xi = across(xc), sibling(xi)
     below, above = up(zhi, "gz"), down(zlo, "gz")
     (ydiff,) = call(turn_kernel, [box], yd, name="turn", flops=10**6)
-    (out,) = call(final_kernel, [box], swept, ydiff, wind, rate, below, above, xc, xi, name="final")
+    (out,) = call(final_kernel, [box], swept, ydiff, near_wind, rate, below, above, xc, xi, name="final")
     return out
 
 

time: 51 us -> 45.7 us (0.90)
  blocking collectives: 14.9 us -> 0 us
  starting transfers between devices: 23.4 us -> 29.1 us
  waiting for transfers between devices: 5.89 us -> 10.1 us
    all_to_all x1 -> x0, blocking collectives: 14.9 us -> none  [body(): lax.all_to_all(spread, 'gx', 0, 0, axis_index_groups=groups, tiled=True)]
    ppermute x0 -> x3, starting transfers between devices: none -> 6.41 us  [outward(): return lax.ppermute(a, 'gx', [(i, move(i)) for i in range(members)])]
    ppermute x0 -> x3, waiting for transfers between devices: none -> 3.78 us  [outward(): return lax.ppermute(a, 'gx', [(i, move(i)) for i in range(members)])]
    ppermute x4, starting transfers between devices: 5.85 us -> 4.64 us  [sibling(): return lax.ppermute(a, 'gx', [(i, i ^ 1) for i in range(members)])]
    ppermute x2, starting transfers between devices: 5.9 us -> 6.47 us  [across(): lax.ppermute(a, 'gx', [(i, (i + 1 if i % 2 else i - 1) % members) for i i...]
    ppermute x4, waiting for transfers between devices: 1.55 us -> 2.09 us  [sibling(): return lax.ppermute(a, 'gx', [(i, i ^ 1) for i in range(members)])]
    unnamed x8 -> x6, local copies, waits for them, and re-layouts: 2 us -> 1.99 us
  transfers between devices with their start and end apart: 15 -> 18, of which waited for: 6 -> 7; matrix products, arithmetic and copies ran while one was open for 0% -> 0% of each run, Pallas kernels for 2% -> 2%
where the time goes in v1:
time: 45.7 us; the launch traced here: 45.6 us
  starting transfers between devices  29.1 us (64%)
  waiting for transfers between devices  10.1 us (22%)
  Pallas kernels  4.21 us (9%)
  local copies, waits for them, and re-layouts  1.99 us (4%)
    ppermute x2, starting transfers between devices, across(): lax.ppermute(a, 'gx', [(i, (i + 1 if i % 2 else i - 1) % members) for i i...  6.47 us
    ppermute x3, starting transfers between devices, outward(): return lax.ppermute(a, 'gx', [(i, move(i)) for i in range(members)])  6.41 us
    ppermute x3, starting transfers between devices, down(): return lax.ppermute(a, axis, [((i + 1) % n, i) for i in range(n)])  5.46 us
    ppermute x4, starting transfers between devices, sibling(): return lax.ppermute(a, 'gx', [(i, i ^ 1) for i in range(members)])  4.64 us
    pallas_call x10, Pallas kernels, call(): pl.pallas_call(kernel, out_shape=shapes, in_specs=[any_space if n in far...  4.21 us
    ppermute x3, waiting for transfers between devices, outward(): return lax.ppermute(a, 'gx', [(i, move(i)) for i in range(members)])  3.78 us
    ppermute x3, starting transfers between devices, up(): return lax.ppermute(a, axis, [(i, (i + 1) % n) for i in range(n)])  3.6 us
    ppermute x3, waiting for transfers between devices, body(): lax.ppermute(send, 'gy', [(i, (i + back) % columns) for i in range(column...  3.05 us
  transfers between devices with their start and end apart: 18, of which 7 were waited for; matrix products, arithmetic and copies ran while one was open for 0% of the time, Pallas kernels for 2%

profile of v1, /device:TPU:1, one launch (start us, length us, event | category | flops | bytes accessed | tf_op | source)
XLA Modules:
  0.0 45.6 jit_solution(8128863296979135010)
XLA Ops:
  0.0 0.0 copy-start
  0.0 0.0 copy-start.1
  0.0 1.0 %copy-done.1 = f32[8,32,256]{2,1,0:T(8,128)S(1)} copy-done((f32[8,32,256]{2,1,0:T(8,128)S(1)}, f32[8,32,256]{2,1,0:T(8,128)}, u32[]{:S(2)}) %copy-start.1) | copy-done | bytes 262168
  1.0 0.1 faces.1
  1.1 2.1 %collective-permute-start = (f32[32,256]{1,0:T(8,128)S(1)}, f32[32,256]{1,0:T(8,128)S(1)}, u32[]{:S(2)}, u32[]{:S(2)}) collective-permute-start(f32[32,256]{1,0:T(8,128)S(1)} %get-tuple-element.33), channel_id=1, source_target_pairs={{0,64},{64,128},{128,192},{192,0},{1,65},{65,129},{129,193},{193,1... | collective-permute-start | bytes 98312 | tf_op jit(solution)/shard_map/ppermute | solution.py:156
  3.2 1.4 %collective-permute-start.1 = (f32[32,256]{1,0:T(8,128)S(1)}, f32[32,256]{1,0:T(8,128)S(1)}, u32[]{:S(2)}, u32[]{:S(2)}) collective-permute-start(f32[32,256]{1,0:T(8,128)S(1)} %get-tuple-element.34), channel_id=1, source_target_pairs={{64,0},{128,64},{192,128},{0,192},{65,1},{129,65},{193,129},{1,193... | collective-permute-start | bytes 98312 | tf_op jit(solution)/shard_map/ppermute | solution.py:160
  4.6 1.4 %collective-permute-start.2 = (f32[8,256]{1,0:T(8,128)S(1)}, f32[8,256]{1,0:T(8,128)S(1)}, u32[]{:S(2)}, u32[]{:S(2)}) collective-permute-start(f32[8,256]{1,0:T(8,128)S(1)} %get-tuple-element.35), channel_id=1, source_target_pairs={{0,1},{1,2},{2,3},{3,0},{4,5},{5,6},{6,7},{7,4},{8,9},{9,10},{10,1... | collective-permute-start | bytes 24584 | tf_op jit(solution)/shard_map/ppermute | solution.py:156
  6.0 1.4 %collective-permute-start.3 = (f32[8,256]{1,0:T(8,128)S(1)}, f32[8,256]{1,0:T(8,128)S(1)}, u32[]{:S(2)}, u32[]{:S(2)}) collective-permute-start(f32[8,256]{1,0:T(8,128)S(1)} %get-tuple-element.36), channel_id=1, source_target_pairs={{1,0},{2,1},{3,2},{0,3},{5,4},{6,5},{7,6},{4,7},{9,8},{10,9},{11,1... | collective-permute-start | bytes 24584 | tf_op jit(solution)/shard_map/ppermute | solution.py:160
  7.4 3.3 %collective-permute-start.4 = (f32[8,256]{1,0:T(8,128)S(1)}, f32[8,256]{1,0:T(8,128)S(1)}, u32[]{:S(2)}, u32[]{:S(2)}) collective-permute-start(f32[8,256]{1,0:T(8,128)S(1)} %get-tuple-element.37), channel_id=1, source_target_pairs={{0,60},{4,8},{8,4},{12,16},{16,12},{20,24},{24,20},{28,32},{32,28}... | collective-permute-start | bytes 24584 | tf_op jit(solution)/shard_map/ppermute | solution.py:163
  10.7 0.0 collective-permute-done.2.south
  10.7 2.7 %collective-permute-start.5 = (f32[8,256]{1,0:T(8,128)S(1)}, f32[8,256]{1,0:T(8,128)S(1)}, u32[]{:S(2)}, u32[]{:S(2)}) collective-permute-start(f32[8,256]{1,0:T(8,128)S(1)} %get-tuple-element.38), channel_id=1, source_target_pairs={{0,4},{4,0},{8,12},{12,8},{16,20},{20,16},{24,28},{28,24},{32,36},... | collective-permute-start | bytes 24584 | tf_op jit(solution)/shard_map/ppermute | solution.py:166
  13.4 0.0 copy-done
  13.4 1.0 %copy-done.2 = bf16[3,8,32,256]{3,2,1,0:T(8,128)(2,1)S(1)} copy-done((bf16[3,8,32,256]{3,2,1,0:T(8,128)(2,1)S(1)}, bf16[3,8,32,256]{3,2,1,0:T(8,128)(2,1)}, u32[]{:S(2)}) %copy-start.2) | copy-done | bytes 393240
  14.4 0.7 %matrix.1 = (f32[32,8,256]{2,1,0:T(8,128)S(1)}, f32[32,8,256]{2,1,0:T(8,128)S(1)}, f32[32,8,256]{2,1,0:T(8,128)S(1)}, f32[32,8,256]{2,1,0:T(8,128)S(1)}, f32[32,...) custom-call(f32[8,32,256]{2,1,0:T(8,128)S(1)} %copy-done, ...), custom_call_target="tpu_custom_call" | custom-call | flops 1000000 | bytes 4161536 | tf_op jit(solution)/shard_map/matrix/pallas_call | solution.py:20
  15.2 0.0 collective-permute-done.3.north
  15.2 0.0 collective-permute-done.4.xc
  15.2 0.0 collective-permute-done.5.xi
  15.2 0.0 collective-permute-done.below
  15.2 0.0 collective-permute-done.1.above
  15.2 1.1 %explicit.1 = (f32[32,8,256]{2,1,0:T(8,128)S(1)}, f32[5,8,256]{2,1,0:T(8,128)S(1)}, f32[8,32,256]{2,1,0:T(8,128)}) custom-call(f32[8,32,256]{2,1,0:T(8,128)S(1)} %copy-done.1, bf16[3,8,32,256]{3,2,1,0:T(8,128)(2,1)S(1)} %get-tuple-element.32.wind_ref, f32[8,32,256]{2,1,0:T(8,128)S(1)} %copy-done, f32[32,256]{1,0:T(8,128)S(1)} %collective-permute-done.below, ...), custom_call_target="tpu_custom_call" | custom-call | bytes 3022848 | tf_op jit(solution)/shard_map/explicit/pallas_call | solution.py:20
  16.3 0.0 collective-permute-start.6
  16.3 1.2 %collective-permute-done.6.got_ref.other_ref = f32[5,8,256]{2,1,0:T(8,128)S(1)} collective-permute-done((f32[5,8,256]{2,1,0:T(8,128)S(1)}, f32[5,8,256]{2,1,0:T(8,128)S(1)}, u32[]{:S(2)}, u32[]{:S(2)}) %collective-permute-start.6) | collective-permute-done | bytes 40992 | tf_op jit(solution)/shard_map/ppermute | solution.py:166
  17.6 3.0 %collective-permute-start.7 = (f32[5,8,256]{2,1,0:T(8,128)S(1)}, f32[5,8,256]{2,1,0:T(8,128)S(1)}, u32[]{:S(2)}, u32[]{:S(2)}) collective-permute-start(f32[5,8,256]{2,1,0:T(8,128)S(1)} %chip.1.own_ref), channel_id=1, source_target_pairs={{0,8},{4,60},{8,16},{12,4},{16,24},{20,12},{24,32},{28,20},{32,40}... | collective-permute-start | bytes 122888 | tf_op jit(solution)/shard_map/ppermute | solution.py:376
  20.6 2.5 %collective-permute-start.9 = (f32[5,8,256]{2,1,0:T(8,128)S(1)}, f32[5,8,256]{2,1,0:T(8,128)S(1)}, u32[]{:S(2)}, u32[]{:S(2)}) collective-permute-start(f32[5,8,256]{2,1,0:T(8,128)S(1)} %chip.1.own_ref), channel_id=1, source_target_pairs={{0,32},{4,36},{8,40},{12,44},{16,48},{20,52},{24,56},{28,60},{32,0... | collective-permute-start | bytes 122888 | tf_op jit(solution)/shard_map/ppermute | solution.py:376
  23.1 0.0 collective-permute-done.7.got_ref.near_ref
  23.1 0.9 %collective-permute-start.8 = (f32[5,8,256]{2,1,0:T(8,128)S(1)}, f32[5,8,256]{2,1,0:T(8,128)S(1)}, u32[]{:S(2)}, u32[]{:S(2)}) collective-permute-start(f32[5,8,256]{2,1,0:T(8,128)S(1)} %pair.1), channel_id=1, source_target_pairs={{0,16},{4,52},{8,24},{12,60},{16,32},{20,4},{24,40},{28,12},{32,48... | collective-permute-start | bytes 122888 | tf_op jit(solution)/shard_map/ppermute | solution.py:376
  24.0 3.4 %collective-permute-done.9.opposite_ref = f32[5,8,256]{2,1,0:T(8,128)S(1)} collective-permute-done((f32[5,8,256]{2,1,0:T(8,128)S(1)}, f32[5,8,256]{2,1,0:T(8,128)S(1)}, u32[]{:S(2)}, u32[]{:S(2)}) %collective-permute-start.9) | collective-permute-done | bytes 40992 | tf_op jit(solution)/shard_map/ppermute | solution.py:376
  27.4 0.4 collective-permute-done.8.far_ref
  27.8 1.9 %collective-permute-start.10 = (f32[5,8,256]{2,1,0:T(8,128)S(1)}, f32[5,8,256]{2,1,0:T(8,128)S(1)}, u32[]{:S(2)}, u32[]{:S(2)}) collective-permute-start(f32[5,8,256]{2,1,0:T(8,128)S(1)} %side.1.side_ref), channel_id=1, source_target_pairs={{0,4},{4,0},{8,12},{12,8},{16,20},{20,16},{24,28},{28,24},{32,36},... | collective-permute-start | bytes 122888 | tf_op jit(solution)/shard_map/ppermute | solution.py:166
  29.7 0.9 %collective-permute-done.10.got_ref = f32[5,8,256]{2,1,0:T(8,128)S(1)} collective-permute-done((f32[5,8,256]{2,1,0:T(8,128)S(1)}, f32[5,8,256]{2,1,0:T(8,128)S(1)}, u32[]{:S(2)}, u32[]{:S(2)}) %collective-permute-start.10) | collective-permute-done | bytes 40992 | tf_op jit(solution)/shard_map/ppermute | solution.py:166
  30.6 0.8 %x_finish.1 = (f32[32,8,256]{2,1,0:T(8,128)S(1)}, f32[3,2,8,256]{3,2,1,0:T(8,128)S(1)}, f32[8,256]{1,0:T(8,128)S(1)}, f32[32,8,256]{2,1,0:T(8,128)}) custom-call(f32[5,8,256]{2,1,0:T(8,128)S(1)} %get-tuple-element.43.own_ref.ends_ref, f32[5,8,256]{2,1,0:T(8,128)S(1)} %collective-permute-done.6.got_ref.other_ref, f32[5,8,256]{2,1,0:T(8,128)S(1)} %side.1.side_ref, ...), custom_call_target="tpu_custom_call" | custom-call | bytes 2285568 | tf_op jit(solution)/shard_map/x_finish/pallas_call | solution.py:20
  31.4 1.5 %collective-permute-start.13 = (f32[8,256]{1,0:T(8,128)S(1)}, f32[8,256]{1,0:T(8,128)S(1)}, u32[]{:S(2)}, u32[]{:S(2)}) collective-permute-start(f32[8,256]{1,0:T(8,128)S(1)} %get-tuple-element.48.own_ref), channel_id=1, source_target_pairs={{0,3},{1,0},{2,1},{3,2},{4,7},{5,4},{6,5},{7,6},{8,11},{9,8},{10,9... | collective-permute-start | bytes 24584 | tf_op jit(solution)/shard_map/ppermute | solution.py:406
  32.9 0.4 collective-permute-start.12
  33.3 0.7 %collective-permute-start.11 = (f32[8,256]{1,0:T(8,128)S(1)}, f32[8,256]{1,0:T(8,128)S(1)}, u32[]{:S(2)}, u32[]{:S(2)}) collective-permute-start(f32[8,256]{1,0:T(8,128)S(1)} %get-tuple-element.48.own_ref), channel_id=1, source_target_pairs={{0,1},{1,2},{2,3},{3,0},{4,5},{5,6},{6,7},{7,4},{8,9},{9,10},{10,1... | collective-permute-start | bytes 24584 | tf_op jit(solution)/shard_map/ppermute | solution.py:406
  34.0 0.0 collective-permute-done.13.refs_2_
  34.0 3.0 %collective-permute-done.12.refs_1_ = f32[8,256]{1,0:T(8,128)S(1)} collective-permute-done((f32[8,256]{1,0:T(8,128)S(1)}, f32[8,256]{1,0:T(8,128)S(1)}, u32[]{:S(2)}, u32[]{:S(2)}) %collective-permute-start.12) | collective-permute-done | bytes 8224 | tf_op jit(solution)/shard_map/ppermute | solution.py:406
  36.9 0.1 collective-permute-done.11.refs_0_
  37.0 0.3 y_finish.1
  37.4 0.1 collective-permute-start.14
  37.5 2.7 %collective-permute-start.15 = (f32[32,256]{1,0:T(8,128)S(1)}, f32[32,256]{1,0:T(8,128)S(1)}, u32[]{:S(2)}, u32[]{:S(2)}) collective-permute-start(f32[32,256]{1,0:T(8,128)S(1)} %get-tuple-element.56), channel_id=1, source_target_pairs={{64,0},{128,64},{192,128},{0,192},{65,1},{129,65},{193,129},{1,193... | collective-permute-start | bytes 98312 | tf_op jit(solution)/shard_map/ppermute | solution.py:160
  40.1 3.2 %collective-permute-start.16 = (f32[8,256]{1,0:T(8,128)S(1)}, f32[8,256]{1,0:T(8,128)S(1)}, u32[]{:S(2)}, u32[]{:S(2)}) collective-permute-start(f32[8,256]{1,0:T(8,128)S(1)} %get-tuple-element.57), channel_id=1, source_target_pairs={{0,60},{4,8},{8,4},{12,16},{16,12},{20,24},{24,20},{28,32},{32,28}... | collective-permute-start | bytes 24584 | tf_op jit(solution)/shard_map/ppermute | solution.py:163
  43.3 0.0 collective-permute-start.17
  43.3 0.1 turn.1.yd_ref
  43.5 1.2 %collective-permute-done.16.xc = f32[8,256]{1,0:T(8,128)S(1)} collective-permute-done((f32[8,256]{1,0:T(8,128)S(1)}, f32[8,256]{1,0:T(8,128)S(1)}, u32[]{:S(2)}, u32[]{:S(2)}) %collective-permute-start.16) | collective-permute-done | bytes 8224 | tf_op jit(solution)/shard_map/ppermute | solution.py:163
  44.7 0.0 collective-permute-done.17.xi
  44.7 0.0 collective-permute-done.14.below
  44.7 0.0 collective-permute-done.15.above
  44.7 0.9 %final.1 = f32[8,32,256]{2,1,0:T(8,128)} custom-call(f32[8,32,256]{2,1,0:T(8,128)S(1)} %get-tuple-element.53.s_ref, f32[8,32,256]{2,1,0:T(8,128)S(1)} %turn.1.yd_ref, bf16[3,8,32,256]{3,2,1,0:T(8,128)(2,1)S(1)} %get-tuple-element.32.wind_ref, f32[8,32,256]{2,1,0:T(8,128)S(1)} %copy-done, f32[32,256]{1,0:T(8,128)S(1)} %collective-permute-done.14.below, ...), custom_call_target="tpu_custom_call" | custom-call | bytes 1916928 | tf_op jit(solution)/shard_map/final/pallas_call | solution.py:20
  (4 shorter events, 0.1 us)
Async XLA Ops:
  0.0 13.4 %copy-start = (f32[8,32,256]{2,1,0:T(8,128)S(1)}, f32[8,32,256]{2,1,0:T(8,128)}, u32[]{:S(2)}) copy-start(f32[8,32,256]{2,1,0:T(8,128)} %k_ref.5) | copy-start | bytes 786436
  0.0 1.0 %copy-start.1 = (f32[8,32,256]{2,1,0:T(8,128)S(1)}, f32[8,32,256]{2,1,0:T(8,128)}, u32[]{:S(2)}) copy-start(f32[8,32,256]{2,1,0:T(8,128)} %f_ref.3) | copy-start | bytes 786436
  1.1 14.1 %collective-permute-start = (f32[32,256]{1,0:T(8,128)S(1)}, f32[32,256]{1,0:T(8,128)S(1)}, u32[]{:S(2)}, u32[]{:S(2)}) collective-permute-start(f32[32,256]{1,0:T(8,128)S(1)} %get-tuple-element.33), channel_id=1, source_target_pairs={{0,64},{64,128},{128,192},{192,0},{1,65},{65,129},{129,193},{193,1... | collective-permute-start | bytes 98312 | tf_op jit(solution)/shard_map/ppermute | solution.py:156
  3.2 12.0 %collective-permute-start.1 = (f32[32,256]{1,0:T(8,128)S(1)}, f32[32,256]{1,0:T(8,128)S(1)}, u32[]{:S(2)}, u32[]{:S(2)}) collective-permute-start(f32[32,256]{1,0:T(8,128)S(1)} %get-tuple-element.34), channel_id=1, source_target_pairs={{64,0},{128,64},{192,128},{0,192},{65,1},{129,65},{193,129},{1,193... | collective-permute-start | bytes 98312 | tf_op jit(solution)/shard_map/ppermute | solution.py:160
  4.6 6.1 %collective-permute-start.2 = (f32[8,256]{1,0:T(8,128)S(1)}, f32[8,256]{1,0:T(8,128)S(1)}, u32[]{:S(2)}, u32[]{:S(2)}) collective-permute-start(f32[8,256]{1,0:T(8,128)S(1)} %get-tuple-element.35), channel_id=1, source_target_pairs={{0,1},{1,2},{2,3},{3,0},{4,5},{5,6},{6,7},{7,4},{8,9},{9,10},{10,1... | collective-permute-start | bytes 24584 | tf_op jit(solution)/shard_map/ppermute | solution.py:156
  6.0 9.2 %collective-permute-start.3 = (f32[8,256]{1,0:T(8,128)S(1)}, f32[8,256]{1,0:T(8,128)S(1)}, u32[]{:S(2)}, u32[]{:S(2)}) collective-permute-start(f32[8,256]{1,0:T(8,128)S(1)} %get-tuple-element.36), channel_id=1, source_target_pairs={{1,0},{2,1},{3,2},{0,3},{5,4},{6,5},{7,6},{4,7},{9,8},{10,9},{11,1... | collective-permute-start | bytes 24584 | tf_op jit(solution)/shard_map/ppermute | solution.py:160
  7.4 7.7 %collective-permute-start.4 = (f32[8,256]{1,0:T(8,128)S(1)}, f32[8,256]{1,0:T(8,128)S(1)}, u32[]{:S(2)}, u32[]{:S(2)}) collective-permute-start(f32[8,256]{1,0:T(8,128)S(1)} %get-tuple-element.37), channel_id=1, source_target_pairs={{0,60},{4,8},{8,4},{12,16},{16,12},{20,24},{24,20},{28,32},{32,28}... | collective-permute-start | bytes 24584 | tf_op jit(solution)/shard_map/ppermute | solution.py:163
  10.7 4.5 %collective-permute-start.5 = (f32[8,256]{1,0:T(8,128)S(1)}, f32[8,256]{1,0:T(8,128)S(1)}, u32[]{:S(2)}, u32[]{:S(2)}) collective-permute-start(f32[8,256]{1,0:T(8,128)S(1)} %get-tuple-element.38), channel_id=1, source_target_pairs={{0,4},{4,0},{8,12},{12,8},{16,20},{20,16},{24,28},{28,24},{32,36},... | collective-permute-start | bytes 24584 | tf_op jit(solution)/shard_map/ppermute | solution.py:166
  13.4 1.0 %copy-start.2 = (bf16[3,8,32,256]{3,2,1,0:T(8,128)(2,1)S(1)}, bf16[3,8,32,256]{3,2,1,0:T(8,128)(2,1)}, u32[]{:S(2)}) copy-start(bf16[3,8,32,256]{3,2,1,0:T(8,128)(2,1)} %far_wind.1) | copy-start | bytes 1179652
  16.3 1.2 %collective-permute-start.6 = (f32[5,8,256]{2,1,0:T(8,128)S(1)}, f32[5,8,256]{2,1,0:T(8,128)S(1)}, u32[]{:S(2)}, u32[]{:S(2)}) collective-permute-start(f32[5,8,256]{2,1,0:T(8,128)S(1)} %get-tuple-element.43.own_ref.ends_ref), channel_id=1, source_target_pairs={{0,4},{4,0},{8,12},{12,8},{16,20},{20,16},{24,28},{28,24},{32,36},... | collective-permute-start | bytes 122888 | tf_op jit(solution)/shard_map/ppermute | solution.py:166
  17.6 5.5 %collective-permute-start.7 = (f32[5,8,256]{2,1,0:T(8,128)S(1)}, f32[5,8,256]{2,1,0:T(8,128)S(1)}, u32[]{:S(2)}, u32[]{:S(2)}) collective-permute-start(f32[5,8,256]{2,1,0:T(8,128)S(1)} %chip.1.own_ref), channel_id=1, source_target_pairs={{0,8},{4,60},{8,16},{12,4},{16,24},{20,12},{24,32},{28,20},{32,40}... | collective-permute-start | bytes 122888 | tf_op jit(solution)/shard_map/ppermute | solution.py:376
  20.6 6.8 %collective-permute-start.9 = (f32[5,8,256]{2,1,0:T(8,128)S(1)}, f32[5,8,256]{2,1,0:T(8,128)S(1)}, u32[]{:S(2)}, u32[]{:S(2)}) collective-permute-start(f32[5,8,256]{2,1,0:T(8,128)S(1)} %chip.1.own_ref), channel_id=1, source_target_pairs={{0,32},{4,36},{8,40},{12,44},{16,48},{20,52},{24,56},{28,60},{32,0... | collective-permute-start | bytes 122888 | tf_op jit(solution)/shard_map/ppermute | solution.py:376
  23.1 4.7 %collective-permute-start.8 = (f32[5,8,256]{2,1,0:T(8,128)S(1)}, f32[5,8,256]{2,1,0:T(8,128)S(1)}, u32[]{:S(2)}, u32[]{:S(2)}) collective-permute-start(f32[5,8,256]{2,1,0:T(8,128)S(1)} %pair.1), channel_id=1, source_target_pairs={{0,16},{4,52},{8,24},{12,60},{16,32},{20,4},{24,40},{28,12},{32,48... | collective-permute-start | bytes 122888 | tf_op jit(solution)/shard_map/ppermute | solution.py:376
  27.8 2.8 %collective-permute-start.10 = (f32[5,8,256]{2,1,0:T(8,128)S(1)}, f32[5,8,256]{2,1,0:T(8,128)S(1)}, u32[]{:S(2)}, u32[]{:S(2)}) collective-permute-start(f32[5,8,256]{2,1,0:T(8,128)S(1)} %side.1.side_ref), channel_id=1, source_target_pairs={{0,4},{4,0},{8,12},{12,8},{16,20},{20,16},{24,28},{28,24},{32,36},... | collective-permute-start | bytes 122888 | tf_op jit(solution)/shard_map/ppermute | solution.py:166
  31.4 2.6 %collective-permute-start.13 = (f32[8,256]{1,0:T(8,128)S(1)}, f32[8,256]{1,0:T(8,128)S(1)}, u32[]{:S(2)}, u32[]{:S(2)}) collective-permute-start(f32[8,256]{1,0:T(8,128)S(1)} %get-tuple-element.48.own_ref), channel_id=1, source_target_pairs={{0,3},{1,0},{2,1},{3,2},{4,7},{5,4},{6,5},{7,6},{8,11},{9,8},{10,9... | collective-permute-start | bytes 24584 | tf_op jit(solution)/shard_map/ppermute | solution.py:406
  32.9 4.0 %collective-permute-start.12 = (f32[8,256]{1,0:T(8,128)S(1)}, f32[8,256]{1,0:T(8,128)S(1)}, u32[]{:S(2)}, u32[]{:S(2)}) collective-permute-start(f32[8,256]{1,0:T(8,128)S(1)} %get-tuple-element.48.own_ref), channel_id=1, source_target_pairs={{0,2},{1,3},{2,0},{3,1},{4,6},{5,7},{6,4},{7,5},{8,10},{9,11},{10,... | collective-permute-start | bytes 24584 | tf_op jit(solution)/shard_map/ppermute | solution.py:406
  33.3 3.7 %collective-permute-start.11 = (f32[8,256]{1,0:T(8,128)S(1)}, f32[8,256]{1,0:T(8,128)S(1)}, u32[]{:S(2)}, u32[]{:S(2)}) collective-permute-start(f32[8,256]{1,0:T(8,128)S(1)} %get-tuple-element.48.own_ref), channel_id=1, source_target_pairs={{0,1},{1,2},{2,3},{3,0},{4,5},{5,6},{6,7},{7,4},{8,9},{9,10},{10,1... | collective-permute-start | bytes 24584 | tf_op jit(solution)/shard_map/ppermute | solution.py:406
  37.4 7.3 %collective-permute-start.14 = (f32[32,256]{1,0:T(8,128)S(1)}, f32[32,256]{1,0:T(8,128)S(1)}, u32[]{:S(2)}, u32[]{:S(2)}) collective-permute-start(f32[32,256]{1,0:T(8,128)S(1)} %get-tuple-element.55), channel_id=1, source_target_pairs={{0,64},{64,128},{128,192},{192,0},{1,65},{65,129},{129,193},{193,1... | collective-permute-start | bytes 98312 | tf_op jit(solution)/shard_map/ppermute | solution.py:156
  37.5 7.2 %collective-permute-start.15 = (f32[32,256]{1,0:T(8,128)S(1)}, f32[32,256]{1,0:T(8,128)S(1)}, u32[]{:S(2)}, u32[]{:S(2)}) collective-permute-start(f32[32,256]{1,0:T(8,128)S(1)} %get-tuple-element.56), channel_id=1, source_target_pairs={{64,0},{128,64},{192,128},{0,192},{65,1},{129,65},{193,129},{1,193... | collective-permute-start | bytes 98312 | tf_op jit(solution)/shard_map/ppermute | solution.py:160
  40.1 4.5 %collective-permute-start.16 = (f32[8,256]{1,0:T(8,128)S(1)}, f32[8,256]{1,0:T(8,128)S(1)}, u32[]{:S(2)}, u32[]{:S(2)}) collective-permute-start(f32[8,256]{1,0:T(8,128)S(1)} %get-tuple-element.57), channel_id=1, source_target_pairs={{0,60},{4,8},{8,4},{12,16},{16,12},{20,24},{24,20},{28,32},{32,28}... | collective-permute-start | bytes 24584 | tf_op jit(solution)/shard_map/ppermute | solution.py:163
  43.3 1.3 %collective-permute-start.17 = (f32[8,256]{1,0:T(8,128)S(1)}, f32[8,256]{1,0:T(8,128)S(1)}, u32[]{:S(2)}, u32[]{:S(2)}) collective-permute-start(f32[8,256]{1,0:T(8,128)S(1)} %get-tuple-element.58), channel_id=1, source_target_pairs={{0,4},{4,0},{8,12},{12,8},{16,20},{20,16},{24,28},{28,24},{32,36},... | collective-permute-start | bytes 24584 | tf_op jit(solution)/shard_map/ppermute | solution.py:166

commit v2 on v1

--- a/solution.py
+++ b/solution.py
@@ -12,17 +12,18 @@
 VMEM_BYTES = 24 * 2**20
 
 
-def call(kernel, outs, *ins, name, flops=0, far=(), scratch=()):
-    shapes = [jax.ShapeDtypeStruct(s, jnp.float32) if isinstance(s, tuple) else s for s in outs]
+def call(kernel, outs, *ins, name, flops=0, scratch=(), far_in=(), far_out=(), alias=None):
+    shapes = [jax.ShapeDtypeStruct(s, jnp.float32) for s in outs]
     vm = pl.BlockSpec(memory_space=pltpu.VMEM)
-    any_space = pl.BlockSpec(memory_space=pltpu.HBM)
+    far = pl.BlockSpec(memory_space=pl.ANY)
     size = 4 * (sum(x.size for x in ins) + sum(x.size for x in shapes))
     return pl.pallas_call(
         kernel,
         out_shape=shapes,
-        in_specs=[any_space if n in far else vm for n in range(len(ins))],
-        out_specs=[vm] * len(outs),
+        in_specs=[far if n in far_in else vm for n in range(len(ins))],
+        out_specs=[far if n in far_out else vm for n in range(len(outs))],
         scratch_shapes=list(scratch),
+        input_output_aliases=alias or {},
         compiler_params=pltpu.CompilerParams(vmem_limit_bytes=VMEM_BYTES),
         cost_estimate=pl.CostEstimate(flops=flops, bytes_accessed=size, transcendentals=0),
         name=name,
@@ -136,20 +137,41 @@
     c = reach * reach
     subs = 8
     steps = ny // subs
+    wide = -(-(lines + 2 * nz) // 128) * 128
+    order = (1, 3, 2)
 
     def core():
         return lax.rem(lax.axis_index("gx"), 2)
 
-    def faces_kernel(f_ref, zlo, zhi, ylo, yhi, xc, xi):
-        zlo[...] = f_ref[0]
-        zhi[...] = f_ref[nz - 1]
+    def faces_kernel(f_ref, own, give, xc):
+        odd = core() == 1
+        low, high = f_ref[0], f_ref[nz - 1]
+        own[0:nx] = jnp.where(odd, low, high)
+        give[0:nx] = jnp.where(odd, high, low)
         flat = f_ref[...].reshape(lines, ny)
-        ylo[...] = flat[:, :128].T[:8]
-        yhi[...] = flat[:, ny - 128 :].T[120:]
-        first, last = f_ref[:, 0, :], f_ref[:, nx - 1, :]
+        low = flat[:, :128].T[:1]
+        high = flat[:, ny - 128 :].T[127:]
+        pad = jnp.zeros((7, lines), jnp.float32)
+        own[nx : nx + 8] = jnp.concatenate([jnp.where(odd, low, high), pad], axis=0)
+        give[nx : nx + 8] = jnp.concatenate([jnp.where(odd, high, low), pad], axis=0)
+        xc[...], give[nx + 8 :] = x_faces(f_ref)
+
+    def x_faces(ref):
         odd = core() == 1
-        xc[...] = jnp.where(odd, last, first)
-        xi[...] = jnp.where(odd, first, last)
+        first, last = ref[:, 0, :], ref[:, nx - 1, :]
+        return jnp.where(odd, last, first), jnp.where(odd, first, last)
+
+    def both_faces_kernel(own, got, k_ref, f_ref, planes, columns_out, cross_out, inner):
+        planes[0:nx] = own[0:nx]
+        planes[nx:] = got[0:nx]
+        columns_out[0:8] = own[nx:]
+        columns_out[8:16] = got[nx : nx + 8]
+        cross_out[0] = f_ref[...]
+        cross_out[1], inner[...] = x_faces(k_ref)
+
+    def relay_kernel(planes, columns_in, out_ref):
+        out_ref[0:nx] = planes[nx:]
+        out_ref[nx:] = columns_in[8:16]
 
     def up(a, axis):
         n = lax.axis_size(axis)
@@ -159,33 +181,57 @@
         n = lax.axis_size(axis)
         return lax.ppermute(a, axis, [((i + 1) % n, i) for i in range(n)])
 
+    def y_outward(a):
+        pairs = []
+        for x in range(members):
+            for y in range(columns):
+                pairs.append((x * columns + y, x * columns + (y + (-1 if x % 2 else 1)) % columns))
+        return lax.ppermute(a, ("gx", "gy"), pairs)
+
+    def z_outward(a):
+        pairs = []
+        for z in range(levels):
+            for x in range(members):
+                pairs.append((z * members + x, (z + (-1 if x % 2 else 1)) % levels * members + x))
+        return lax.ppermute(a, ("gz", "gx"), pairs)
+
     def across(a):
         return lax.ppermute(a, "gx", [(i, (i + 1 if i % 2 else i - 1) % members) for i in range(members)])
 
     def sibling(a):
         return lax.ppermute(a, "gx", [(i, i ^ 1) for i in range(members)])
 
+    def x_sides(cross, inner):
+        odd = core() == 1
+        return jnp.where(odd, inner, cross), jnp.where(odd, cross, inner)
+
     def x_rows(cross, inner):
         index = lax.axis_index("gx")
-        odd = core() == 1
-        west = jnp.where(index == 0, 0.0, jnp.where(odd, inner, cross))
-        east = jnp.where(index == members - 1, 0.0, jnp.where(odd, cross, inner))
-        return west, east
+        west, east = x_sides(cross, inner)
+        return jnp.where(index == 0, 0.0, west), jnp.where(index == members - 1, 0.0, east)
 
     def z_planes(below, above):
         index = lax.axis_index("gz")
         return jnp.where(index == 0, 0.0, below), jnp.where(index == levels - 1, 0.0, above)
 
-    def matrix_kernel(
-        k_ref, far_wind, d_ref, w_ref, l_ref, r_ref, yd_ref, yw_ref, yl_ref, yr_ref, c_ref, wind_ref, sem
-    ):
-        fetch = pltpu.make_async_copy(far_wind, wind_ref, sem)
-        fetch.start()
+    def x_matrix_kernel(k_ref, d_ref, w_ref, l_ref, r_ref):
         d_ref[...] = 1.0 / (c * jnp.swapaxes(k_ref[...], 0, 1))
         factor(d_ref, w_ref, l_ref, r_ref, nx)
-        yd_ref[...] = jnp.swapaxes(d_ref[...].reshape(lines, ny).T.reshape(subs, steps, lines), 0, 1)
-        factor(yd_ref, yw_ref, yl_ref, yr_ref, steps)
-        L, C, R = yl_ref[0], yr_ref[0], yr_ref[steps - 1]
+
+    def y_matrix_kernel(x_ref, xc, other_ref, d_ref, w_ref, l_ref, r_ref, c_ref):
+        west, east = x_sides(xc[1], other_ref[5])
+        d = jnp.concatenate(
+            [
+                x_ref[...].reshape(lines, ny),
+                1.0 / (c * west),
+                1.0 / (c * east),
+                jnp.ones((wide - lines - 2 * nz, ny), jnp.float32),
+            ],
+            axis=0,
+        )
+        d_ref[...] = jnp.swapaxes(d.T.reshape(subs, steps, wide), 0, 1)
+        factor(d_ref, w_ref, l_ref, r_ref, steps)
+        L, C, R = l_ref[0], r_ref[0], r_ref[steps - 1]
         for level in range(3):
             shift = subs - (1 << level)
             bL, bC, bR = pltpu.roll(L, shift, 0), pltpu.roll(C, shift, 0), pltpu.roll(R, shift, 0)
@@ -198,17 +244,18 @@
             c_ref[3, n] = value
         for n in range(3, 7):
             c_ref[3, n] = jnp.zeros_like(L)
-        fetch.wait()
 
     def explicit_kernel(
-        f_ref, wind_ref, k_ref, below, above, south, north, xc, xi, d_ref, w_ref, l_ref, r_ref,
+        f_ref, wind_ref, k_ref, planes, columns_in, relayed, xc, got, kin, d_ref, w_ref, l_ref, r_ref,
         base_ref, ends_ref, e_ref,
     ):
-        west, east = x_rows(xc[...], xi[...])
-        low, high = z_planes(below[...], above[...])
+        west, east = x_rows(xc[0], got[nx + 8 :])
+        odd = core() == 1
+        low, high = z_planes(*choose(odd, (relayed[0:nx], planes[0:nx]), (planes[0:nx], relayed[0:nx])))
         gy = lax.axis_index("gy")
-        left = jnp.where(gy == 0, 0.0, south[7:8])
-        right = jnp.where(gy == columns - 1, 0.0, north[0:1])
+        near, far = columns_in[0:1], relayed[nx : nx + 1]
+        left = jnp.where(gy == 0, 0.0, jnp.where(odd, far, near))
+        right = jnp.where(gy == columns - 1, 0.0, jnp.where(odd, near, far))
         left = jnp.broadcast_to(left, (128, lines)).T
         right = jnp.broadcast_to(right, (128, lines)).T
         lane = lax.broadcasted_iota(jnp.int32, (nx, 128), 1)
@@ -227,7 +274,7 @@
             )
         e = jnp.swapaxes(e_ref[...], 0, 1)
         sweep(lambda i: e[i] * d_ref[i], w_ref, base_ref, nx)
-        ends = (base_ref[0], base_ref[nx - 1], l_ref[0], r_ref[0], r_ref[nx - 1])
+        ends = (base_ref[0], base_ref[nx - 1], l_ref[0], r_ref[0], r_ref[nx - 1], kin[...])
         for n, v in enumerate(ends):
             ends_ref[n] = v
 
@@ -287,8 +334,11 @@
         after = jnp.where(odd, rp + rg * last_b, first_b)
         for i in range(nx):
             s_ref[i] = base_ref[i] + l_ref[i] * before + r_ref[i] * after
-        t = s_ref[...].reshape(lines, ny).T
-        q = jnp.swapaxes(t.reshape(subs, steps, lines), 0, 1)
+        s_ref[nx], s_ref[nx + 1] = before, after
+        for i in range(nx + 2, wide // nz):
+            s_ref[i] = zero
+        t = s_ref[...].reshape(wide, ny).T
+        q = jnp.swapaxes(t.reshape(subs, steps, wide), 0, 1)
         sweep(lambda i: q[i] * d_ref[i], w_ref, ybase_ref, steps)
         b0, b1 = ybase_ref[0], ybase_ref[steps - 1]
         for level in range(3):
@@ -301,16 +351,16 @@
             b0, b1 = b0 + x * (o0 + bL * b1), o1 + y * inner
         for n, v in enumerate((b0, b1, c_ref[3, 0], c_ref[3, 1], c_ref[3, 2])):
             send_ref[n : n + 1] = v[0:1]
-        send_ref[5:8] = jnp.zeros((3, lines), jnp.float32)
+        send_ref[5:8] = jnp.zeros((3, wide), jnp.float32)
 
     def y_finish_kernel(
         own_ref, *refs,
     ):
-        got, (ybase_ref, up_ref, l_ref, r_ref, c_ref), (s_ref, yd_ref, xc, xi, zlo, zhi) = (
+        got, (ybase_ref, up_ref, l_ref, r_ref, c_ref), (s_ref, t_ref, ends_ref, west, east, zlo, zhi) = (
             refs[: columns - 1], refs[columns - 1 : columns + 4], refs[columns + 4 :],
         )
         index = lax.axis_index("gy")
-        messages = [own_ref[...]] + [ref[...] for ref in got]
+        messages = {0: own_ref[...]} | {back: ref[...] for back, ref in zip(order, got)}
         blocks = []
         for m in range(columns):
             v = messages[0]
@@ -324,9 +374,9 @@
         right = rp + rg * last
         first = (mine[0] + mine[2] * lp + mine[3] * right) / (1.0 - mine[2] * lg)
         left = lp + lg * first
-        sub = lax.broadcasted_iota(jnp.int32, (subs, lines), 0)
-        L = jnp.broadcast_to(left, (subs, lines))
-        R = jnp.broadcast_to(right, (subs, lines))
+        sub = lax.broadcasted_iota(jnp.int32, (subs, wide), 0)
+        L = jnp.broadcast_to(left, (subs, wide))
+        R = jnp.broadcast_to(right, (subs, wide))
         for level in (2, 1, 0):
             step = 1 << level
             x, _, bL, _, bC, _, z = (c_ref[level, n] for n in range(7))
@@ -337,60 +387,93 @@
                 jnp.where(upper, pltpu.roll(a, step, 0), L),
                 jnp.where(upper, pltpu.roll(R, step, 0), b),
             )
+        ends_ref[...] = jnp.concatenate([left, right], axis=0)
         for i in range(steps):
-            ybase_ref_i = ybase_ref[i] + l_ref[i] * L + r_ref[i] * R
-            yd_ref[i] = ybase_ref_i
-        s = jnp.swapaxes(yd_ref[...].reshape(steps, subs, lines), 0, 1).reshape(ny, lines)
-        row = lax.broadcasted_iota(jnp.int32, s.shape, 0)
-        north = jnp.where(row == ny - 1, right, pltpu.roll(s, ny - 1, 0))
-        south = jnp.where(row == 0, left, pltpu.roll(s, 1, 0))
-        yd_ref[...] = (north - south).reshape(yd_ref.shape)
-        t = s.T
-        odd = core() == 1
-        low, high = t[:nz], t[lines - nz :]
-        xc[...] = jnp.where(odd, high, low)
-        xi[...] = jnp.where(odd, low, high)
-        s_ref[...] = jnp.swapaxes(t.reshape(nx, nz, ny), 0, 1)
+            t_ref[i] = ybase_ref[i] + l_ref[i] * L + r_ref[i] * R
+        for first in range(0, wide, 128):
+            t = by_rows(t_ref, first).T
+            if first < lines:
+                rows = slice(first // nz, (first + 128) // nz)
+                s_ref[:, rows, :] = jnp.swapaxes(t.reshape(128 // nz, nz, ny), 0, 1)
+            else:
+                west[...] = t[:nz]
+                east[...] = t[nz : 2 * nz]
         zlo[...] = s_ref[0]
         zhi[...] = s_ref[nz - 1]
 
-    def turn_kernel(yd_ref, out_ref):
-        out_ref[...] = jnp.swapaxes(yd_ref[...].reshape(ny, lines).T.reshape(nx, nz, ny), 0, 1)
-
-    def final_kernel(s_ref, yd_ref, wind_ref, k_ref, below, above, xc, xi, out_ref):
-        west, east = x_rows(xc[...], xi[...])
-        low, high = z_planes(below[...], above[...])
+    def by_rows(ref, first):
+        return jnp.swapaxes(ref[:, :, first : first + 128], 0, 1).reshape(ny, 128)
+
+    def inner_kernel(
+        t_ref, ends_ref, s_ref, wind_ref, k_ref, west, east, out_ref, edge_ref, factor_ref, yd_ref, buffer, sems
+    ):
+        for first in range(0, lines, 128):
+            s = by_rows(t_ref, first)
+            left, right = (ends_ref[n : n + 1, first : first + 128] for n in range(2))
+            row = lax.broadcasted_iota(jnp.int32, s.shape, 0)
+            north = jnp.where(row == ny - 1, right, pltpu.roll(s, ny - 1, 0))
+            south = jnp.where(row == 0, left, pltpu.roll(s, 1, 0))
+            rows = slice(first // nz, (first + 128) // nz)
+            yd_ref[:, rows, :] = jnp.swapaxes((north - south).T.reshape(128 // nz, nz, ny), 0, 1)
+        none = jnp.zeros((nx, ny), jnp.float32)
+        copies = []
         for z in range(nz):
-            out_ref[z] = stencil(
+            value = stencil(
                 z, s_ref[z],
-                s_ref[z - 1] if z else low,
-                s_ref[z + 1] if z < nz - 1 else high,
+                s_ref[z - 1] if z else none,
+                s_ref[z + 1] if z < nz - 1 else none,
                 west[z : z + 1], east[z : z + 1], yd_ref[z], wind_ref, k_ref[z],
             )
-
-    box, xbox, ybox = (nz, nx, ny), (nx, nz, ny), (steps, subs, lines)
+            if 0 < z < nz - 1:
+                buffer[z - 1] = value
+                copies.append(pltpu.make_async_copy(buffer.at[z - 1], out_ref.at[z], sems.at[z - 1]))
+                copies[-1].start()
+            else:
+                n = 1 if z else 0
+                edge_ref[n] = value
+                lift = QUARTER * wind_ref[0, z].astype(jnp.float32)
+                factor_ref[n] = VERTICAL * k_ref[z] + (-lift if n else lift)
+        for copy in copies:
+            copy.wait()
+
+    def final_kernel(part_ref, edge_ref, factor_ref, first, second, out_ref, buffer, sems):
+        low, high = z_planes(first[...], second[...])
+        buffer[0] = edge_ref[0] + factor_ref[0] * low
+        buffer[1] = edge_ref[1] + factor_ref[1] * high
+        copies = [pltpu.make_async_copy(buffer.at[n], out_ref.at[z], sems.at[n]) for n, z in enumerate((0, nz - 1))]
+        for copy in copies:
+            copy.start()
+        for copy in copies:
+            copy.wait()
+
+    box, xbox, ybox = (nz, nx, ny), (nx, nz, ny), (steps, subs, wide)
     five = (5, nz, ny)
 
     def outward(a, distance):
         move = lambda i: ((i // 2 + (-distance if i % 2 else distance)) % chips) * 2 + i % 2
         return lax.ppermute(a, "gx", [(i, move(i)) for i in range(members)])
 
-    zlo, zhi, ylo, yhi, xc, xi = call(
-        faces_kernel, [(nx, ny), (nx, ny), (8, lines), (8, lines), (nz, ny), (nz, ny)], field, name="faces"
-    )
-    xc, xi = across(xc), sibling(xi)
-    below, above = up(zhi, "gz"), down(zlo, "gz")
-    south, north = up(yhi, "gy"), down(ylo, "gy")
-    dx, wx, lx, rx, dy, wy, ly, ry, cy, near_wind = call(
-        matrix_kernel,
-        [xbox] * 4 + [ybox] * 4 + [(4, 7, subs, lines), jax.ShapeDtypeStruct(wind.shape, wind.dtype)],
-        rate, wind, name="matrix", flops=10**6, far=(1,), scratch=[pltpu.SemaphoreType.DMA],
-    )
-    base, ends, _ = call(
-        explicit_kernel, [xbox, five, box],
-        field, near_wind, rate, below, above, south, north, xc, xi, dx, wx, lx, rx, name="explicit",
+    own, give, xc = call(
+        faces_kernel, [(nx + 8, ny), (nx + 8 + nz, ny), (nz, ny)], field, name="faces", flops=10**10
+    )
+    got = sibling(give)
+    planes, edges, xc, kin = call(
+        both_faces_kernel, [(2 * nx, ny), (16, lines), (2, nz, ny), (nz, ny)], own, got, rate, xc, name="both_faces"
+    )
+    planes, edges = z_outward(planes), y_outward(edges)
+    (relay,) = call(relay_kernel, [(nx + 8, ny)], planes, edges, name="relay")
+    relayed = sibling(relay)
+    xc = across(xc)
+    dx, wx, lx, rx = call(x_matrix_kernel, [xbox] * 4, rate, name="x_matrix", flops=5 * 10**9)
+    base, ends = call(
+        explicit_kernel, [xbox, (6, nz, ny)],
+        field, wind, rate, planes, edges, relayed, xc, got, kin, dx, wx, lx, rx, name="explicit",
+        scratch=[pltpu.VMEM(box, jnp.float32)],
     )
     other = sibling(ends)
+    dy, wy, ly, ry, cy = call(
+        y_matrix_kernel, [ybox] * 4 + [(4, 7, subs, wide)], dx, xc, other, name="y_matrix", flops=10**6
+    )
     (chip,) = call(chip_kernel, [five], ends, other, name="chip")
     opposite = outward(chip, chips // 2)
     near = outward(chip, 1)
@@ -398,22 +481,34 @@
     distant = outward(pair, 2)
     (side,) = call(side_kernel, [five], near, distant, opposite, name="side")
     facing = sibling(side)
-    ybase, ups, send, _ = call(
-        x_finish_kernel, [ybox, (3, 2, subs, lines), (8, lines), xbox],
+    ybase, ups, send = call(
+        x_finish_kernel, [ybox, (3, 2, subs, wide), (8, wide)],
         ends, other, side, facing, base, lx, rx, dy, wy, cy, name="x_finish",
+        scratch=[pltpu.VMEM((wide // nz, nz, ny), jnp.float32)],
     )
     ring = [
         lax.ppermute(send, "gy", [(i, (i + back) % columns) for i in range(columns)])
-        for back in range(1, columns)
+        for back in order
     ]
-    swept, yd, xc, xi, zlo, zhi = call(
-        y_finish_kernel, [box, ybox, (nz, ny), (nz, ny), (nx, ny), (nx, ny)],
+    swept, turned, sides, west, east, zlo, zhi = call(
+        y_finish_kernel, [box, ybox, (2, wide), (nz, ny), (nz, ny), (nx, ny), (nx, ny)],
         send, *ring, ybase, ups, ly, ry, cy, name="y_finish",
     )
-    xc, xi = across(xc), sibling(xi)
     below, above = up(zhi, "gz"), down(zlo, "gz")
-    (ydiff,) = call(turn_kernel, [box], yd, name="turn", flops=10**6)
-    (out,) = call(final_kernel, [box], swept, ydiff, near_wind, rate, below, above, xc, xi, name="final")
+    plane_pair = (2, nx, ny)
+    part, edge, factors = call(
+        inner_kernel, [box, plane_pair, plane_pair],
+        turned, sides, swept, wind, rate, west, east, name="inner", flops=5 * 10**9, far_out=(0,),
+        scratch=[
+            pltpu.VMEM(box, jnp.float32),
+            pltpu.VMEM((nz - 2, nx, ny), jnp.float32),
+            pltpu.SemaphoreType.DMA((nz - 2,)),
+        ],
+    )
+    (out,) = call(
+        final_kernel, [box], part, edge, factors, below, above, name="final", far_in=(0,), far_out=(0,), alias={0: 0},
+        scratch=[pltpu.VMEM(plane_pair, jnp.float32), pltpu.SemaphoreType.DMA((2,))],
+    )
     return out
 
 

time: 45.7 us -> 43.5 us (0.952)
  the two profiles are of different devices: /device:TPU:1 before, /device:TPU:2 now
where the time goes in v2:
time: 43.5 us; the launch traced here: 42.7 us
  starting transfers between devices  22.8 us (52%)
  waiting for transfers between devices  14.5 us (33%)
  Pallas kernels  4.22 us (10%)
  local copies, waits for them, and re-layouts  1.01 us (2%)
    ppermute x3, starting transfers between devices, outward(): return lax.ppermute(a, 'gx', [(i, move(i)) for i in range(members)])  7.54 us
    ppermute x1, starting transfers between devices, across(): lax.ppermute(a, 'gx', [(i, (i + 1 if i % 2 else i - 1) % members) for i i...  5.54 us
    ppermute x3, waiting for transfers between devices, outward(): return lax.ppermute(a, 'gx', [(i, move(i)) for i in range(members)])  4.64 us
    pallas_call x13, Pallas kernels, call(): pl.pallas_call(kernel, out_shape=shapes, in_specs=[far if n in far_in els...  4.22 us
    ppermute x3, starting transfers between devices, body(): lax.ppermute(send, 'gy', [(i, (i + back) % columns) for i in range(column...  4.09 us
    ppermute x3, waiting for transfers between devices, body(): lax.ppermute(send, 'gy', [(i, (i + back) % columns) for i in range(column...  3.93 us
    ppermute x4, waiting for transfers between devices, sibling(): return lax.ppermute(a, 'gx', [(i, i ^ 1) for i in range(members)])  3.04 us
    ppermute x1, starting transfers between devices, y_outward(): return lax.ppermute(a, ('gx', 'gy'), pairs)  1.58 us
  transfers between devices with their start and end apart: 15, of which 11 were waited for; matrix products, arithmetic and copies ran while one was open for 0% of the time, Pallas kernels for 5%

profile of v2, /device:TPU:2, one launch (start us, length us, event | category | flops | bytes accessed | tf_op | source)
XLA Modules:
  0.0 42.7 jit_solution(6691249799899888324)
XLA Ops:
  0.0 0.0 copy-start
  0.0 0.0 copy-start.2
  0.0 1.0 %copy-done.2 = f32[8,32,256]{2,1,0:T(8,128)S(1)} copy-done((f32[8,32,256]{2,1,0:T(8,128)S(1)}, f32[8,32,256]{2,1,0:T(8,128)}, u32[]{:S(2)}) %copy-start.2) | copy-done | bytes 262168
  1.0 0.1 faces.1
  1.1 0.1 collective-permute-start
  1.2 1.2 %collective-permute-done.got = f32[48,256]{1,0:T(8,128)S(1)} collective-permute-done((f32[48,256]{1,0:T(8,128)S(1)}, f32[48,256]{1,0:T(8,128)S(1)}, u32[]{:S(2)}, u32[]{:S(2)}) %collective-permute-start) | collective-permute-done | bytes 49184 | tf_op jit(solution)/shard_map/ppermute | solution.py:202
  2.4 0.0 copy-done
  2.5 1.6 %collective-permute-start.1 = (f32[64,256]{1,0:T(8,128)S(1)}, f32[64,256]{1,0:T(8,128)S(1)}, u32[]{:S(2)}, u32[]{:S(2)}) collective-permute-start(f32[64,256]{1,0:T(8,128)S(1)} %get-tuple-element.39), channel_id=1, source_target_pairs={{0,64},{4,196},{8,72},{12,204},{16,80},{20,212},{24,88},{28,220},{... | collective-permute-start | bytes 196616 | tf_op jit(solution)/shard_map/ppermute | solution.py:196
  4.0 1.6 %collective-permute-start.2 = (f32[16,256]{1,0:T(8,128)S(1)}, f32[16,256]{1,0:T(8,128)S(1)}, u32[]{:S(2)}, u32[]{:S(2)}) collective-permute-start(f32[16,256]{1,0:T(8,128)S(1)} %get-tuple-element.40), channel_id=1, source_target_pairs={{0,1},{1,2},{2,3},{3,0},{4,7},{5,4},{6,5},{7,6},{8,9},{9,10},{10,1... | collective-permute-start | bytes 49160 | tf_op jit(solution)/shard_map/ppermute | solution.py:189
  5.6 5.5 %collective-permute-start.4 = (f32[2,8,256]{2,1,0:T(8,128)S(1)}, f32[2,8,256]{2,1,0:T(8,128)S(1)}, u32[]{:S(2)}, u32[]{:S(2)}) collective-permute-start(f32[2,8,256]{2,1,0:T(8,128)S(1)} %get-tuple-element.41), channel_id=1, source_target_pairs={{0,60},{4,8},{8,4},{12,16},{16,12},{20,24},{24,20},{28,32},{32,28}... | collective-permute-start | bytes 49160 | tf_op jit(solution)/shard_map/ppermute | solution.py:199
  11.2 0.0 collective-permute-done.2.columns_in
  11.2 0.0 collective-permute-done.1.planes
  11.2 0.0 copy-start.1
  11.2 0.0 copy-start.3
  11.2 0.1 collective-permute-start.3
  11.3 0.4 x_matrix.1
  11.7 0.9 %collective-permute-done.4.xc = f32[2,8,256]{2,1,0:T(8,128)S(1)} collective-permute-done((f32[2,8,256]{2,1,0:T(8,128)S(1)}, f32[2,8,256]{2,1,0:T(8,128)S(1)}, u32[]{:S(2)}, u32[]{:S(2)}) %collective-permute-start.4) | collective-permute-done | bytes 16416 | tf_op jit(solution)/shard_map/ppermute | solution.py:199
  12.6 0.0 collective-permute-done.3.relayed
  12.6 0.0 copy-done.1
  12.6 0.0 copy-done.3
  12.6 0.5 %explicit.1 = (f32[32,8,256]{2,1,0:T(8,128)S(1)}, f32[6,8,256]{2,1,0:T(8,128)S(1)}) custom-call(f32[8,32,256]{2,1,0:T(8,128)S(1)} %copy-done.3, bf16[3,8,32,256]{3,2,1,0:T(8,128)(2,1)S(1)} %copy-done.1, f32[8,32,256]{2,1,0:T(8,128)S(1)} %copy-done, f32[64,256]{1,0:T(8,128)S(1)} %collective-permute-done.1.planes, ...), custom_call_target="tpu_custom_call" | custom-call | bytes 2867200 | tf_op jit(solution)/shard_map/explicit/pallas_call | solution.py:20
  13.1 0.1 collective-permute-start.5
  13.3 1.2 %collective-permute-done.5.got_ref.other_ref = f32[6,8,256]{2,1,0:T(8,128)S(1)} collective-permute-done((f32[6,8,256]{2,1,0:T(8,128)S(1)}, f32[6,8,256]{2,1,0:T(8,128)S(1)}, u32[]{:S(2)}, u32[]{:S(2)}) %collective-permute-start.5) | collective-permute-done | bytes 49184 | tf_op jit(solution)/shard_map/ppermute | solution.py:202
  14.5 0.1 collective-permute-start.6
  14.6 5.9 %collective-permute-start.8 = (f32[5,8,256]{2,1,0:T(8,128)S(1)}, f32[5,8,256]{2,1,0:T(8,128)S(1)}, u32[]{:S(2)}, u32[]{:S(2)}) collective-permute-start(f32[5,8,256]{2,1,0:T(8,128)S(1)} %chip.1.own_ref), channel_id=1, source_target_pairs={{0,32},{4,36},{8,40},{12,44},{16,48},{20,52},{24,56},{28,60},{32,0... | collective-permute-start | bytes 122888 | tf_op jit(solution)/shard_map/ppermute | solution.py:454
  20.5 0.0 collective-permute-done.6.got_ref.near_ref
  20.5 1.5 %collective-permute-start.7 = (f32[5,8,256]{2,1,0:T(8,128)S(1)}, f32[5,8,256]{2,1,0:T(8,128)S(1)}, u32[]{:S(2)}, u32[]{:S(2)}) collective-permute-start(f32[5,8,256]{2,1,0:T(8,128)S(1)} %pair.1), channel_id=1, source_target_pairs={{0,16},{4,52},{8,24},{12,60},{16,32},{20,4},{24,40},{28,12},{32,48... | collective-permute-start | bytes 122888 | tf_op jit(solution)/shard_map/ppermute | solution.py:454
  22.1 0.9 %collective-permute-done.8.opposite_ref = f32[5,8,256]{2,1,0:T(8,128)S(1)} collective-permute-done((f32[5,8,256]{2,1,0:T(8,128)S(1)}, f32[5,8,256]{2,1,0:T(8,128)S(1)}, u32[]{:S(2)}, u32[]{:S(2)}) %collective-permute-start.8) | collective-permute-done | bytes 40992 | tf_op jit(solution)/shard_map/ppermute | solution.py:454
  22.9 3.8 %collective-permute-done.7.far_ref = f32[5,8,256]{2,1,0:T(8,128)S(1)} collective-permute-done((f32[5,8,256]{2,1,0:T(8,128)S(1)}, f32[5,8,256]{2,1,0:T(8,128)S(1)}, u32[]{:S(2)}, u32[]{:S(2)}) %collective-permute-start.7) | collective-permute-done | bytes 40992 | tf_op jit(solution)/shard_map/ppermute | solution.py:454
  26.7 0.1 collective-permute-start.9
  26.8 0.6 %y_matrix.1 = (f32[32,8,384]{2,1,0:T(8,128)S(1)}, f32[32,8,384]{2,1,0:T(8,128)S(1)}, f32[32,8,384]{2,1,0:T(8,128)S(1)}, f32[32,8,384]{2,1,0:T(8,128)S(1)}, f32[4,7,8,384]{3,2,1,0:T(8,128)S(1)}) custom-call(f32[32,8,256]{2,1,0:T(8,128)S(1)} %get-tuple-element.43.d_ref.x_ref, f32[2,8,256]{2,1,0:T(8,128)S(1)} %collective-permute-done.4.xc, ...), custom_call_target="tpu_custom_call" | custom-call | flops 1000000 | bytes 2244608 | tf_op jit(solution)/shard_map/y_matrix/pallas_call | solution.py:20
  27.4 0.6 %collective-permute-done.9.got_ref = f32[5,8,256]{2,1,0:T(8,128)S(1)} collective-permute-done((f32[5,8,256]{2,1,0:T(8,128)S(1)}, f32[5,8,256]{2,1,0:T(8,128)S(1)}, u32[]{:S(2)}, u32[]{:S(2)}) %collective-permute-start.9) | collective-permute-done | bytes 40992 | tf_op jit(solution)/shard_map/ppermute | solution.py:202
  28.0 0.4 x_finish.1
  28.4 2.1 %collective-permute-start.12 = (f32[8,384]{1,0:T(8,128)S(1)}, f32[8,384]{1,0:T(8,128)S(1)}, u32[]{:S(2)}, u32[]{:S(2)}) collective-permute-start(f32[8,384]{1,0:T(8,128)S(1)} %get-tuple-element.52.own_ref), channel_id=1, source_target_pairs={{0,2},{1,3},{2,0},{3,1},{4,6},{5,7},{6,4},{7,5},{8,10},{9,11},{10,... | collective-permute-start | bytes 36872 | tf_op jit(solution)/shard_map/ppermute | solution.py:490
  30.5 1.1 %collective-permute-start.11 = (f32[8,384]{1,0:T(8,128)S(1)}, f32[8,384]{1,0:T(8,128)S(1)}, u32[]{:S(2)}, u32[]{:S(2)}) collective-permute-start(f32[8,384]{1,0:T(8,128)S(1)} %get-tuple-element.52.own_ref), channel_id=1, source_target_pairs={{0,3},{1,0},{2,1},{3,2},{4,7},{5,4},{6,5},{7,6},{8,11},{9,8},{10,9... | collective-permute-start | bytes 36872 | tf_op jit(solution)/shard_map/ppermute | solution.py:490
  31.6 1.0 %collective-permute-start.10 = (f32[8,384]{1,0:T(8,128)S(1)}, f32[8,384]{1,0:T(8,128)S(1)}, u32[]{:S(2)}, u32[]{:S(2)}) collective-permute-start(f32[8,384]{1,0:T(8,128)S(1)} %get-tuple-element.52.own_ref), channel_id=1, source_target_pairs={{0,1},{1,2},{2,3},{3,0},{4,5},{5,6},{6,7},{7,4},{8,9},{9,10},{10,1... | collective-permute-start | bytes 36872 | tf_op jit(solution)/shard_map/ppermute | solution.py:490
  32.5 1.2 %collective-permute-done.12.refs_2_ = f32[8,384]{1,0:T(8,128)S(1)} collective-permute-done((f32[8,384]{1,0:T(8,128)S(1)}, f32[8,384]{1,0:T(8,128)S(1)}, u32[]{:S(2)}, u32[]{:S(2)}) %collective-permute-start.12) | collective-permute-done | bytes 12320 | tf_op jit(solution)/shard_map/ppermute | solution.py:490
  33.7 0.5 %collective-permute-done.11.refs_1_ = f32[8,384]{1,0:T(8,128)S(1)} collective-permute-done((f32[8,384]{1,0:T(8,128)S(1)}, f32[8,384]{1,0:T(8,128)S(1)}, u32[]{:S(2)}, u32[]{:S(2)}) %collective-permute-start.11) | collective-permute-done | bytes 12320 | tf_op jit(solution)/shard_map/ppermute | solution.py:490
  34.2 2.3 %collective-permute-done.10.refs_0_ = f32[8,384]{1,0:T(8,128)S(1)} collective-permute-done((f32[8,384]{1,0:T(8,128)S(1)}, f32[8,384]{1,0:T(8,128)S(1)}, u32[]{:S(2)}, u32[]{:S(2)}) %collective-permute-start.10) | collective-permute-done | bytes 12320 | tf_op jit(solution)/shard_map/ppermute | solution.py:490
  36.5 0.4 y_finish.1
  36.8 1.3 %collective-permute-start.13 = (f32[32,256]{1,0:T(8,128)S(1)}, f32[32,256]{1,0:T(8,128)S(1)}, u32[]{:S(2)}, u32[]{:S(2)}) collective-permute-start(f32[32,256]{1,0:T(8,128)S(1)} %get-tuple-element.65), channel_id=1, source_target_pairs={{0,64},{64,128},{128,192},{192,0},{1,65},{65,129},{129,193},{193,1... | collective-permute-start | bytes 98312 | tf_op jit(solution)/shard_map/ppermute | solution.py:178
  38.1 0.8 %collective-permute-start.14 = (f32[32,256]{1,0:T(8,128)S(1)}, f32[32,256]{1,0:T(8,128)S(1)}, u32[]{:S(2)}, u32[]{:S(2)}) collective-permute-start(f32[32,256]{1,0:T(8,128)S(1)} %get-tuple-element.66), channel_id=1, source_target_pairs={{64,0},{128,64},{192,128},{0,192},{65,1},{129,65},{193,129},{1,193... | collective-permute-start | bytes 98312 | tf_op jit(solution)/shard_map/ppermute | solution.py:182
  38.9 1.1 %inner.1 = (f32[8,32,256]{2,1,0:T(8,128)}, f32[2,32,256]{2,1,0:T(8,128)S(1)}, f32[2,32,256]{2,1,0:T(8,128)S(1)}) custom-call(f32[32,8,384]{2,1,0:T(8,128)S(1)} %get-tuple-element.57.t_ref, f32[2,384]{1,0:T(2,128)S(1)} %get-tuple-element.58.ends_ref, f32[8,32,256]{2,1,0:T(8,128)S(1)} %get-tuple-element.59.s_ref, bf16[3,8,32,256]{3,2,1,0:T(8,128)(2,1)S(1)} %copy-done.1, ...), custom_call_target="tpu_custom_call" | custom-call | flops 5000000000 | bytes 2116608 | tf_op jit(solution)/shard_map/inner/pallas_call | solution.py:20
  40.0 0.8 %collective-permute-done.13.first = f32[32,256]{1,0:T(8,128)S(1)} collective-permute-done((f32[32,256]{1,0:T(8,128)S(1)}, f32[32,256]{1,0:T(8,128)S(1)}, u32[]{:S(2)}, u32[]{:S(2)}) %collective-permute-start.13) | collective-permute-done | bytes 32800 | tf_op jit(solution)/shard_map/ppermute | solution.py:178
  40.8 1.2 %collective-permute-done.14.second = f32[32,256]{1,0:T(8,128)S(1)} collective-permute-done((f32[32,256]{1,0:T(8,128)S(1)}, f32[32,256]{1,0:T(8,128)S(1)}, u32[]{:S(2)}, u32[]{:S(2)}) %collective-permute-start.14) | collective-permute-done | bytes 32800 | tf_op jit(solution)/shard_map/ppermute | solution.py:182
  42.0 0.7 %final.1 = f32[8,32,256]{2,1,0:T(8,128)} custom-call(f32[8,32,256]{2,1,0:T(8,128)} %get-tuple-element.62.part_ref, f32[2,32,256]{2,1,0:T(8,128)S(1)} %get-tuple-element.63.edge_ref, f32[2,32,256]{2,1,0:T(8,128)S(1)} %get-tuple-element.64.factor_ref, f32[32,256]{1,0:T(8,128)S(1)} %collective-permute-done.13.first, ...), custom_call_target="tpu_custom_call", output_to_operand_aliasing={{}: (0, {})} | custom-call | bytes 720896 | tf_op jit(solution)/shard_map/final/pallas_call | solution.py:20
  (5 shorter events, 0.1 us)
Async XLA Ops:
  0.0 2.5 %copy-start = (f32[8,32,256]{2,1,0:T(8,128)S(1)}, f32[8,32,256]{2,1,0:T(8,128)}, u32[]{:S(2)}) copy-start(f32[8,32,256]{2,1,0:T(8,128)} %k_ref.7) | copy-start | bytes 786436
  0.0 1.0 %copy-start.2 = (f32[8,32,256]{2,1,0:T(8,128)S(1)}, f32[8,32,256]{2,1,0:T(8,128)}, u32[]{:S(2)}) copy-start(f32[8,32,256]{2,1,0:T(8,128)} %f_ref.3) | copy-start | bytes 786436
  1.1 1.3 %collective-permute-start = (f32[48,256]{1,0:T(8,128)S(1)}, f32[48,256]{1,0:T(8,128)S(1)}, u32[]{:S(2)}, u32[]{:S(2)}) collective-permute-start(f32[48,256]{1,0:T(8,128)S(1)} %get-tuple-element.37), channel_id=1, source_target_pairs={{0,4},{4,0},{8,12},{12,8},{16,20},{20,16},{24,28},{28,24},{32,36},... | collective-permute-start | bytes 147464 | tf_op jit(solution)/shard_map/ppermute | solution.py:202
  2.5 8.7 %collective-permute-start.1 = (f32[64,256]{1,0:T(8,128)S(1)}, f32[64,256]{1,0:T(8,128)S(1)}, u32[]{:S(2)}, u32[]{:S(2)}) collective-permute-start(f32[64,256]{1,0:T(8,128)S(1)} %get-tuple-element.39), channel_id=1, source_target_pairs={{0,64},{4,196},{8,72},{12,204},{16,80},{20,212},{24,88},{28,220},{... | collective-permute-start | bytes 196616 | tf_op jit(solution)/shard_map/ppermute | solution.py:196
  4.0 7.1 %collective-permute-start.2 = (f32[16,256]{1,0:T(8,128)S(1)}, f32[16,256]{1,0:T(8,128)S(1)}, u32[]{:S(2)}, u32[]{:S(2)}) collective-permute-start(f32[16,256]{1,0:T(8,128)S(1)} %get-tuple-element.40), channel_id=1, source_target_pairs={{0,1},{1,2},{2,3},{3,0},{4,7},{5,4},{6,5},{7,6},{8,9},{9,10},{10,1... | collective-permute-start | bytes 49160 | tf_op jit(solution)/shard_map/ppermute | solution.py:189
  5.6 7.0 %collective-permute-start.4 = (f32[2,8,256]{2,1,0:T(8,128)S(1)}, f32[2,8,256]{2,1,0:T(8,128)S(1)}, u32[]{:S(2)}, u32[]{:S(2)}) collective-permute-start(f32[2,8,256]{2,1,0:T(8,128)S(1)} %get-tuple-element.41), channel_id=1, source_target_pairs={{0,60},{4,8},{8,4},{12,16},{16,12},{20,24},{24,20},{28,32},{32,28}... | collective-permute-start | bytes 49160 | tf_op jit(solution)/shard_map/ppermute | solution.py:199
  11.2 1.4 %copy-start.1 = (bf16[3,8,32,256]{3,2,1,0:T(8,128)(2,1)S(1)}, bf16[3,8,32,256]{3,2,1,0:T(8,128)(2,1)}, u32[]{:S(2)}) copy-start(bf16[3,8,32,256]{3,2,1,0:T(8,128)(2,1)} %wind_ref.3) | copy-start | bytes 1179652
  11.2 1.4 %copy-start.3 = (f32[8,32,256]{2,1,0:T(8,128)S(1)}, f32[8,32,256]{2,1,0:T(8,128)}, u32[]{:S(2)}) copy-start(f32[8,32,256]{2,1,0:T(8,128)} %f_ref.3) | copy-start | bytes 786436
  11.2 1.4 %collective-permute-start.3 = (f32[40,256]{1,0:T(8,128)S(1)}, f32[40,256]{1,0:T(8,128)S(1)}, u32[]{:S(2)}, u32[]{:S(2)}) collective-permute-start(f32[40,256]{1,0:T(8,128)S(1)} %relay.1), channel_id=1, source_target_pairs={{0,4},{4,0},{8,12},{12,8},{16,20},{20,16},{24,28},{28,24},{32,36},... | collective-permute-start | bytes 122888 | tf_op jit(solution)/shard_map/ppermute | solution.py:202
  13.1 1.3 %collective-permute-start.5 = (f32[6,8,256]{2,1,0:T(8,128)S(1)}, f32[6,8,256]{2,1,0:T(8,128)S(1)}, u32[]{:S(2)}, u32[]{:S(2)}) collective-permute-start(f32[6,8,256]{2,1,0:T(8,128)S(1)} %get-tuple-element.47.own_ref.ends_ref), channel_id=1, source_target_pairs={{0,4},{4,0},{8,12},{12,8},{16,20},{20,16},{24,28},{28,24},{32,36},... | collective-permute-start | bytes 147464 | tf_op jit(solution)/shard_map/ppermute | solution.py:202
  14.5 6.0 %collective-permute-start.6 = (f32[5,8,256]{2,1,0:T(8,128)S(1)}, f32[5,8,256]{2,1,0:T(8,128)S(1)}, u32[]{:S(2)}, u32[]{:S(2)}) collective-permute-start(f32[5,8,256]{2,1,0:T(8,128)S(1)} %chip.1.own_ref), channel_id=1, source_target_pairs={{0,8},{4,60},{8,16},{12,4},{16,24},{20,12},{24,32},{28,20},{32,40}... | collective-permute-start | bytes 122888 | tf_op jit(solution)/shard_map/ppermute | solution.py:454
  14.6 8.4 %collective-permute-start.8 = (f32[5,8,256]{2,1,0:T(8,128)S(1)}, f32[5,8,256]{2,1,0:T(8,128)S(1)}, u32[]{:S(2)}, u32[]{:S(2)}) collective-permute-start(f32[5,8,256]{2,1,0:T(8,128)S(1)} %chip.1.own_ref), channel_id=1, source_target_pairs={{0,32},{4,36},{8,40},{12,44},{16,48},{20,52},{24,56},{28,60},{32,0... | collective-permute-start | bytes 122888 | tf_op jit(solution)/shard_map/ppermute | solution.py:454
  20.5 6.2 %collective-permute-start.7 = (f32[5,8,256]{2,1,0:T(8,128)S(1)}, f32[5,8,256]{2,1,0:T(8,128)S(1)}, u32[]{:S(2)}, u32[]{:S(2)}) collective-permute-start(f32[5,8,256]{2,1,0:T(8,128)S(1)} %pair.1), channel_id=1, source_target_pairs={{0,16},{4,52},{8,24},{12,60},{16,32},{20,4},{24,40},{28,12},{32,48... | collective-permute-start | bytes 122888 | tf_op jit(solution)/shard_map/ppermute | solution.py:454
  26.7 1.3 %collective-permute-start.9 = (f32[5,8,256]{2,1,0:T(8,128)S(1)}, f32[5,8,256]{2,1,0:T(8,128)S(1)}, u32[]{:S(2)}, u32[]{:S(2)}) collective-permute-start(f32[5,8,256]{2,1,0:T(8,128)S(1)} %side.1.side_ref), channel_id=1, source_target_pairs={{0,4},{4,0},{8,12},{12,8},{16,20},{20,16},{24,28},{28,24},{32,36},... | collective-permute-start | bytes 122888 | tf_op jit(solution)/shard_map/ppermute | solution.py:202
  28.4 5.3 %collective-permute-start.12 = (f32[8,384]{1,0:T(8,128)S(1)}, f32[8,384]{1,0:T(8,128)S(1)}, u32[]{:S(2)}, u32[]{:S(2)}) collective-permute-start(f32[8,384]{1,0:T(8,128)S(1)} %get-tuple-element.52.own_ref), channel_id=1, source_target_pairs={{0,2},{1,3},{2,0},{3,1},{4,6},{5,7},{6,4},{7,5},{8,10},{9,11},{10,... | collective-permute-start | bytes 36872 | tf_op jit(solution)/shard_map/ppermute | solution.py:490
  30.5 3.7 %collective-permute-start.11 = (f32[8,384]{1,0:T(8,128)S(1)}, f32[8,384]{1,0:T(8,128)S(1)}, u32[]{:S(2)}, u32[]{:S(2)}) collective-permute-start(f32[8,384]{1,0:T(8,128)S(1)} %get-tuple-element.52.own_ref), channel_id=1, source_target_pairs={{0,3},{1,0},{2,1},{3,2},{4,7},{5,4},{6,5},{7,6},{8,11},{9,8},{10,9... | collective-permute-start | bytes 36872 | tf_op jit(solution)/shard_map/ppermute | solution.py:490
  31.6 4.9 %collective-permute-start.10 = (f32[8,384]{1,0:T(8,128)S(1)}, f32[8,384]{1,0:T(8,128)S(1)}, u32[]{:S(2)}, u32[]{:S(2)}) collective-permute-start(f32[8,384]{1,0:T(8,128)S(1)} %get-tuple-element.52.own_ref), channel_id=1, source_target_pairs={{0,1},{1,2},{2,3},{3,0},{4,5},{5,6},{6,7},{7,4},{8,9},{9,10},{10,1... | collective-permute-start | bytes 36872 | tf_op jit(solution)/shard_map/ppermute | solution.py:490
  36.8 4.0 %collective-permute-start.13 = (f32[32,256]{1,0:T(8,128)S(1)}, f32[32,256]{1,0:T(8,128)S(1)}, u32[]{:S(2)}, u32[]{:S(2)}) collective-permute-start(f32[32,256]{1,0:T(8,128)S(1)} %get-tuple-element.65), channel_id=1, source_target_pairs={{0,64},{64,128},{128,192},{192,0},{1,65},{65,129},{129,193},{193,1... | collective-permute-start | bytes 98312 | tf_op jit(solution)/shard_map/ppermute | solution.py:178
  38.1 3.9 %collective-permute-start.14 = (f32[32,256]{1,0:T(8,128)S(1)}, f32[32,256]{1,0:T(8,128)S(1)}, u32[]{:S(2)}, u32[]{:S(2)}) collective-permute-start(f32[32,256]{1,0:T(8,128)S(1)} %get-tuple-element.66), channel_id=1, source_target_pairs={{64,0},{128,64},{192,128},{0,192},{65,1},{129,65},{193,129},{1,193... | collective-permute-start | bytes 98312 | tf_op jit(solution)/shard_map/ppermute | solution.py:182

commit v3 on v2

--- a/solution.py
+++ b/solution.py
@@ -146,54 +146,57 @@
     def faces_kernel(f_ref, own, give, xc):
         odd = core() == 1
         low, high = f_ref[0], f_ref[nz - 1]
-        own[0:nx] = jnp.where(odd, low, high)
-        give[0:nx] = jnp.where(odd, high, low)
+        own[0:nx] = jnp.where(odd, high, low)
+        give[0:nx] = jnp.where(odd, low, high)
         flat = f_ref[...].reshape(lines, ny)
         low = flat[:, :128].T[:1]
         high = flat[:, ny - 128 :].T[127:]
         pad = jnp.zeros((7, lines), jnp.float32)
-        own[nx : nx + 8] = jnp.concatenate([jnp.where(odd, low, high), pad], axis=0)
-        give[nx : nx + 8] = jnp.concatenate([jnp.where(odd, high, low), pad], axis=0)
-        xc[...], give[nx + 8 :] = x_faces(f_ref)
+        own[nx : nx + 8] = jnp.concatenate([jnp.where(odd, high, low), pad], axis=0)
+        give[nx : nx + 8] = jnp.concatenate([jnp.where(odd, low, high), pad], axis=0)
+        xc[0:nz], give[nx + 8 :] = x_faces(f_ref)
 
     def x_faces(ref):
         odd = core() == 1
         first, last = ref[:, 0, :], ref[:, nx - 1, :]
         return jnp.where(odd, last, first), jnp.where(odd, first, last)
 
-    def both_faces_kernel(own, got, k_ref, f_ref, planes, columns_out, cross_out, inner):
-        planes[0:nx] = own[0:nx]
-        planes[nx:] = got[0:nx]
-        columns_out[0:8] = own[nx:]
-        columns_out[8:16] = got[nx : nx + 8]
-        cross_out[0] = f_ref[...]
-        cross_out[1], inner[...] = x_faces(k_ref)
+    def both_faces_kernel(own, got, planes, columns_out):
+        planes[0:nx] = got[0:nx]
+        planes[nx:] = own[0:nx]
+        columns_out[0:8] = got[nx : nx + 8]
+        columns_out[8:16] = own[nx:]
 
     def relay_kernel(planes, columns_in, out_ref):
         out_ref[0:nx] = planes[nx:]
         out_ref[nx:] = columns_in[8:16]
-
-    def up(a, axis):
-        n = lax.axis_size(axis)
-        return lax.ppermute(a, axis, [(i, (i + 1) % n) for i in range(n)])
-
-    def down(a, axis):
-        n = lax.axis_size(axis)
-        return lax.ppermute(a, axis, [((i + 1) % n, i) for i in range(n)])
 
     def y_outward(a):
         pairs = []
         for x in range(members):
             for y in range(columns):
-                pairs.append((x * columns + y, x * columns + (y + (-1 if x % 2 else 1)) % columns))
+                pairs.append((x * columns + y, (x ^ 1) * columns + (y + (1 if x % 2 else -1)) % columns))
         return lax.ppermute(a, ("gx", "gy"), pairs)
 
     def z_outward(a):
         pairs = []
         for z in range(levels):
             for x in range(members):
-                pairs.append((z * members + x, (z + (-1 if x % 2 else 1)) % levels * members + x))
+                to = z + (1 if x % 2 else -1)
+                pairs.append((z * members + x, to * members + (x ^ 1) if 0 <= to < levels else z * members + (x ^ 2)))
         return lax.ppermute(a, ("gz", "gx"), pairs)
+
+    def z_swap(a, parity):
+        pairs = []
+        for z in range(levels):
+            for x in range(members):
+                to = z + (1 if z % 2 == parity else -1)
+                pairs.append((z * members + x, to * members + x if 0 <= to < levels else z * members + (x ^ 1)))
+        return lax.ppermute(a, ("gz", "gx"), pairs)
+
+    def z_order(low, high):
+        even = lax.rem(lax.axis_index("gz"), 2) == 0
+        return jnp.where(even, high, low), jnp.where(even, low, high)
 
     def across(a):
         return lax.ppermute(a, "gx", [(i, (i + 1 if i % 2 else i - 1) % members) for i in range(members)])
@@ -218,8 +221,8 @@
         d_ref[...] = 1.0 / (c * jnp.swapaxes(k_ref[...], 0, 1))
         factor(d_ref, w_ref, l_ref, r_ref, nx)
 
-    def y_matrix_kernel(x_ref, xc, other_ref, d_ref, w_ref, l_ref, r_ref, c_ref):
-        west, east = x_sides(xc[1], other_ref[5])
+    def y_matrix_kernel(x_ref, near_ref, other_ref, d_ref, w_ref, l_ref, r_ref, c_ref):
+        west, east = x_sides(near_ref[5], other_ref[6])
         d = jnp.concatenate(
             [
                 x_ref[...].reshape(lines, ny),
@@ -246,10 +249,10 @@
             c_ref[3, n] = jnp.zeros_like(L)
 
     def explicit_kernel(
-        f_ref, wind_ref, k_ref, planes, columns_in, relayed, xc, got, kin, d_ref, w_ref, l_ref, r_ref,
+        f_ref, wind_ref, k_ref, planes, columns_in, relayed, xc, got, d_ref, w_ref, l_ref, r_ref,
         base_ref, ends_ref, e_ref,
     ):
-        west, east = x_rows(xc[0], got[nx + 8 :])
+        west, east = x_rows(xc[0:nz], got[nx + 8 :])
         odd = core() == 1
         low, high = z_planes(*choose(odd, (relayed[0:nx], planes[0:nx]), (planes[0:nx], relayed[0:nx])))
         gy = lax.axis_index("gy")
@@ -274,7 +277,7 @@
             )
         e = jnp.swapaxes(e_ref[...], 0, 1)
         sweep(lambda i: e[i] * d_ref[i], w_ref, base_ref, nx)
-        ends = (base_ref[0], base_ref[nx - 1], l_ref[0], r_ref[0], r_ref[nx - 1], kin[...])
+        ends = (base_ref[0], base_ref[nx - 1], l_ref[0], r_ref[0], r_ref[nx - 1]) + x_faces(k_ref)
         for n, v in enumerate(ends):
             ends_ref[n] = v
 
@@ -288,14 +291,15 @@
         own, got = read(own_ref), read(got_ref)
         return choose(own_first, own, got), choose(own_first, got, own)
 
-    def chip_kernel(own_ref, got_ref, out_ref):
+    def chip_kernel(own_ref, got_ref, out_ref, near_ref):
         b0, b1, L, C, R = merge(*ordered(own_ref, got_ref, core() == 0))
         chip = lax.axis_index("gx") // 2
         first, last = chip == 0, chip == chips - 1
         L, R = jnp.where(first, 0.0, L), jnp.where(last, 0.0, R)
         C = jnp.where(jnp.logical_or(first, last), 0.0, C)
         for n, v in enumerate((b0, b1, L, C, R)):
-            out_ref[n] = v
+            out_ref[n] = near_ref[n] = v
+        near_ref[5] = own_ref[5]
 
     def pair_kernel(own_ref, got_ref, out_ref):
         for n, v in enumerate(merge(*ordered(own_ref, got_ref, core() == 1))):
@@ -356,7 +360,7 @@
     def y_finish_kernel(
         own_ref, *refs,
     ):
-        got, (ybase_ref, up_ref, l_ref, r_ref, c_ref), (s_ref, t_ref, ends_ref, west, east, zlo, zhi) = (
+        got, (ybase_ref, up_ref, l_ref, r_ref, c_ref), (s_ref, t_ref, ends_ref, west, east, first_plane, second_plane) = (
             refs[: columns - 1], refs[columns - 1 : columns + 4], refs[columns + 4 :],
         )
         index = lax.axis_index("gy")
@@ -365,7 +369,7 @@
         for m in range(columns):
             v = messages[0]
             for back in range(1, columns):
-                v = jnp.where(lax.rem(index - m + columns, columns) == back, messages[back], v)
+                v = jnp.where(lax.bitwise_xor(index, back) == m, messages[back], v)
             blocks.append(tuple(v[n : n + 1] for n in range(5)))
         mine = tuple(messages[0][n : n + 1] for n in range(5))
         lp, lg, rp, rg = chain_ends(blocks, index)
@@ -398,8 +402,7 @@
             else:
                 west[...] = t[:nz]
                 east[...] = t[nz : 2 * nz]
-        zlo[...] = s_ref[0]
-        zhi[...] = s_ref[nz - 1]
+        first_plane[...], second_plane[...] = z_order(s_ref[0], s_ref[nz - 1])
 
     def by_rows(ref, first):
         return jnp.swapaxes(ref[:, :, first : first + 128], 0, 1).reshape(ny, 128)
@@ -437,7 +440,7 @@
             copy.wait()
 
     def final_kernel(part_ref, edge_ref, factor_ref, first, second, out_ref, buffer, sems):
-        low, high = z_planes(first[...], second[...])
+        low, high = z_planes(*z_order(first[...], second[...]))
         buffer[0] = edge_ref[0] + factor_ref[0] * low
         buffer[1] = edge_ref[1] + factor_ref[1] * high
         copies = [pltpu.make_async_copy(buffer.at[n], out_ref.at[z], sems.at[n]) for n, z in enumerate((0, nz - 1))]
@@ -457,26 +460,24 @@
         faces_kernel, [(nx + 8, ny), (nx + 8 + nz, ny), (nz, ny)], field, name="faces", flops=10**10
     )
     got = sibling(give)
-    planes, edges, xc, kin = call(
-        both_faces_kernel, [(2 * nx, ny), (16, lines), (2, nz, ny), (nz, ny)], own, got, rate, xc, name="both_faces"
-    )
+    planes, edges = call(both_faces_kernel, [(2 * nx, ny), (16, lines)], own, got, name="both_faces")
     planes, edges = z_outward(planes), y_outward(edges)
     (relay,) = call(relay_kernel, [(nx + 8, ny)], planes, edges, name="relay")
     relayed = sibling(relay)
     xc = across(xc)
     dx, wx, lx, rx = call(x_matrix_kernel, [xbox] * 4, rate, name="x_matrix", flops=5 * 10**9)
     base, ends = call(
-        explicit_kernel, [xbox, (6, nz, ny)],
-        field, wind, rate, planes, edges, relayed, xc, got, kin, dx, wx, lx, rx, name="explicit",
+        explicit_kernel, [xbox, (7, nz, ny)],
+        field, wind, rate, planes, edges, relayed, xc, got, dx, wx, lx, rx, name="explicit",
         scratch=[pltpu.VMEM(box, jnp.float32)],
     )
     other = sibling(ends)
+    chip, chip_near = call(chip_kernel, [five, (6, nz, ny)], ends, other, name="chip")
+    opposite = outward(chip, chips // 2)
+    near = across(chip_near)
     dy, wy, ly, ry, cy = call(
-        y_matrix_kernel, [ybox] * 4 + [(4, 7, subs, wide)], dx, xc, other, name="y_matrix", flops=10**6
-    )
-    (chip,) = call(chip_kernel, [five], ends, other, name="chip")
-    opposite = outward(chip, chips // 2)
-    near = outward(chip, 1)
+        y_matrix_kernel, [ybox] * 4 + [(4, 7, subs, wide)], dx, near, other, name="y_matrix", flops=10**6
+    )
     (pair,) = call(pair_kernel, [five], chip, near, name="pair")
     distant = outward(pair, 2)
     (side,) = call(side_kernel, [five], near, distant, opposite, name="side")
@@ -487,14 +488,14 @@
         scratch=[pltpu.VMEM((wide // nz, nz, ny), jnp.float32)],
     )
     ring = [
-        lax.ppermute(send, "gy", [(i, (i + back) % columns) for i in range(columns)])
+        lax.ppermute(send, "gy", [(i, i ^ back) for i in range(columns)])
         for back in order
     ]
-    swept, turned, sides, west, east, zlo, zhi = call(
+    swept, turned, sides, west, east, first, second = call(
         y_finish_kernel, [box, ybox, (2, wide), (nz, ny), (nz, ny), (nx, ny), (nx, ny)],
         send, *ring, ybase, ups, ly, ry, cy, name="y_finish",
     )
-    below, above = up(zhi, "gz"), down(zlo, "gz")
+    first, second = z_swap(first, 0), z_swap(second, 1)
     plane_pair = (2, nx, ny)
     part, edge, factors = call(
         inner_kernel, [box, plane_pair, plane_pair],
@@ -506,7 +507,7 @@
         ],
     )
     (out,) = call(
-        final_kernel, [box], part, edge, factors, below, above, name="final", far_in=(0,), far_out=(0,), alias={0: 0},
+        final_kernel, [box], part, edge, factors, first, second, name="final", far_in=(0,), far_out=(0,), alias={0: 0},
         scratch=[pltpu.VMEM(plane_pair, jnp.float32), pltpu.SemaphoreType.DMA((2,))],
     )
     return out

time: 43.5 us -> 41 us (0.943); the launches traced: 42.7 us -> 40.9 us
  waiting for transfers between devices: 14.5 us -> 13.1 us
    ppermute x3 -> x2, starting transfers between devices: 7.54 us -> 3.91 us  [outward(): return lax.ppermute(a, 'gx', [(i, move(i)) for i in range(members)])]
    ppermute x5, waiting for transfers between devices: 5.91 us -> 3.84 us  [the longest x3 2.5 us: body(): lax.ppermute(send, 'gy', [(i, i ^ back) for i in range(columns)])]
    ppermute x1 -> x2, starting transfers between devices: 5.54 us -> 7.42 us  [across(): lax.ppermute(a, 'gx', [(i, (i + 1 if i % 2 else i - 1) % members) for i i...]
    ppermute x3 -> x2, waiting for transfers between devices: 4.64 us -> 5.47 us  [outward(): return lax.ppermute(a, 'gx', [(i, move(i)) for i in range(members)])]
    ppermute x1, starting transfers between devices: 1.58 us -> 2.19 us  [y_outward(): return lax.ppermute(a, ('gx', 'gy'), pairs)]
    ppermute x1, starting transfers between devices: 1.57 us -> 2.04 us  [z_outward(): return lax.ppermute(a, ('gz', 'gx'), pairs)]
    ppermute x1 -> x2, waiting for transfers between devices: 0.88 us -> 0.8 us  [across(): lax.ppermute(a, 'gx', [(i, (i + 1 if i % 2 else i - 1) % members) for i i...]
  transfers between devices with their start and end apart: 15 -> 15, of which waited for: 11 -> 10; matrix products, arithmetic and copies ran while one was open for 0% -> 0% of each run, Pallas kernels for 5% -> 5%
where the time goes in v3:
time: 41 us; the launch traced here: 40.9 us
  starting transfers between devices  22.5 us (55%)
  waiting for transfers between devices  13.1 us (32%)
  Pallas kernels  4.24 us (10%)
  local copies, waits for them, and re-layouts  0.97 us (2%)
    ppermute x2, starting transfers between devices, across(): lax.ppermute(a, 'gx', [(i, (i + 1 if i % 2 else i - 1) % members) for i i...  7.42 us
    ppermute x2, waiting for transfers between devices, outward(): return lax.ppermute(a, 'gx', [(i, move(i)) for i in range(members)])  5.47 us
    pallas_call x13, Pallas kernels, call(): pl.pallas_call(kernel, out_shape=shapes, in_specs=[far if n in far_in els...  4.24 us
    ppermute x2, starting transfers between devices, outward(): return lax.ppermute(a, 'gx', [(i, move(i)) for i in range(members)])  3.91 us
    ppermute x3, starting transfers between devices, body(): lax.ppermute(send, 'gy', [(i, i ^ back) for i in range(columns)])  3.57 us
    ppermute x4, waiting for transfers between devices, sibling(): return lax.ppermute(a, 'gx', [(i, i ^ 1) for i in range(members)])  2.98 us
    ppermute x2, starting transfers between devices, z_swap(): return lax.ppermute(a, ('gz', 'gx'), pairs)  2.9 us
    ppermute x3, waiting for transfers between devices, body(): lax.ppermute(send, 'gy', [(i, i ^ back) for i in range(columns)])  2.5 us
  transfers between devices with their start and end apart: 15, of which 10 were waited for; matrix products, arithmetic and copies ran while one was open for 0% of the time, Pallas kernels for 5%

profile of v3, /device:TPU:2, one launch (start us, length us, event | category | flops | bytes accessed | tf_op | source)
XLA Modules:
  0.0 40.9 jit_solution(8401279839022514185)
XLA Ops:
  0.0 0.0 copy-start.1
  0.0 0.9 %copy-done.1 = f32[8,32,256]{2,1,0:T(8,128)S(1)} copy-done((f32[8,32,256]{2,1,0:T(8,128)S(1)}, f32[8,32,256]{2,1,0:T(8,128)}, u32[]{:S(2)}) %copy-start.1) | copy-done | bytes 262168
  1.0 0.0 copy-start.3
  1.0 0.1 faces.1
  1.1 0.1 collective-permute-start
  1.2 1.2 %collective-permute-done.got = f32[48,256]{1,0:T(8,128)S(1)} collective-permute-done((f32[48,256]{1,0:T(8,128)S(1)}, f32[48,256]{1,0:T(8,128)S(1)}, u32[]{:S(2)}, u32[]{:S(2)}) %collective-permute-start) | collective-permute-done | bytes 49184 | tf_op jit(solution)/shard_map/ppermute | solution.py:205
  2.4 2.0 %collective-permute-start.1 = (f32[64,256]{1,0:T(8,128)S(1)}, f32[64,256]{1,0:T(8,128)S(1)}, u32[]{:S(2)}, u32[]{:S(2)}) collective-permute-start(f32[64,256]{1,0:T(8,128)S(1)} %get-tuple-element.38), channel_id=1, source_target_pairs={{0,8},{4,64},{8,0},{12,72},{16,24},{20,80},{24,16},{28,88},{32,40}... | collective-permute-start | bytes 196616 | tf_op jit(solution)/shard_map/ppermute | solution.py:187
  4.4 2.2 %collective-permute-start.2 = (f32[16,256]{1,0:T(8,128)S(1)}, f32[16,256]{1,0:T(8,128)S(1)}, u32[]{:S(2)}, u32[]{:S(2)}) collective-permute-start(f32[16,256]{1,0:T(8,128)S(1)} %get-tuple-element.39), channel_id=1, source_target_pairs={{0,7},{1,4},{2,5},{3,6},{4,1},{5,2},{6,3},{7,0},{8,15},{9,12},{10,... | collective-permute-start | bytes 49160 | tf_op jit(solution)/shard_map/ppermute | solution.py:179
  6.6 3.2 %collective-permute-start.4 = (f32[8,256]{1,0:T(8,128)S(1)}, f32[8,256]{1,0:T(8,128)S(1)}, u32[]{:S(2)}, u32[]{:S(2)}) collective-permute-start(f32[8,256]{1,0:T(8,128)S(1)} %get-tuple-element.40), channel_id=1, source_target_pairs={{0,60},{4,8},{8,4},{12,16},{16,12},{20,24},{24,20},{28,32},{32,28}... | collective-permute-start | bytes 24584 | tf_op jit(solution)/shard_map/ppermute | solution.py:202
  9.9 0.0 collective-permute-done.2.columns_in
  9.9 0.0 collective-permute-done.1.planes
  9.9 0.0 copy-start
  9.9 0.0 copy-start.2
  9.9 0.1 collective-permute-start.3
  10.0 0.0 copy-done.3
  10.0 0.4 %x_matrix.1 = (f32[32,8,256]{2,1,0:T(8,128)S(1)}, f32[32,8,256]{2,1,0:T(8,128)S(1)}, f32[32,8,256]{2,1,0:T(8,128)S(1)}, f32[32,8,256]{2,1,0:T(8,128)S(1)}) custom-call(f32[8,32,256]{2,1,0:T(8,128)S(1)} %copy-done.3), custom_call_target="tpu_custom_call" | custom-call | flops 5000000000 | bytes 1310720 | tf_op jit(solution)/shard_map/x_matrix/pallas_call | solution.py:20
  10.4 0.8 %collective-permute-done.4.xc = f32[8,256]{1,0:T(8,128)S(1)} collective-permute-done((f32[8,256]{1,0:T(8,128)S(1)}, f32[8,256]{1,0:T(8,128)S(1)}, u32[]{:S(2)}, u32[]{:S(2)}) %collective-permute-start.4) | collective-permute-done | bytes 8224 | tf_op jit(solution)/shard_map/ppermute | solution.py:202
  11.2 0.0 collective-permute-done.3.relayed
  11.2 0.0 copy-done
  11.2 0.0 copy-done.2
  11.2 0.6 %explicit.1 = (f32[32,8,256]{2,1,0:T(8,128)S(1)}, f32[7,8,256]{2,1,0:T(8,128)S(1)}) custom-call(f32[8,32,256]{2,1,0:T(8,128)S(1)} %copy-done.2, bf16[3,8,32,256]{3,2,1,0:T(8,128)(2,1)S(1)} %copy-done, f32[8,32,256]{2,1,0:T(8,128)S(1)} %copy-done.3, f32[64,256]{1,0:T(8,128)S(1)} %collective-permute-done.1.planes, ...), custom_call_target="tpu_custom_call" | custom-call | bytes 2859008 | tf_op jit(solution)/shard_map/explicit/pallas_call | solution.py:20
  11.8 0.2 collective-permute-start.5
  12.0 1.1 %collective-permute-done.5.got_ref.other_ref = f32[7,8,256]{2,1,0:T(8,128)S(1)} collective-permute-done((f32[7,8,256]{2,1,0:T(8,128)S(1)}, f32[7,8,256]{2,1,0:T(8,128)S(1)}, u32[]{:S(2)}, u32[]{:S(2)}) %collective-permute-start.5) | collective-permute-done | bytes 57376 | tf_op jit(solution)/shard_map/ppermute | solution.py:205
  13.1 4.2 %collective-permute-start.6 = (f32[6,8,256]{2,1,0:T(8,128)S(1)}, f32[6,8,256]{2,1,0:T(8,128)S(1)}, u32[]{:S(2)}, u32[]{:S(2)}) collective-permute-start(f32[6,8,256]{2,1,0:T(8,128)S(1)} %get-tuple-element.46), channel_id=1, source_target_pairs={{0,60},{4,8},{8,4},{12,16},{16,12},{20,24},{24,20},{28,32},{32,28}... | collective-permute-start | bytes 147464 | tf_op jit(solution)/shard_map/ppermute | solution.py:202
  17.3 2.9 %collective-permute-start.8 = (f32[5,8,256]{2,1,0:T(8,128)S(1)}, f32[5,8,256]{2,1,0:T(8,128)S(1)}, u32[]{:S(2)}, u32[]{:S(2)}) collective-permute-start(f32[5,8,256]{2,1,0:T(8,128)S(1)} %get-tuple-element.47.own_ref), channel_id=1, source_target_pairs={{0,32},{4,36},{8,40},{12,44},{16,48},{20,52},{24,56},{28,60},{32,0... | collective-permute-start | bytes 122888 | tf_op jit(solution)/shard_map/ppermute | solution.py:457
  20.2 0.0 collective-permute-done.6.got_ref.near_ref
  20.2 1.0 %collective-permute-start.7 = (f32[5,8,256]{2,1,0:T(8,128)S(1)}, f32[5,8,256]{2,1,0:T(8,128)S(1)}, u32[]{:S(2)}, u32[]{:S(2)}) collective-permute-start(f32[5,8,256]{2,1,0:T(8,128)S(1)} %pair.1), channel_id=1, source_target_pairs={{0,16},{4,52},{8,24},{12,60},{16,32},{20,4},{24,40},{28,12},{32,48... | collective-permute-start | bytes 122888 | tf_op jit(solution)/shard_map/ppermute | solution.py:457
  21.3 4.5 %collective-permute-done.8.opposite_ref = f32[5,8,256]{2,1,0:T(8,128)S(1)} collective-permute-done((f32[5,8,256]{2,1,0:T(8,128)S(1)}, f32[5,8,256]{2,1,0:T(8,128)S(1)}, u32[]{:S(2)}, u32[]{:S(2)}) %collective-permute-start.8) | collective-permute-done | bytes 40992 | tf_op jit(solution)/shard_map/ppermute | solution.py:457
  25.7 1.0 %collective-permute-done.7.far_ref = f32[5,8,256]{2,1,0:T(8,128)S(1)} collective-permute-done((f32[5,8,256]{2,1,0:T(8,128)S(1)}, f32[5,8,256]{2,1,0:T(8,128)S(1)}, u32[]{:S(2)}, u32[]{:S(2)}) %collective-permute-start.7) | collective-permute-done | bytes 40992 | tf_op jit(solution)/shard_map/ppermute | solution.py:457
  26.8 0.1 collective-permute-start.9
  26.9 0.6 %y_matrix.1 = (f32[32,8,384]{2,1,0:T(8,128)S(1)}, f32[32,8,384]{2,1,0:T(8,128)S(1)}, f32[32,8,384]{2,1,0:T(8,128)S(1)}, f32[32,8,384]{2,1,0:T(8,128)S(1)}, f32[4,7,8,384]{3,2,1,0:T(8,128)S(1)}) custom-call(f32[32,8,256]{2,1,0:T(8,128)S(1)} %get-tuple-element.41.d_ref.x_ref, f32[6,8,256]{2,1,0:T(8,128)S(1)} %collective-permute-done.6.got_ref.near_ref, ...), custom_call_target="tpu_custom_call" | custom-call | flops 1000000 | bytes 2285568 | tf_op jit(solution)/shard_map/y_matrix/pallas_call | solution.py:20
  27.4 0.6 %collective-permute-done.9.got_ref = f32[5,8,256]{2,1,0:T(8,128)S(1)} collective-permute-done((f32[5,8,256]{2,1,0:T(8,128)S(1)}, f32[5,8,256]{2,1,0:T(8,128)S(1)}, u32[]{:S(2)}, u32[]{:S(2)}) %collective-permute-start.9) | collective-permute-done | bytes 40992 | tf_op jit(solution)/shard_map/ppermute | solution.py:205
  28.1 0.4 %x_finish.1 = (f32[32,8,384]{2,1,0:T(8,128)S(1)}, f32[3,2,8,384]{3,2,1,0:T(8,128)S(1)}, f32[8,384]{1,0:T(8,128)S(1)}) custom-call(f32[7,8,256]{2,1,0:T(8,128)S(1)} %get-tuple-element.45.own_ref.ends_ref, f32[7,8,256]{2,1,0:T(8,128)S(1)} %collective-permute-done.5.got_ref.other_ref, f32[5,8,256]{2,1,0:T(8,128)S(1)} %side.1.side_ref, ...), custom_call_target="tpu_custom_call" | custom-call | bytes 2592768 | tf_op jit(solution)/shard_map/x_finish/pallas_call | solution.py:20
  28.5 1.1 %collective-permute-start.12 = (f32[8,384]{1,0:T(8,128)S(1)}, f32[8,384]{1,0:T(8,128)S(1)}, u32[]{:S(2)}, u32[]{:S(2)}) collective-permute-start(f32[8,384]{1,0:T(8,128)S(1)} %get-tuple-element.52.own_ref), channel_id=1, source_target_pairs={{0,2},{1,3},{2,0},{3,1},{4,6},{5,7},{6,4},{7,5},{8,10},{9,11},{10,... | collective-permute-start | bytes 36872 | tf_op jit(solution)/shard_map/ppermute | solution.py:491
  29.5 1.3 %collective-permute-start.11 = (f32[8,384]{1,0:T(8,128)S(1)}, f32[8,384]{1,0:T(8,128)S(1)}, u32[]{:S(2)}, u32[]{:S(2)}) collective-permute-start(f32[8,384]{1,0:T(8,128)S(1)} %get-tuple-element.52.own_ref), channel_id=1, source_target_pairs={{0,3},{1,2},{2,1},{3,0},{4,7},{5,6},{6,5},{7,4},{8,11},{9,10},{10,... | collective-permute-start | bytes 36872 | tf_op jit(solution)/shard_map/ppermute | solution.py:491
  30.9 1.2 %collective-permute-start.10 = (f32[8,384]{1,0:T(8,128)S(1)}, f32[8,384]{1,0:T(8,128)S(1)}, u32[]{:S(2)}, u32[]{:S(2)}) collective-permute-start(f32[8,384]{1,0:T(8,128)S(1)} %get-tuple-element.52.own_ref), channel_id=1, source_target_pairs={{0,1},{1,0},{2,3},{3,2},{4,5},{5,4},{6,7},{7,6},{8,9},{9,8},{10,11... | collective-permute-start | bytes 36872 | tf_op jit(solution)/shard_map/ppermute | solution.py:491
  32.1 1.7 %collective-permute-done.12.refs_2_ = f32[8,384]{1,0:T(8,128)S(1)} collective-permute-done((f32[8,384]{1,0:T(8,128)S(1)}, f32[8,384]{1,0:T(8,128)S(1)}, u32[]{:S(2)}, u32[]{:S(2)}) %collective-permute-start.12) | collective-permute-done | bytes 12320 | tf_op jit(solution)/shard_map/ppermute | solution.py:491
  33.8 0.7 %collective-permute-done.11.refs_1_ = f32[8,384]{1,0:T(8,128)S(1)} collective-permute-done((f32[8,384]{1,0:T(8,128)S(1)}, f32[8,384]{1,0:T(8,128)S(1)}, u32[]{:S(2)}, u32[]{:S(2)}) %collective-permute-start.11) | collective-permute-done | bytes 12320 | tf_op jit(solution)/shard_map/ppermute | solution.py:491
  34.5 0.1 collective-permute-done.10.refs_0_
  34.6 0.3 y_finish.1
  34.9 1.4 %collective-permute-start.13 = (f32[32,256]{1,0:T(8,128)S(1)}, f32[32,256]{1,0:T(8,128)S(1)}, u32[]{:S(2)}, u32[]{:S(2)}) collective-permute-start(f32[32,256]{1,0:T(8,128)S(1)} %get-tuple-element.65), channel_id=1, source_target_pairs={{0,64},{4,68},{8,72},{12,76},{16,80},{20,84},{24,88},{28,92},{32,9... | collective-permute-start | bytes 98312 | tf_op jit(solution)/shard_map/ppermute | solution.py:195
  36.4 1.5 %collective-permute-start.14 = (f32[32,256]{1,0:T(8,128)S(1)}, f32[32,256]{1,0:T(8,128)S(1)}, u32[]{:S(2)}, u32[]{:S(2)}) collective-permute-start(f32[32,256]{1,0:T(8,128)S(1)} %get-tuple-element.66), channel_id=1, source_target_pairs={{0,4},{4,0},{8,12},{12,8},{16,20},{20,16},{24,28},{28,24},{32,36},... | collective-permute-start | bytes 98312 | tf_op jit(solution)/shard_map/ppermute | solution.py:195
  37.8 1.1 %inner.1 = (f32[8,32,256]{2,1,0:T(8,128)}, f32[2,32,256]{2,1,0:T(8,128)S(1)}, f32[2,32,256]{2,1,0:T(8,128)S(1)}) custom-call(f32[32,8,384]{2,1,0:T(8,128)S(1)} %get-tuple-element.57.t_ref, f32[2,384]{1,0:T(2,128)S(1)} %get-tuple-element.58.ends_ref, f32[8,32,256]{2,1,0:T(8,128)S(1)} %get-tuple-element.59.s_ref, bf16[3,8,32,256]{3,2,1,0:T(8,128)(2,1)S(1)} %copy-done, ...), custom_call_target="tpu_custom_call" | custom-call | flops 5000000000 | bytes 2116608 | tf_op jit(solution)/shard_map/inner/pallas_call | solution.py:20
  38.9 0.0 collective-permute-done.13.first
  38.9 1.3 %collective-permute-done.14.second = f32[32,256]{1,0:T(8,128)S(1)} collective-permute-done((f32[32,256]{1,0:T(8,128)S(1)}, f32[32,256]{1,0:T(8,128)S(1)}, u32[]{:S(2)}, u32[]{:S(2)}) %collective-permute-start.14) | collective-permute-done | bytes 32800 | tf_op jit(solution)/shard_map/ppermute | solution.py:195
  40.3 0.7 %final.1 = f32[8,32,256]{2,1,0:T(8,128)} custom-call(f32[8,32,256]{2,1,0:T(8,128)} %get-tuple-element.62.part_ref, f32[2,32,256]{2,1,0:T(8,128)S(1)} %get-tuple-element.63.edge_ref, f32[2,32,256]{2,1,0:T(8,128)S(1)} %get-tuple-element.64.factor_ref, f32[32,256]{1,0:T(8,128)S(1)} %collective-permute-done.13.first, ...), custom_call_target="tpu_custom_call", output_to_operand_aliasing={{}: (0, {})} | custom-call | bytes 720896 | tf_op jit(solution)/shard_map/final/pallas_call | solution.py:20
  (5 shorter events, 0.1 us)
Async XLA Ops:
  0.0 0.9 %copy-start.1 = (f32[8,32,256]{2,1,0:T(8,128)S(1)}, f32[8,32,256]{2,1,0:T(8,128)}, u32[]{:S(2)}) copy-start(f32[8,32,256]{2,1,0:T(8,128)} %f_ref.3) | copy-start | bytes 786436
  1.0 9.1 %copy-start.3 = (f32[8,32,256]{2,1,0:T(8,128)S(1)}, f32[8,32,256]{2,1,0:T(8,128)}, u32[]{:S(2)}) copy-start(f32[8,32,256]{2,1,0:T(8,128)} %k_ref.5) | copy-start | bytes 786436
  1.1 1.3 %collective-permute-start = (f32[48,256]{1,0:T(8,128)S(1)}, f32[48,256]{1,0:T(8,128)S(1)}, u32[]{:S(2)}, u32[]{:S(2)}) collective-permute-start(f32[48,256]{1,0:T(8,128)S(1)} %get-tuple-element.37), channel_id=1, source_target_pairs={{0,4},{4,0},{8,12},{12,8},{16,20},{20,16},{24,28},{28,24},{32,36},... | collective-permute-start | bytes 147464 | tf_op jit(solution)/shard_map/ppermute | solution.py:205
  2.4 7.5 %collective-permute-start.1 = (f32[64,256]{1,0:T(8,128)S(1)}, f32[64,256]{1,0:T(8,128)S(1)}, u32[]{:S(2)}, u32[]{:S(2)}) collective-permute-start(f32[64,256]{1,0:T(8,128)S(1)} %get-tuple-element.38), channel_id=1, source_target_pairs={{0,8},{4,64},{8,0},{12,72},{16,24},{20,80},{24,16},{28,88},{32,40}... | collective-permute-start | bytes 196616 | tf_op jit(solution)/shard_map/ppermute | solution.py:187
  4.4 5.4 %collective-permute-start.2 = (f32[16,256]{1,0:T(8,128)S(1)}, f32[16,256]{1,0:T(8,128)S(1)}, u32[]{:S(2)}, u32[]{:S(2)}) collective-permute-start(f32[16,256]{1,0:T(8,128)S(1)} %get-tuple-element.39), channel_id=1, source_target_pairs={{0,7},{1,4},{2,5},{3,6},{4,1},{5,2},{6,3},{7,0},{8,15},{9,12},{10,... | collective-permute-start | bytes 49160 | tf_op jit(solution)/shard_map/ppermute | solution.py:179
  6.6 4.6 %collective-permute-start.4 = (f32[8,256]{1,0:T(8,128)S(1)}, f32[8,256]{1,0:T(8,128)S(1)}, u32[]{:S(2)}, u32[]{:S(2)}) collective-permute-start(f32[8,256]{1,0:T(8,128)S(1)} %get-tuple-element.40), channel_id=1, source_target_pairs={{0,60},{4,8},{8,4},{12,16},{16,12},{20,24},{24,20},{28,32},{32,28}... | collective-permute-start | bytes 24584 | tf_op jit(solution)/shard_map/ppermute | solution.py:202
  9.9 1.4 %copy-start = (bf16[3,8,32,256]{3,2,1,0:T(8,128)(2,1)S(1)}, bf16[3,8,32,256]{3,2,1,0:T(8,128)(2,1)}, u32[]{:S(2)}) copy-start(bf16[3,8,32,256]{3,2,1,0:T(8,128)(2,1)} %wind_ref.3) | copy-start | bytes 1179652
  9.9 1.4 %copy-start.2 = (f32[8,32,256]{2,1,0:T(8,128)S(1)}, f32[8,32,256]{2,1,0:T(8,128)}, u32[]{:S(2)}) copy-start(f32[8,32,256]{2,1,0:T(8,128)} %f_ref.3) | copy-start | bytes 786436
  9.9 1.3 %collective-permute-start.3 = (f32[40,256]{1,0:T(8,128)S(1)}, f32[40,256]{1,0:T(8,128)S(1)}, u32[]{:S(2)}, u32[]{:S(2)}) collective-permute-start(f32[40,256]{1,0:T(8,128)S(1)} %relay.1), channel_id=1, source_target_pairs={{0,4},{4,0},{8,12},{12,8},{16,20},{20,16},{24,28},{28,24},{32,36},... | collective-permute-start | bytes 122888 | tf_op jit(solution)/shard_map/ppermute | solution.py:205
  11.8 1.3 %collective-permute-start.5 = (f32[7,8,256]{2,1,0:T(8,128)S(1)}, f32[7,8,256]{2,1,0:T(8,128)S(1)}, u32[]{:S(2)}, u32[]{:S(2)}) collective-permute-start(f32[7,8,256]{2,1,0:T(8,128)S(1)} %get-tuple-element.45.own_ref.ends_ref), channel_id=1, source_target_pairs={{0,4},{4,0},{8,12},{12,8},{16,20},{20,16},{24,28},{28,24},{32,36},... | collective-permute-start | bytes 172040 | tf_op jit(solution)/shard_map/ppermute | solution.py:205
  13.1 7.1 %collective-permute-start.6 = (f32[6,8,256]{2,1,0:T(8,128)S(1)}, f32[6,8,256]{2,1,0:T(8,128)S(1)}, u32[]{:S(2)}, u32[]{:S(2)}) collective-permute-start(f32[6,8,256]{2,1,0:T(8,128)S(1)} %get-tuple-element.46), channel_id=1, source_target_pairs={{0,60},{4,8},{8,4},{12,16},{16,12},{20,24},{24,20},{28,32},{32,28}... | collective-permute-start | bytes 147464 | tf_op jit(solution)/shard_map/ppermute | solution.py:202
  17.3 8.4 %collective-permute-start.8 = (f32[5,8,256]{2,1,0:T(8,128)S(1)}, f32[5,8,256]{2,1,0:T(8,128)S(1)}, u32[]{:S(2)}, u32[]{:S(2)}) collective-permute-start(f32[5,8,256]{2,1,0:T(8,128)S(1)} %get-tuple-element.47.own_ref), channel_id=1, source_target_pairs={{0,32},{4,36},{8,40},{12,44},{16,48},{20,52},{24,56},{28,60},{32,0... | collective-permute-start | bytes 122888 | tf_op jit(solution)/shard_map/ppermute | solution.py:457
  20.2 6.5 %collective-permute-start.7 = (f32[5,8,256]{2,1,0:T(8,128)S(1)}, f32[5,8,256]{2,1,0:T(8,128)S(1)}, u32[]{:S(2)}, u32[]{:S(2)}) collective-permute-start(f32[5,8,256]{2,1,0:T(8,128)S(1)} %pair.1), channel_id=1, source_target_pairs={{0,16},{4,52},{8,24},{12,60},{16,32},{20,4},{24,40},{28,12},{32,48... | collective-permute-start | bytes 122888 | tf_op jit(solution)/shard_map/ppermute | solution.py:457
  26.8 1.3 %collective-permute-start.9 = (f32[5,8,256]{2,1,0:T(8,128)S(1)}, f32[5,8,256]{2,1,0:T(8,128)S(1)}, u32[]{:S(2)}, u32[]{:S(2)}) collective-permute-start(f32[5,8,256]{2,1,0:T(8,128)S(1)} %side.1.side_ref), channel_id=1, source_target_pairs={{0,4},{4,0},{8,12},{12,8},{16,20},{20,16},{24,28},{28,24},{32,36},... | collective-permute-start | bytes 122888 | tf_op jit(solution)/shard_map/ppermute | solution.py:205
  28.5 5.3 %collective-permute-start.12 = (f32[8,384]{1,0:T(8,128)S(1)}, f32[8,384]{1,0:T(8,128)S(1)}, u32[]{:S(2)}, u32[]{:S(2)}) collective-permute-start(f32[8,384]{1,0:T(8,128)S(1)} %get-tuple-element.52.own_ref), channel_id=1, source_target_pairs={{0,2},{1,3},{2,0},{3,1},{4,6},{5,7},{6,4},{7,5},{8,10},{9,11},{10,... | collective-permute-start | bytes 36872 | tf_op jit(solution)/shard_map/ppermute | solution.py:491
  29.5 4.9 %collective-permute-start.11 = (f32[8,384]{1,0:T(8,128)S(1)}, f32[8,384]{1,0:T(8,128)S(1)}, u32[]{:S(2)}, u32[]{:S(2)}) collective-permute-start(f32[8,384]{1,0:T(8,128)S(1)} %get-tuple-element.52.own_ref), channel_id=1, source_target_pairs={{0,3},{1,2},{2,1},{3,0},{4,7},{5,6},{6,5},{7,4},{8,11},{9,10},{10,... | collective-permute-start | bytes 36872 | tf_op jit(solution)/shard_map/ppermute | solution.py:491
  30.9 3.7 %collective-permute-start.10 = (f32[8,384]{1,0:T(8,128)S(1)}, f32[8,384]{1,0:T(8,128)S(1)}, u32[]{:S(2)}, u32[]{:S(2)}) collective-permute-start(f32[8,384]{1,0:T(8,128)S(1)} %get-tuple-element.52.own_ref), channel_id=1, source_target_pairs={{0,1},{1,0},{2,3},{3,2},{4,5},{5,4},{6,7},{7,6},{8,9},{9,8},{10,11... | collective-permute-start | bytes 36872 | tf_op jit(solution)/shard_map/ppermute | solution.py:491
  34.9 4.0 %collective-permute-start.13 = (f32[32,256]{1,0:T(8,128)S(1)}, f32[32,256]{1,0:T(8,128)S(1)}, u32[]{:S(2)}, u32[]{:S(2)}) collective-permute-start(f32[32,256]{1,0:T(8,128)S(1)} %get-tuple-element.65), channel_id=1, source_target_pairs={{0,64},{4,68},{8,72},{12,76},{16,80},{20,84},{24,88},{28,92},{32,9... | collective-permute-start | bytes 98312 | tf_op jit(solution)/shard_map/ppermute | solution.py:195
  36.4 3.9 %collective-permute-start.14 = (f32[32,256]{1,0:T(8,128)S(1)}, f32[32,256]{1,0:T(8,128)S(1)}, u32[]{:S(2)}, u32[]{:S(2)}) collective-permute-start(f32[32,256]{1,0:T(8,128)S(1)} %get-tuple-element.66), channel_id=1, source_target_pairs={{0,4},{4,0},{8,12},{12,8},{16,20},{20,16},{24,28},{28,24},{32,36},... | collective-permute-start | bytes 98312 | tf_op jit(solution)/shard_map/ppermute | solution.py:195

commit v4 on v3

--- a/solution.py
+++ b/solution.py
@@ -291,7 +291,7 @@
         own, got = read(own_ref), read(got_ref)
         return choose(own_first, own, got), choose(own_first, got, own)
 
-    def chip_kernel(own_ref, got_ref, out_ref, near_ref):
+    def chip_kernel(own_ref, got_ref, out_ref, near_ref, half_ref):
         b0, b1, L, C, R = merge(*ordered(own_ref, got_ref, core() == 0))
         chip = lax.axis_index("gx") // 2
         first, last = chip == 0, chip == chips - 1
@@ -299,17 +299,20 @@
         C = jnp.where(jnp.logical_or(first, last), 0.0, C)
         for n, v in enumerate((b0, b1, L, C, R)):
             out_ref[n] = near_ref[n] = v
+            half_ref[n] = jnp.where(core() == 1, v[:, ny // 2 :], v[:, : ny // 2])
         near_ref[5] = own_ref[5]
 
     def pair_kernel(own_ref, got_ref, out_ref):
         for n, v in enumerate(merge(*ordered(own_ref, got_ref, core() == 1))):
             out_ref[n] = v
 
-    def side_kernel(near_ref, far_ref, opposite_ref, out_ref):
-        three = merge(*ordered(near_ref, far_ref, core() == 1))
-        four = merge(read(opposite_ref), three)
-        for n, v in enumerate(choose(core() == 0, four, three)):
-            out_ref[n] = v
+    def keep_kernel(got_ref, out_ref):
+        out_ref[...] = got_ref[...]
+
+    def side_kernel(near_ref, far_ref, half_ref, out_ref):
+        for n, v in enumerate(merge(*ordered(near_ref, far_ref, core() == 1))):
+            out_ref[n, :, :ny] = v
+            out_ref[n, :, ny:] = half_ref[n]
 
     def x_finish_kernel(
         ends_ref, other_ref, side_ref, got_ref, base_ref, l_ref, r_ref, d_ref, w_ref, c_ref,
@@ -319,12 +322,14 @@
         chip = lax.axis_index("gx") // 2
         a, b = ordered(ends_ref, other_ref, core() == 0)
         left, right = ordered(side_ref, got_ref, core() == 0)
+        opposite = tuple(jnp.concatenate([x[:, ny:], y[:, ny:]], axis=1) for x, y in zip(left, right))
+        left, right = tuple(v[:, :ny] for v in left), tuple(v[:, :ny] for v in right)
         zero = jnp.zeros_like(a[0])
         lp, lg = zero, zero
-        for block in (right, left):
+        for block in (right, opposite, left):
             lp, lg = close_left(lp, lg, block)
         rp, rg = zero, zero
-        for block in (left, right):
+        for block in (left, opposite, right):
             rp, rg = close_right(rp, rg, block)
         lp, lg = jnp.where(chip == 0, 0.0, lp), jnp.where(chip == 0, 0.0, lg)
         rp, rg = jnp.where(chip == chips - 1, 0.0, rp), jnp.where(chip == chips - 1, 0.0, rg)
@@ -472,15 +477,17 @@
         scratch=[pltpu.VMEM(box, jnp.float32)],
     )
     other = sibling(ends)
-    chip, chip_near = call(chip_kernel, [five, (6, nz, ny)], ends, other, name="chip")
-    opposite = outward(chip, chips // 2)
+    half = (5, nz, ny // 2)
+    chip, chip_near, chip_half = call(chip_kernel, [five, (6, nz, ny), half], ends, other, name="chip")
+    opposite = outward(chip_half, chips // 2)
+    (opposite,) = call(keep_kernel, [half], opposite, name="keep", flops=5 * 10**9)
     near = across(chip_near)
     dy, wy, ly, ry, cy = call(
         y_matrix_kernel, [ybox] * 4 + [(4, 7, subs, wide)], dx, near, other, name="y_matrix", flops=10**6
     )
     (pair,) = call(pair_kernel, [five], chip, near, name="pair")
     distant = outward(pair, 2)
-    (side,) = call(side_kernel, [five], near, distant, opposite, name="side")
+    (side,) = call(side_kernel, [(5, nz, ny + ny // 2)], near, distant, opposite, name="side")
     facing = sibling(side)
     ybase, ups, send = call(
         x_finish_kernel, [ybox, (3, 2, subs, wide), (8, wide)],

time: 41 us -> 40.8 us (level)
  waiting for transfers between devices: 13.1 us -> 12.4 us
    pallas_call x13 -> x14, Pallas kernels: 4.24 us -> 4.22 us  [call(): pl.pallas_call(kernel, out_shape=shapes, in_specs=[far if n in far_in els...]
  transfers between devices with their start and end apart: 15 -> 15, of which waited for: 10 -> 9; matrix products, arithmetic and copies ran while one was open for 0% -> 0% of each run, Pallas kernels for 5% -> 5%
where the time goes in v4:
time: 40.8 us; the launch traced here: 40.4 us
  starting transfers between devices  22.6 us (55%)
  waiting for transfers between devices  12.4 us (30%)
  Pallas kernels  4.22 us (10%)
  local copies, waits for them, and re-layouts  0.97 us (2%)
    ppermute x2, starting transfers between devices, across(): lax.ppermute(a, 'gx', [(i, (i + 1 if i % 2 else i - 1) % members) for i i...  7.42 us
    ppermute x2, waiting for transfers between devices, outward(): return lax.ppermute(a, 'gx', [(i, move(i)) for i in range(members)])  5.18 us
    pallas_call x14, Pallas kernels, call(): pl.pallas_call(kernel, out_shape=shapes, in_specs=[far if n in far_in els...  4.22 us
    ppermute x2, starting transfers between devices, outward(): return lax.ppermute(a, 'gx', [(i, move(i)) for i in range(members)])  3.91 us
    ppermute x3, starting transfers between devices, body(): lax.ppermute(send, 'gy', [(i, i ^ back) for i in range(columns)])  3.57 us
    ppermute x2, starting transfers between devices, z_swap(): return lax.ppermute(a, ('gz', 'gx'), pairs)  3.03 us
    ppermute x4, waiting for transfers between devices, sibling(): return lax.ppermute(a, 'gx', [(i, i ^ 1) for i in range(members)])  3.01 us
    ppermute x3, waiting for transfers between devices, body(): lax.ppermute(send, 'gy', [(i, i ^ back) for i in range(columns)])  2.44 us
  transfers between devices with their start and end apart: 15, of which 9 were waited for; matrix products, arithmetic and copies ran while one was open for 0% of the time, Pallas kernels for 5%

profile of v4, /device:TPU:2, one launch (start us, length us, event | category | flops | bytes accessed | tf_op | source)
XLA Modules:
  0.0 40.4 jit_solution(8033161749165568646)
XLA Ops:
  0.0 0.0 copy-start.1
  0.0 0.9 %copy-done.1 = f32[8,32,256]{2,1,0:T(8,128)S(1)} copy-done((f32[8,32,256]{2,1,0:T(8,128)S(1)}, f32[8,32,256]{2,1,0:T(8,128)}, u32[]{:S(2)}) %copy-start.1) | copy-done | bytes 262168
  1.0 0.0 copy-start.3
  1.0 0.1 faces.1
  1.1 0.1 collective-permute-start
  1.2 1.2 %collective-permute-done.got = f32[48,256]{1,0:T(8,128)S(1)} collective-permute-done((f32[48,256]{1,0:T(8,128)S(1)}, f32[48,256]{1,0:T(8,128)S(1)}, u32[]{:S(2)}, u32[]{:S(2)}) %collective-permute-start) | collective-permute-done | bytes 49184 | tf_op jit(solution)/shard_map/ppermute | solution.py:205
  2.4 2.0 %collective-permute-start.1 = (f32[64,256]{1,0:T(8,128)S(1)}, f32[64,256]{1,0:T(8,128)S(1)}, u32[]{:S(2)}, u32[]{:S(2)}) collective-permute-start(f32[64,256]{1,0:T(8,128)S(1)} %get-tuple-element.39), channel_id=1, source_target_pairs={{0,8},{4,64},{8,0},{12,72},{16,24},{20,80},{24,16},{28,88},{32,40}... | collective-permute-start | bytes 196616 | tf_op jit(solution)/shard_map/ppermute | solution.py:187
  4.4 2.2 %collective-permute-start.2 = (f32[16,256]{1,0:T(8,128)S(1)}, f32[16,256]{1,0:T(8,128)S(1)}, u32[]{:S(2)}, u32[]{:S(2)}) collective-permute-start(f32[16,256]{1,0:T(8,128)S(1)} %get-tuple-element.40), channel_id=1, source_target_pairs={{0,7},{1,4},{2,5},{3,6},{4,1},{5,2},{6,3},{7,0},{8,15},{9,12},{10,... | collective-permute-start | bytes 49160 | tf_op jit(solution)/shard_map/ppermute | solution.py:179
  6.6 3.2 %collective-permute-start.4 = (f32[8,256]{1,0:T(8,128)S(1)}, f32[8,256]{1,0:T(8,128)S(1)}, u32[]{:S(2)}, u32[]{:S(2)}) collective-permute-start(f32[8,256]{1,0:T(8,128)S(1)} %get-tuple-element.41), channel_id=1, source_target_pairs={{0,60},{4,8},{8,4},{12,16},{16,12},{20,24},{24,20},{28,32},{32,28}... | collective-permute-start | bytes 24584 | tf_op jit(solution)/shard_map/ppermute | solution.py:202
  9.9 0.0 collective-permute-done.2.columns_in
  9.9 0.0 collective-permute-done.1.planes
  9.9 0.0 copy-start
  9.9 0.0 copy-start.2
  9.9 0.1 collective-permute-start.3
  10.0 0.0 copy-done.3
  10.0 0.4 %x_matrix.1 = (f32[32,8,256]{2,1,0:T(8,128)S(1)}, f32[32,8,256]{2,1,0:T(8,128)S(1)}, f32[32,8,256]{2,1,0:T(8,128)S(1)}, f32[32,8,256]{2,1,0:T(8,128)S(1)}) custom-call(f32[8,32,256]{2,1,0:T(8,128)S(1)} %copy-done.3), custom_call_target="tpu_custom_call" | custom-call | flops 5000000000 | bytes 1310720 | tf_op jit(solution)/shard_map/x_matrix/pallas_call | solution.py:20
  10.4 0.8 %collective-permute-done.4.xc = f32[8,256]{1,0:T(8,128)S(1)} collective-permute-done((f32[8,256]{1,0:T(8,128)S(1)}, f32[8,256]{1,0:T(8,128)S(1)}, u32[]{:S(2)}, u32[]{:S(2)}) %collective-permute-start.4) | collective-permute-done | bytes 8224 | tf_op jit(solution)/shard_map/ppermute | solution.py:202
  11.2 0.0 collective-permute-done.3.relayed
  11.2 0.0 copy-done
  11.2 0.0 copy-done.2
  11.2 0.5 %explicit.1 = (f32[32,8,256]{2,1,0:T(8,128)S(1)}, f32[7,8,256]{2,1,0:T(8,128)S(1)}) custom-call(f32[8,32,256]{2,1,0:T(8,128)S(1)} %copy-done.2, bf16[3,8,32,256]{3,2,1,0:T(8,128)(2,1)S(1)} %copy-done, f32[8,32,256]{2,1,0:T(8,128)S(1)} %copy-done.3, f32[64,256]{1,0:T(8,128)S(1)} %collective-permute-done.1.planes, ...), custom_call_target="tpu_custom_call" | custom-call | bytes 2859008 | tf_op jit(solution)/shard_map/explicit/pallas_call | solution.py:20
  11.8 0.2 collective-permute-start.5
  12.0 1.1 %collective-permute-done.5.got_ref.other_ref = f32[7,8,256]{2,1,0:T(8,128)S(1)} collective-permute-done((f32[7,8,256]{2,1,0:T(8,128)S(1)}, f32[7,8,256]{2,1,0:T(8,128)S(1)}, u32[]{:S(2)}, u32[]{:S(2)}) %collective-permute-start.5) | collective-permute-done | bytes 57376 | tf_op jit(solution)/shard_map/ppermute | solution.py:205
  13.1 4.2 %collective-permute-start.6 = (f32[6,8,256]{2,1,0:T(8,128)S(1)}, f32[6,8,256]{2,1,0:T(8,128)S(1)}, u32[]{:S(2)}, u32[]{:S(2)}) collective-permute-start(f32[6,8,256]{2,1,0:T(8,128)S(1)} %get-tuple-element.47), channel_id=1, source_target_pairs={{0,60},{4,8},{8,4},{12,16},{16,12},{20,24},{24,20},{28,32},{32,28}... | collective-permute-start | bytes 147464 | tf_op jit(solution)/shard_map/ppermute | solution.py:202
  17.3 2.9 %collective-permute-start.8 = (f32[5,8,128]{2,1,0:T(8,128)S(1)}, f32[5,8,128]{2,1,0:T(8,128)S(1)}, u32[]{:S(2)}, u32[]{:S(2)}) collective-permute-start(f32[5,8,128]{2,1,0:T(8,128)S(1)} %get-tuple-element.49), channel_id=1, source_target_pairs={{0,32},{4,36},{8,40},{12,44},{16,48},{20,52},{24,56},{28,60},{32,0... | collective-permute-start | bytes 61448 | tf_op jit(solution)/shard_map/ppermute | solution.py:462
  20.2 0.0 collective-permute-done.6.got_ref.near_ref
  20.2 1.0 %collective-permute-start.7 = (f32[5,8,256]{2,1,0:T(8,128)S(1)}, f32[5,8,256]{2,1,0:T(8,128)S(1)}, u32[]{:S(2)}, u32[]{:S(2)}) collective-permute-start(f32[5,8,256]{2,1,0:T(8,128)S(1)} %pair.1), channel_id=1, source_target_pairs={{0,16},{4,52},{8,24},{12,60},{16,32},{20,4},{24,40},{28,12},{32,48... | collective-permute-start | bytes 122888 | tf_op jit(solution)/shard_map/ppermute | solution.py:462
  21.3 3.8 %collective-permute-done.8.got_ref = f32[5,8,128]{2,1,0:T(8,128)S(1)} collective-permute-done((f32[5,8,128]{2,1,0:T(8,128)S(1)}, f32[5,8,128]{2,1,0:T(8,128)S(1)}, u32[]{:S(2)}, u32[]{:S(2)}) %collective-permute-start.8) | collective-permute-done | bytes 20512 | tf_op jit(solution)/shard_map/ppermute | solution.py:462
  25.0 1.4 %collective-permute-done.7.far_ref = f32[5,8,256]{2,1,0:T(8,128)S(1)} collective-permute-done((f32[5,8,256]{2,1,0:T(8,128)S(1)}, f32[5,8,256]{2,1,0:T(8,128)S(1)}, u32[]{:S(2)}, u32[]{:S(2)}) %collective-permute-start.7) | collective-permute-done | bytes 40992 | tf_op jit(solution)/shard_map/ppermute | solution.py:462
  26.5 0.1 collective-permute-start.9
  26.6 0.5 %y_matrix.1 = (f32[32,8,384]{2,1,0:T(8,128)S(1)}, f32[32,8,384]{2,1,0:T(8,128)S(1)}, f32[32,8,384]{2,1,0:T(8,128)S(1)}, f32[32,8,384]{2,1,0:T(8,128)S(1)}, f32[4,7,8,384]{3,2,1,0:T(8,128)S(1)}) custom-call(f32[32,8,256]{2,1,0:T(8,128)S(1)} %get-tuple-element.42.d_ref.x_ref, f32[6,8,256]{2,1,0:T(8,128)S(1)} %collective-permute-done.6.got_ref.near_ref, ...), custom_call_target="tpu_custom_call" | custom-call | flops 1000000 | bytes 2285568 | tf_op jit(solution)/shard_map/y_matrix/pallas_call | solution.py:20
  27.1 0.7 %collective-permute-done.9.got_ref = f32[5,8,384]{2,1,0:T(8,128)S(1)} collective-permute-done((f32[5,8,384]{2,1,0:T(8,128)S(1)}, f32[5,8,384]{2,1,0:T(8,128)S(1)}, u32[]{:S(2)}, u32[]{:S(2)}) %collective-permute-start.9) | collective-permute-done | bytes 61472 | tf_op jit(solution)/shard_map/ppermute | solution.py:205
  27.8 0.4 %x_finish.1 = (f32[32,8,384]{2,1,0:T(8,128)S(1)}, f32[3,2,8,384]{3,2,1,0:T(8,128)S(1)}, f32[8,384]{1,0:T(8,128)S(1)}) custom-call(f32[7,8,256]{2,1,0:T(8,128)S(1)} %get-tuple-element.46.own_ref.ends_ref, f32[7,8,256]{2,1,0:T(8,128)S(1)} %collective-permute-done.5.got_ref.other_ref, f32[5,8,384]{2,1,0:T(8,128)S(1)} %side.1.side_ref, ...), custom_call_target="tpu_custom_call" | custom-call | bytes 2633728 | tf_op jit(solution)/shard_map/x_finish/pallas_call | solution.py:20
  28.2 1.1 %collective-permute-start.12 = (f32[8,384]{1,0:T(8,128)S(1)}, f32[8,384]{1,0:T(8,128)S(1)}, u32[]{:S(2)}, u32[]{:S(2)}) collective-permute-start(f32[8,384]{1,0:T(8,128)S(1)} %get-tuple-element.54.own_ref), channel_id=1, source_target_pairs={{0,2},{1,3},{2,0},{3,1},{4,6},{5,7},{6,4},{7,5},{8,10},{9,11},{10,... | collective-permute-start | bytes 36872 | tf_op jit(solution)/shard_map/ppermute | solution.py:498
  29.3 1.2 %collective-permute-start.11 = (f32[8,384]{1,0:T(8,128)S(1)}, f32[8,384]{1,0:T(8,128)S(1)}, u32[]{:S(2)}, u32[]{:S(2)}) collective-permute-start(f32[8,384]{1,0:T(8,128)S(1)} %get-tuple-element.54.own_ref), channel_id=1, source_target_pairs={{0,3},{1,2},{2,1},{3,0},{4,7},{5,6},{6,5},{7,4},{8,11},{9,10},{10,... | collective-permute-start | bytes 36872 | tf_op jit(solution)/shard_map/ppermute | solution.py:498
  30.5 1.3 %collective-permute-start.10 = (f32[8,384]{1,0:T(8,128)S(1)}, f32[8,384]{1,0:T(8,128)S(1)}, u32[]{:S(2)}, u32[]{:S(2)}) collective-permute-start(f32[8,384]{1,0:T(8,128)S(1)} %get-tuple-element.54.own_ref), channel_id=1, source_target_pairs={{0,1},{1,0},{2,3},{3,2},{4,5},{5,4},{6,7},{7,6},{8,9},{9,8},{10,11... | collective-permute-start | bytes 36872 | tf_op jit(solution)/shard_map/ppermute | solution.py:498
  31.8 1.7 %collective-permute-done.12.refs_2_ = f32[8,384]{1,0:T(8,128)S(1)} collective-permute-done((f32[8,384]{1,0:T(8,128)S(1)}, f32[8,384]{1,0:T(8,128)S(1)}, u32[]{:S(2)}, u32[]{:S(2)}) %collective-permute-start.12) | collective-permute-done | bytes 12320 | tf_op jit(solution)/shard_map/ppermute | solution.py:498
  33.5 0.7 %collective-permute-done.11.refs_1_ = f32[8,384]{1,0:T(8,128)S(1)} collective-permute-done((f32[8,384]{1,0:T(8,128)S(1)}, f32[8,384]{1,0:T(8,128)S(1)}, u32[]{:S(2)}, u32[]{:S(2)}) %collective-permute-start.11) | collective-permute-done | bytes 12320 | tf_op jit(solution)/shard_map/ppermute | solution.py:498
  34.2 0.0 collective-permute-done.10.refs_0_
  34.2 0.3 y_finish.1
  34.6 1.2 %collective-permute-start.13 = (f32[32,256]{1,0:T(8,128)S(1)}, f32[32,256]{1,0:T(8,128)S(1)}, u32[]{:S(2)}, u32[]{:S(2)}) collective-permute-start(f32[32,256]{1,0:T(8,128)S(1)} %get-tuple-element.67), channel_id=1, source_target_pairs={{0,64},{4,68},{8,72},{12,76},{16,80},{20,84},{24,88},{28,92},{32,9... | collective-permute-start | bytes 98312 | tf_op jit(solution)/shard_map/ppermute | solution.py:195
  35.8 1.8 %collective-permute-start.14 = (f32[32,256]{1,0:T(8,128)S(1)}, f32[32,256]{1,0:T(8,128)S(1)}, u32[]{:S(2)}, u32[]{:S(2)}) collective-permute-start(f32[32,256]{1,0:T(8,128)S(1)} %get-tuple-element.68), channel_id=1, source_target_pairs={{0,4},{4,0},{8,12},{12,8},{16,20},{20,16},{24,28},{28,24},{32,36},... | collective-permute-start | bytes 98312 | tf_op jit(solution)/shard_map/ppermute | solution.py:195
  37.6 1.1 %inner.1 = (f32[8,32,256]{2,1,0:T(8,128)}, f32[2,32,256]{2,1,0:T(8,128)S(1)}, f32[2,32,256]{2,1,0:T(8,128)S(1)}) custom-call(f32[32,8,384]{2,1,0:T(8,128)S(1)} %get-tuple-element.59.t_ref, f32[2,384]{1,0:T(2,128)S(1)} %get-tuple-element.60.ends_ref, f32[8,32,256]{2,1,0:T(8,128)S(1)} %get-tuple-element.61.s_ref, bf16[3,8,32,256]{3,2,1,0:T(8,128)(2,1)S(1)} %copy-done, ...), custom_call_target="tpu_custom_call" | custom-call | flops 5000000000 | bytes 2116608 | tf_op jit(solution)/shard_map/inner/pallas_call | solution.py:20
  38.7 0.0 collective-permute-done.13.first
  38.7 1.0 %collective-permute-done.14.second = f32[32,256]{1,0:T(8,128)S(1)} collective-permute-done((f32[32,256]{1,0:T(8,128)S(1)}, f32[32,256]{1,0:T(8,128)S(1)}, u32[]{:S(2)}, u32[]{:S(2)}) %collective-permute-start.14) | collective-permute-done | bytes 32800 | tf_op jit(solution)/shard_map/ppermute | solution.py:195
  39.7 0.7 %final.1 = f32[8,32,256]{2,1,0:T(8,128)} custom-call(f32[8,32,256]{2,1,0:T(8,128)} %get-tuple-element.64.part_ref, f32[2,32,256]{2,1,0:T(8,128)S(1)} %get-tuple-element.65.edge_ref, f32[2,32,256]{2,1,0:T(8,128)S(1)} %get-tuple-element.66.factor_ref, f32[32,256]{1,0:T(8,128)S(1)} %collective-permute-done.13.first, ...), custom_call_target="tpu_custom_call", output_to_operand_aliasing={{}: (0, {})} | custom-call | bytes 720896 | tf_op jit(solution)/shard_map/final/pallas_call | solution.py:20
  (6 shorter events, 0.1 us)
Async XLA Ops:
  0.0 0.9 %copy-start.1 = (f32[8,32,256]{2,1,0:T(8,128)S(1)}, f32[8,32,256]{2,1,0:T(8,128)}, u32[]{:S(2)}) copy-start(f32[8,32,256]{2,1,0:T(8,128)} %f_ref.3) | copy-start | bytes 786436
  1.0 9.1 %copy-start.3 = (f32[8,32,256]{2,1,0:T(8,128)S(1)}, f32[8,32,256]{2,1,0:T(8,128)}, u32[]{:S(2)}) copy-start(f32[8,32,256]{2,1,0:T(8,128)} %k_ref.5) | copy-start | bytes 786436
  1.1 1.3 %collective-permute-start = (f32[48,256]{1,0:T(8,128)S(1)}, f32[48,256]{1,0:T(8,128)S(1)}, u32[]{:S(2)}, u32[]{:S(2)}) collective-permute-start(f32[48,256]{1,0:T(8,128)S(1)} %get-tuple-element.38), channel_id=1, source_target_pairs={{0,4},{4,0},{8,12},{12,8},{16,20},{20,16},{24,28},{28,24},{32,36},... | collective-permute-start | bytes 147464 | tf_op jit(solution)/shard_map/ppermute | solution.py:205
  2.4 7.5 %collective-permute-start.1 = (f32[64,256]{1,0:T(8,128)S(1)}, f32[64,256]{1,0:T(8,128)S(1)}, u32[]{:S(2)}, u32[]{:S(2)}) collective-permute-start(f32[64,256]{1,0:T(8,128)S(1)} %get-tuple-element.39), channel_id=1, source_target_pairs={{0,8},{4,64},{8,0},{12,72},{16,24},{20,80},{24,16},{28,88},{32,40}... | collective-permute-start | bytes 196616 | tf_op jit(solution)/shard_map/ppermute | solution.py:187
  4.4 5.4 %collective-permute-start.2 = (f32[16,256]{1,0:T(8,128)S(1)}, f32[16,256]{1,0:T(8,128)S(1)}, u32[]{:S(2)}, u32[]{:S(2)}) collective-permute-start(f32[16,256]{1,0:T(8,128)S(1)} %get-tuple-element.40), channel_id=1, source_target_pairs={{0,7},{1,4},{2,5},{3,6},{4,1},{5,2},{6,3},{7,0},{8,15},{9,12},{10,... | collective-permute-start | bytes 49160 | tf_op jit(solution)/shard_map/ppermute | solution.py:179
  6.6 4.6 %collective-permute-start.4 = (f32[8,256]{1,0:T(8,128)S(1)}, f32[8,256]{1,0:T(8,128)S(1)}, u32[]{:S(2)}, u32[]{:S(2)}) collective-permute-start(f32[8,256]{1,0:T(8,128)S(1)} %get-tuple-element.41), channel_id=1, source_target_pairs={{0,60},{4,8},{8,4},{12,16},{16,12},{20,24},{24,20},{28,32},{32,28}... | collective-permute-start | bytes 24584 | tf_op jit(solution)/shard_map/ppermute | solution.py:202
  9.9 1.4 %copy-start = (bf16[3,8,32,256]{3,2,1,0:T(8,128)(2,1)S(1)}, bf16[3,8,32,256]{3,2,1,0:T(8,128)(2,1)}, u32[]{:S(2)}) copy-start(bf16[3,8,32,256]{3,2,1,0:T(8,128)(2,1)} %wind_ref.3) | copy-start | bytes 1179652
  9.9 1.4 %copy-start.2 = (f32[8,32,256]{2,1,0:T(8,128)S(1)}, f32[8,32,256]{2,1,0:T(8,128)}, u32[]{:S(2)}) copy-start(f32[8,32,256]{2,1,0:T(8,128)} %f_ref.3) | copy-start | bytes 786436
  9.9 1.3 %collective-permute-start.3 = (f32[40,256]{1,0:T(8,128)S(1)}, f32[40,256]{1,0:T(8,128)S(1)}, u32[]{:S(2)}, u32[]{:S(2)}) collective-permute-start(f32[40,256]{1,0:T(8,128)S(1)} %relay.1), channel_id=1, source_target_pairs={{0,4},{4,0},{8,12},{12,8},{16,20},{20,16},{24,28},{28,24},{32,36},... | collective-permute-start | bytes 122888 | tf_op jit(solution)/shard_map/ppermute | solution.py:205
  11.8 1.3 %collective-permute-start.5 = (f32[7,8,256]{2,1,0:T(8,128)S(1)}, f32[7,8,256]{2,1,0:T(8,128)S(1)}, u32[]{:S(2)}, u32[]{:S(2)}) collective-permute-start(f32[7,8,256]{2,1,0:T(8,128)S(1)} %get-tuple-element.46.own_ref.ends_ref), channel_id=1, source_target_pairs={{0,4},{4,0},{8,12},{12,8},{16,20},{20,16},{24,28},{28,24},{32,36},... | collective-permute-start | bytes 172040 | tf_op jit(solution)/shard_map/ppermute | solution.py:205
  13.1 7.1 %collective-permute-start.6 = (f32[6,8,256]{2,1,0:T(8,128)S(1)}, f32[6,8,256]{2,1,0:T(8,128)S(1)}, u32[]{:S(2)}, u32[]{:S(2)}) collective-permute-start(f32[6,8,256]{2,1,0:T(8,128)S(1)} %get-tuple-element.47), channel_id=1, source_target_pairs={{0,60},{4,8},{8,4},{12,16},{16,12},{20,24},{24,20},{28,32},{32,28}... | collective-permute-start | bytes 147464 | tf_op jit(solution)/shard_map/ppermute | solution.py:202
  17.3 7.7 %collective-permute-start.8 = (f32[5,8,128]{2,1,0:T(8,128)S(1)}, f32[5,8,128]{2,1,0:T(8,128)S(1)}, u32[]{:S(2)}, u32[]{:S(2)}) collective-permute-start(f32[5,8,128]{2,1,0:T(8,128)S(1)} %get-tuple-element.49), channel_id=1, source_target_pairs={{0,32},{4,36},{8,40},{12,44},{16,48},{20,52},{24,56},{28,60},{32,0... | collective-permute-start | bytes 61448 | tf_op jit(solution)/shard_map/ppermute | solution.py:462
  20.2 6.2 %collective-permute-start.7 = (f32[5,8,256]{2,1,0:T(8,128)S(1)}, f32[5,8,256]{2,1,0:T(8,128)S(1)}, u32[]{:S(2)}, u32[]{:S(2)}) collective-permute-start(f32[5,8,256]{2,1,0:T(8,128)S(1)} %pair.1), channel_id=1, source_target_pairs={{0,16},{4,52},{8,24},{12,60},{16,32},{20,4},{24,40},{28,12},{32,48... | collective-permute-start | bytes 122888 | tf_op jit(solution)/shard_map/ppermute | solution.py:462
  26.5 1.3 %collective-permute-start.9 = (f32[5,8,384]{2,1,0:T(8,128)S(1)}, f32[5,8,384]{2,1,0:T(8,128)S(1)}, u32[]{:S(2)}, u32[]{:S(2)}) collective-permute-start(f32[5,8,384]{2,1,0:T(8,128)S(1)} %side.1.side_ref), channel_id=1, source_target_pairs={{0,4},{4,0},{8,12},{12,8},{16,20},{20,16},{24,28},{28,24},{32,36},... | collective-permute-start | bytes 184328 | tf_op jit(solution)/shard_map/ppermute | solution.py:205
  28.2 5.3 %collective-permute-start.12 = (f32[8,384]{1,0:T(8,128)S(1)}, f32[8,384]{1,0:T(8,128)S(1)}, u32[]{:S(2)}, u32[]{:S(2)}) collective-permute-start(f32[8,384]{1,0:T(8,128)S(1)} %get-tuple-element.54.own_ref), channel_id=1, source_target_pairs={{0,2},{1,3},{2,0},{3,1},{4,6},{5,7},{6,4},{7,5},{8,10},{9,11},{10,... | collective-permute-start | bytes 36872 | tf_op jit(solution)/shard_map/ppermute | solution.py:498
  29.3 4.9 %collective-permute-start.11 = (f32[8,384]{1,0:T(8,128)S(1)}, f32[8,384]{1,0:T(8,128)S(1)}, u32[]{:S(2)}, u32[]{:S(2)}) collective-permute-start(f32[8,384]{1,0:T(8,128)S(1)} %get-tuple-element.54.own_ref), channel_id=1, source_target_pairs={{0,3},{1,2},{2,1},{3,0},{4,7},{5,6},{6,5},{7,4},{8,11},{9,10},{10,... | collective-permute-start | bytes 36872 | tf_op jit(solution)/shard_map/ppermute | solution.py:498
  30.5 3.7 %collective-permute-start.10 = (f32[8,384]{1,0:T(8,128)S(1)}, f32[8,384]{1,0:T(8,128)S(1)}, u32[]{:S(2)}, u32[]{:S(2)}) collective-permute-start(f32[8,384]{1,0:T(8,128)S(1)} %get-tuple-element.54.own_ref), channel_id=1, source_target_pairs={{0,1},{1,0},{2,3},{3,2},{4,5},{5,4},{6,7},{7,6},{8,9},{9,8},{10,11... | collective-permute-start | bytes 36872 | tf_op jit(solution)/shard_map/ppermute | solution.py:498
  34.6 4.1 %collective-permute-start.13 = (f32[32,256]{1,0:T(8,128)S(1)}, f32[32,256]{1,0:T(8,128)S(1)}, u32[]{:S(2)}, u32[]{:S(2)}) collective-permute-start(f32[32,256]{1,0:T(8,128)S(1)} %get-tuple-element.67), channel_id=1, source_target_pairs={{0,64},{4,68},{8,72},{12,76},{16,80},{20,84},{24,88},{28,92},{32,9... | collective-permute-start | bytes 98312 | tf_op jit(solution)/shard_map/ppermute | solution.py:195
  35.8 3.9 %collective-permute-start.14 = (f32[32,256]{1,0:T(8,128)S(1)}, f32[32,256]{1,0:T(8,128)S(1)}, u32[]{:S(2)}, u32[]{:S(2)}) collective-permute-start(f32[32,256]{1,0:T(8,128)S(1)} %get-tuple-element.68), channel_id=1, source_target_pairs={{0,4},{4,0},{8,12},{12,8},{16,20},{20,16},{24,28},{28,24},{32,36},... | collective-permute-start | bytes 98312 | tf_op jit(solution)/shard_map/ppermute | solution.py:195

commit v5 on v4

--- a/solution.py
+++ b/solution.py
@@ -190,12 +190,12 @@
         pairs = []
         for z in range(levels):
             for x in range(members):
-                to = z + (1 if z % 2 == parity else -1)
-                pairs.append((z * members + x, to * members + x if 0 <= to < levels else z * members + (x ^ 1)))
+                to = z + (1 if (z + x) % 2 == parity else -1)
+                pairs.append((z * members + x, to * members + x if 0 <= to < levels else z * members + (x ^ 2)))
         return lax.ppermute(a, ("gz", "gx"), pairs)
 
     def z_order(low, high):
-        even = lax.rem(lax.axis_index("gz"), 2) == 0
+        even = lax.rem(lax.axis_index("gz") + lax.axis_index("gx"), 2) == 0
         return jnp.where(even, high, low), jnp.where(even, low, high)
 
     def across(a):

time: 40.8 us -> 40.8 us (level)
  no operation moved by 1% of the time
where the time goes in v5:
time: 40.8 us; the launch traced here: 40.4 us
  starting transfers between devices  22.6 us (55%)
  waiting for transfers between devices  12.4 us (30%)
  Pallas kernels  4.22 us (10%)
  local copies, waits for them, and re-layouts  0.97 us (2%)
    ppermute x2, starting transfers between devices, across(): lax.ppermute(a, 'gx', [(i, (i + 1 if i % 2 else i - 1) % members) for i i...  7.42 us
    ppermute x2, waiting for transfers between devices, outward(): return lax.ppermute(a, 'gx', [(i, move(i)) for i in range(members)])  5.18 us
    pallas_call x14, Pallas kernels, call(): pl.pallas_call(kernel, out_shape=shapes, in_specs=[far if n in far_in els...  4.22 us
    ppermute x2, starting transfers between devices, outward(): return lax.ppermute(a, 'gx', [(i, move(i)) for i in range(members)])  3.91 us
    ppermute x3, starting transfers between devices, body(): lax.ppermute(send, 'gy', [(i, i ^ back) for i in range(columns)])  3.57 us
    ppermute x2, starting transfers between devices, z_swap(): return lax.ppermute(a, ('gz', 'gx'), pairs)  3.03 us
    ppermute x4, waiting for transfers between devices, sibling(): return lax.ppermute(a, 'gx', [(i, i ^ 1) for i in range(members)])  3.01 us
    ppermute x3, waiting for transfers between devices, body(): lax.ppermute(send, 'gy', [(i, i ^ back) for i in range(columns)])  2.44 us
  transfers between devices with their start and end apart: 15, of which 9 were waited for; matrix products, arithmetic and copies ran while one was open for 0% of the time, Pallas kernels for 5%

profile of v5, /device:TPU:2, one launch (start us, length us, event | category | flops | bytes accessed | tf_op | source)
XLA Modules:
  0.0 40.4 jit_solution(8176254574620197559)
XLA Ops:
  0.0 0.0 copy-start.1
  0.0 0.9 %copy-done.1 = f32[8,32,256]{2,1,0:T(8,128)S(1)} copy-done((f32[8,32,256]{2,1,0:T(8,128)S(1)}, f32[8,32,256]{2,1,0:T(8,128)}, u32[]{:S(2)}) %copy-start.1) | copy-done | bytes 262168
  1.0 0.0 copy-start.3
  1.0 0.1 faces.1
  1.1 0.1 collective-permute-start
  1.2 1.2 %collective-permute-done.got = f32[48,256]{1,0:T(8,128)S(1)} collective-permute-done((f32[48,256]{1,0:T(8,128)S(1)}, f32[48,256]{1,0:T(8,128)S(1)}, u32[]{:S(2)}, u32[]{:S(2)}) %collective-permute-start) | collective-permute-done | bytes 49184 | tf_op jit(solution)/shard_map/ppermute | solution.py:205
  2.4 2.0 %collective-permute-start.1 = (f32[64,256]{1,0:T(8,128)S(1)}, f32[64,256]{1,0:T(8,128)S(1)}, u32[]{:S(2)}, u32[]{:S(2)}) collective-permute-start(f32[64,256]{1,0:T(8,128)S(1)} %get-tuple-element.39), channel_id=1, source_target_pairs={{0,8},{4,64},{8,0},{12,72},{16,24},{20,80},{24,16},{28,88},{32,40}... | collective-permute-start | bytes 196616 | tf_op jit(solution)/shard_map/ppermute | solution.py:187
  4.4 2.2 %collective-permute-start.2 = (f32[16,256]{1,0:T(8,128)S(1)}, f32[16,256]{1,0:T(8,128)S(1)}, u32[]{:S(2)}, u32[]{:S(2)}) collective-permute-start(f32[16,256]{1,0:T(8,128)S(1)} %get-tuple-element.40), channel_id=1, source_target_pairs={{0,7},{1,4},{2,5},{3,6},{4,1},{5,2},{6,3},{7,0},{8,15},{9,12},{10,... | collective-permute-start | bytes 49160 | tf_op jit(solution)/shard_map/ppermute | solution.py:179
  6.6 3.2 %collective-permute-start.4 = (f32[8,256]{1,0:T(8,128)S(1)}, f32[8,256]{1,0:T(8,128)S(1)}, u32[]{:S(2)}, u32[]{:S(2)}) collective-permute-start(f32[8,256]{1,0:T(8,128)S(1)} %get-tuple-element.41), channel_id=1, source_target_pairs={{0,60},{4,8},{8,4},{12,16},{16,12},{20,24},{24,20},{28,32},{32,28}... | collective-permute-start | bytes 24584 | tf_op jit(solution)/shard_map/ppermute | solution.py:202
  9.9 0.0 collective-permute-done.2.columns_in
  9.9 0.0 collective-permute-done.1.planes
  9.9 0.0 copy-start
  9.9 0.0 copy-start.2
  9.9 0.1 collective-permute-start.3
  10.0 0.0 copy-done.3
  10.0 0.4 %x_matrix.1 = (f32[32,8,256]{2,1,0:T(8,128)S(1)}, f32[32,8,256]{2,1,0:T(8,128)S(1)}, f32[32,8,256]{2,1,0:T(8,128)S(1)}, f32[32,8,256]{2,1,0:T(8,128)S(1)}) custom-call(f32[8,32,256]{2,1,0:T(8,128)S(1)} %copy-done.3), custom_call_target="tpu_custom_call" | custom-call | flops 5000000000 | bytes 1310720 | tf_op jit(solution)/shard_map/x_matrix/pallas_call | solution.py:20
  10.4 0.8 %collective-permute-done.4.xc = f32[8,256]{1,0:T(8,128)S(1)} collective-permute-done((f32[8,256]{1,0:T(8,128)S(1)}, f32[8,256]{1,0:T(8,128)S(1)}, u32[]{:S(2)}, u32[]{:S(2)}) %collective-permute-start.4) | collective-permute-done | bytes 8224 | tf_op jit(solution)/shard_map/ppermute | solution.py:202
  11.2 0.0 collective-permute-done.3.relayed
  11.2 0.0 copy-done
  11.2 0.0 copy-done.2
  11.2 0.5 %explicit.1 = (f32[32,8,256]{2,1,0:T(8,128)S(1)}, f32[7,8,256]{2,1,0:T(8,128)S(1)}) custom-call(f32[8,32,256]{2,1,0:T(8,128)S(1)} %copy-done.2, bf16[3,8,32,256]{3,2,1,0:T(8,128)(2,1)S(1)} %copy-done, f32[8,32,256]{2,1,0:T(8,128)S(1)} %copy-done.3, f32[64,256]{1,0:T(8,128)S(1)} %collective-permute-done.1.planes, ...), custom_call_target="tpu_custom_call" | custom-call | bytes 2859008 | tf_op jit(solution)/shard_map/explicit/pallas_call | solution.py:20
  11.8 0.2 collective-permute-start.5
  12.0 1.1 %collective-permute-done.5.got_ref.other_ref = f32[7,8,256]{2,1,0:T(8,128)S(1)} collective-permute-done((f32[7,8,256]{2,1,0:T(8,128)S(1)}, f32[7,8,256]{2,1,0:T(8,128)S(1)}, u32[]{:S(2)}, u32[]{:S(2)}) %collective-permute-start.5) | collective-permute-done | bytes 57376 | tf_op jit(solution)/shard_map/ppermute | solution.py:205
  13.1 4.2 %collective-permute-start.6 = (f32[6,8,256]{2,1,0:T(8,128)S(1)}, f32[6,8,256]{2,1,0:T(8,128)S(1)}, u32[]{:S(2)}, u32[]{:S(2)}) collective-permute-start(f32[6,8,256]{2,1,0:T(8,128)S(1)} %get-tuple-element.47), channel_id=1, source_target_pairs={{0,60},{4,8},{8,4},{12,16},{16,12},{20,24},{24,20},{28,32},{32,28}... | collective-permute-start | bytes 147464 | tf_op jit(solution)/shard_map/ppermute | solution.py:202
  17.3 2.9 %collective-permute-start.8 = (f32[5,8,128]{2,1,0:T(8,128)S(1)}, f32[5,8,128]{2,1,0:T(8,128)S(1)}, u32[]{:S(2)}, u32[]{:S(2)}) collective-permute-start(f32[5,8,128]{2,1,0:T(8,128)S(1)} %get-tuple-element.49), channel_id=1, source_target_pairs={{0,32},{4,36},{8,40},{12,44},{16,48},{20,52},{24,56},{28,60},{32,0... | collective-permute-start | bytes 61448 | tf_op jit(solution)/shard_map/ppermute | solution.py:462
  20.2 0.0 collective-permute-done.6.got_ref.near_ref
  20.2 1.0 %collective-permute-start.7 = (f32[5,8,256]{2,1,0:T(8,128)S(1)}, f32[5,8,256]{2,1,0:T(8,128)S(1)}, u32[]{:S(2)}, u32[]{:S(2)}) collective-permute-start(f32[5,8,256]{2,1,0:T(8,128)S(1)} %pair.1), channel_id=1, source_target_pairs={{0,16},{4,52},{8,24},{12,60},{16,32},{20,4},{24,40},{28,12},{32,48... | collective-permute-start | bytes 122888 | tf_op jit(solution)/shard_map/ppermute | solution.py:462
  21.3 3.8 %collective-permute-done.8.got_ref = f32[5,8,128]{2,1,0:T(8,128)S(1)} collective-permute-done((f32[5,8,128]{2,1,0:T(8,128)S(1)}, f32[5,8,128]{2,1,0:T(8,128)S(1)}, u32[]{:S(2)}, u32[]{:S(2)}) %collective-permute-start.8) | collective-permute-done | bytes 20512 | tf_op jit(solution)/shard_map/ppermute | solution.py:462
  25.0 1.4 %collective-permute-done.7.far_ref = f32[5,8,256]{2,1,0:T(8,128)S(1)} collective-permute-done((f32[5,8,256]{2,1,0:T(8,128)S(1)}, f32[5,8,256]{2,1,0:T(8,128)S(1)}, u32[]{:S(2)}, u32[]{:S(2)}) %collective-permute-start.7) | collective-permute-done | bytes 40992 | tf_op jit(solution)/shard_map/ppermute | solution.py:462
  26.5 0.1 collective-permute-start.9
  26.6 0.5 %y_matrix.1 = (f32[32,8,384]{2,1,0:T(8,128)S(1)}, f32[32,8,384]{2,1,0:T(8,128)S(1)}, f32[32,8,384]{2,1,0:T(8,128)S(1)}, f32[32,8,384]{2,1,0:T(8,128)S(1)}, f32[4,7,8,384]{3,2,1,0:T(8,128)S(1)}) custom-call(f32[32,8,256]{2,1,0:T(8,128)S(1)} %get-tuple-element.42.d_ref.x_ref, f32[6,8,256]{2,1,0:T(8,128)S(1)} %collective-permute-done.6.got_ref.near_ref, ...), custom_call_target="tpu_custom_call" | custom-call | flops 1000000 | bytes 2285568 | tf_op jit(solution)/shard_map/y_matrix/pallas_call | solution.py:20
  27.1 0.7 %collective-permute-done.9.got_ref = f32[5,8,384]{2,1,0:T(8,128)S(1)} collective-permute-done((f32[5,8,384]{2,1,0:T(8,128)S(1)}, f32[5,8,384]{2,1,0:T(8,128)S(1)}, u32[]{:S(2)}, u32[]{:S(2)}) %collective-permute-start.9) | collective-permute-done | bytes 61472 | tf_op jit(solution)/shard_map/ppermute | solution.py:205
  27.8 0.4 %x_finish.1 = (f32[32,8,384]{2,1,0:T(8,128)S(1)}, f32[3,2,8,384]{3,2,1,0:T(8,128)S(1)}, f32[8,384]{1,0:T(8,128)S(1)}) custom-call(f32[7,8,256]{2,1,0:T(8,128)S(1)} %get-tuple-element.46.own_ref.ends_ref, f32[7,8,256]{2,1,0:T(8,128)S(1)} %collective-permute-done.5.got_ref.other_ref, f32[5,8,384]{2,1,0:T(8,128)S(1)} %side.1.side_ref, ...), custom_call_target="tpu_custom_call" | custom-call | bytes 2633728 | tf_op jit(solution)/shard_map/x_finish/pallas_call | solution.py:20
  28.2 1.1 %collective-permute-start.12 = (f32[8,384]{1,0:T(8,128)S(1)}, f32[8,384]{1,0:T(8,128)S(1)}, u32[]{:S(2)}, u32[]{:S(2)}) collective-permute-start(f32[8,384]{1,0:T(8,128)S(1)} %get-tuple-element.54.own_ref), channel_id=1, source_target_pairs={{0,2},{1,3},{2,0},{3,1},{4,6},{5,7},{6,4},{7,5},{8,10},{9,11},{10,... | collective-permute-start | bytes 36872 | tf_op jit(solution)/shard_map/ppermute | solution.py:498
  29.3 1.2 %collective-permute-start.11 = (f32[8,384]{1,0:T(8,128)S(1)}, f32[8,384]{1,0:T(8,128)S(1)}, u32[]{:S(2)}, u32[]{:S(2)}) collective-permute-start(f32[8,384]{1,0:T(8,128)S(1)} %get-tuple-element.54.own_ref), channel_id=1, source_target_pairs={{0,3},{1,2},{2,1},{3,0},{4,7},{5,6},{6,5},{7,4},{8,11},{9,10},{10,... | collective-permute-start | bytes 36872 | tf_op jit(solution)/shard_map/ppermute | solution.py:498
  30.5 1.3 %collective-permute-start.10 = (f32[8,384]{1,0:T(8,128)S(1)}, f32[8,384]{1,0:T(8,128)S(1)}, u32[]{:S(2)}, u32[]{:S(2)}) collective-permute-start(f32[8,384]{1,0:T(8,128)S(1)} %get-tuple-element.54.own_ref), channel_id=1, source_target_pairs={{0,1},{1,0},{2,3},{3,2},{4,5},{5,4},{6,7},{7,6},{8,9},{9,8},{10,11... | collective-permute-start | bytes 36872 | tf_op jit(solution)/shard_map/ppermute | solution.py:498
  31.8 1.7 %collective-permute-done.12.refs_2_ = f32[8,384]{1,0:T(8,128)S(1)} collective-permute-done((f32[8,384]{1,0:T(8,128)S(1)}, f32[8,384]{1,0:T(8,128)S(1)}, u32[]{:S(2)}, u32[]{:S(2)}) %collective-permute-start.12) | collective-permute-done | bytes 12320 | tf_op jit(solution)/shard_map/ppermute | solution.py:498
  33.5 0.7 %collective-permute-done.11.refs_1_ = f32[8,384]{1,0:T(8,128)S(1)} collective-permute-done((f32[8,384]{1,0:T(8,128)S(1)}, f32[8,384]{1,0:T(8,128)S(1)}, u32[]{:S(2)}, u32[]{:S(2)}) %collective-permute-start.11) | collective-permute-done | bytes 12320 | tf_op jit(solution)/shard_map/ppermute | solution.py:498
  34.2 0.0 collective-permute-done.10.refs_0_
  34.2 0.3 y_finish.1
  34.6 1.2 %collective-permute-start.13 = (f32[32,256]{1,0:T(8,128)S(1)}, f32[32,256]{1,0:T(8,128)S(1)}, u32[]{:S(2)}, u32[]{:S(2)}) collective-permute-start(f32[32,256]{1,0:T(8,128)S(1)} %get-tuple-element.67), channel_id=1, source_target_pairs={{0,64},{4,12},{8,72},{12,4},{16,80},{20,28},{24,88},{28,20},{32,96... | collective-permute-start | bytes 98312 | tf_op jit(solution)/shard_map/ppermute | solution.py:195
  35.8 1.8 %collective-permute-start.14 = (f32[32,256]{1,0:T(8,128)S(1)}, f32[32,256]{1,0:T(8,128)S(1)}, u32[]{:S(2)}, u32[]{:S(2)}) collective-permute-start(f32[32,256]{1,0:T(8,128)S(1)} %get-tuple-element.68), channel_id=1, source_target_pairs={{0,8},{4,68},{8,0},{12,76},{16,24},{20,84},{24,16},{28,92},{32,40}... | collective-permute-start | bytes 98312 | tf_op jit(solution)/shard_map/ppermute | solution.py:195
  37.6 1.1 %inner.1 = (f32[8,32,256]{2,1,0:T(8,128)}, f32[2,32,256]{2,1,0:T(8,128)S(1)}, f32[2,32,256]{2,1,0:T(8,128)S(1)}) custom-call(f32[32,8,384]{2,1,0:T(8,128)S(1)} %get-tuple-element.59.t_ref, f32[2,384]{1,0:T(2,128)S(1)} %get-tuple-element.60.ends_ref, f32[8,32,256]{2,1,0:T(8,128)S(1)} %get-tuple-element.61.s_ref, bf16[3,8,32,256]{3,2,1,0:T(8,128)(2,1)S(1)} %copy-done, ...), custom_call_target="tpu_custom_call" | custom-call | flops 5000000000 | bytes 2116608 | tf_op jit(solution)/shard_map/inner/pallas_call | solution.py:20
  38.7 0.0 collective-permute-done.13.first
  38.7 1.0 %collective-permute-done.14.second = f32[32,256]{1,0:T(8,128)S(1)} collective-permute-done((f32[32,256]{1,0:T(8,128)S(1)}, f32[32,256]{1,0:T(8,128)S(1)}, u32[]{:S(2)}, u32[]{:S(2)}) %collective-permute-start.14) | collective-permute-done | bytes 32800 | tf_op jit(solution)/shard_map/ppermute | solution.py:195
  39.7 0.7 %final.1 = f32[8,32,256]{2,1,0:T(8,128)} custom-call(f32[8,32,256]{2,1,0:T(8,128)} %get-tuple-element.64.part_ref, f32[2,32,256]{2,1,0:T(8,128)S(1)} %get-tuple-element.65.edge_ref, f32[2,32,256]{2,1,0:T(8,128)S(1)} %get-tuple-element.66.factor_ref, f32[32,256]{1,0:T(8,128)S(1)} %collective-permute-done.13.first, ...), custom_call_target="tpu_custom_call", output_to_operand_aliasing={{}: (0, {})} | custom-call | bytes 720896 | tf_op jit(solution)/shard_map/final/pallas_call | solution.py:20
  (6 shorter events, 0.1 us)
Async XLA Ops:
  0.0 0.9 %copy-start.1 = (f32[8,32,256]{2,1,0:T(8,128)S(1)}, f32[8,32,256]{2,1,0:T(8,128)}, u32[]{:S(2)}) copy-start(f32[8,32,256]{2,1,0:T(8,128)} %f_ref.3) | copy-start | bytes 786436
  1.0 9.1 %copy-start.3 = (f32[8,32,256]{2,1,0:T(8,128)S(1)}, f32[8,32,256]{2,1,0:T(8,128)}, u32[]{:S(2)}) copy-start(f32[8,32,256]{2,1,0:T(8,128)} %k_ref.5) | copy-start | bytes 786436
  1.1 1.3 %collective-permute-start = (f32[48,256]{1,0:T(8,128)S(1)}, f32[48,256]{1,0:T(8,128)S(1)}, u32[]{:S(2)}, u32[]{:S(2)}) collective-permute-start(f32[48,256]{1,0:T(8,128)S(1)} %get-tuple-element.38), channel_id=1, source_target_pairs={{0,4},{4,0},{8,12},{12,8},{16,20},{20,16},{24,28},{28,24},{32,36},... | collective-permute-start | bytes 147464 | tf_op jit(solution)/shard_map/ppermute | solution.py:205
  2.4 7.5 %collective-permute-start.1 = (f32[64,256]{1,0:T(8,128)S(1)}, f32[64,256]{1,0:T(8,128)S(1)}, u32[]{:S(2)}, u32[]{:S(2)}) collective-permute-start(f32[64,256]{1,0:T(8,128)S(1)} %get-tuple-element.39), channel_id=1, source_target_pairs={{0,8},{4,64},{8,0},{12,72},{16,24},{20,80},{24,16},{28,88},{32,40}... | collective-permute-start | bytes 196616 | tf_op jit(solution)/shard_map/ppermute | solution.py:187
  4.4 5.4 %collective-permute-start.2 = (f32[16,256]{1,0:T(8,128)S(1)}, f32[16,256]{1,0:T(8,128)S(1)}, u32[]{:S(2)}, u32[]{:S(2)}) collective-permute-start(f32[16,256]{1,0:T(8,128)S(1)} %get-tuple-element.40), channel_id=1, source_target_pairs={{0,7},{1,4},{2,5},{3,6},{4,1},{5,2},{6,3},{7,0},{8,15},{9,12},{10,... | collective-permute-start | bytes 49160 | tf_op jit(solution)/shard_map/ppermute | solution.py:179
  6.6 4.6 %collective-permute-start.4 = (f32[8,256]{1,0:T(8,128)S(1)}, f32[8,256]{1,0:T(8,128)S(1)}, u32[]{:S(2)}, u32[]{:S(2)}) collective-permute-start(f32[8,256]{1,0:T(8,128)S(1)} %get-tuple-element.41), channel_id=1, source_target_pairs={{0,60},{4,8},{8,4},{12,16},{16,12},{20,24},{24,20},{28,32},{32,28}... | collective-permute-start | bytes 24584 | tf_op jit(solution)/shard_map/ppermute | solution.py:202
  9.9 1.4 %copy-start = (bf16[3,8,32,256]{3,2,1,0:T(8,128)(2,1)S(1)}, bf16[3,8,32,256]{3,2,1,0:T(8,128)(2,1)}, u32[]{:S(2)}) copy-start(bf16[3,8,32,256]{3,2,1,0:T(8,128)(2,1)} %wind_ref.3) | copy-start | bytes 1179652
  9.9 1.4 %copy-start.2 = (f32[8,32,256]{2,1,0:T(8,128)S(1)}, f32[8,32,256]{2,1,0:T(8,128)}, u32[]{:S(2)}) copy-start(f32[8,32,256]{2,1,0:T(8,128)} %f_ref.3) | copy-start | bytes 786436
  9.9 1.3 %collective-permute-start.3 = (f32[40,256]{1,0:T(8,128)S(1)}, f32[40,256]{1,0:T(8,128)S(1)}, u32[]{:S(2)}, u32[]{:S(2)}) collective-permute-start(f32[40,256]{1,0:T(8,128)S(1)} %relay.1), channel_id=1, source_target_pairs={{0,4},{4,0},{8,12},{12,8},{16,20},{20,16},{24,28},{28,24},{32,36},... | collective-permute-start | bytes 122888 | tf_op jit(solution)/shard_map/ppermute | solution.py:205
  11.8 1.3 %collective-permute-start.5 = (f32[7,8,256]{2,1,0:T(8,128)S(1)}, f32[7,8,256]{2,1,0:T(8,128)S(1)}, u32[]{:S(2)}, u32[]{:S(2)}) collective-permute-start(f32[7,8,256]{2,1,0:T(8,128)S(1)} %get-tuple-element.46.own_ref.ends_ref), channel_id=1, source_target_pairs={{0,4},{4,0},{8,12},{12,8},{16,20},{20,16},{24,28},{28,24},{32,36},... | collective-permute-start | bytes 172040 | tf_op jit(solution)/shard_map/ppermute | solution.py:205
  13.1 7.1 %collective-permute-start.6 = (f32[6,8,256]{2,1,0:T(8,128)S(1)}, f32[6,8,256]{2,1,0:T(8,128)S(1)}, u32[]{:S(2)}, u32[]{:S(2)}) collective-permute-start(f32[6,8,256]{2,1,0:T(8,128)S(1)} %get-tuple-element.47), channel_id=1, source_target_pairs={{0,60},{4,8},{8,4},{12,16},{16,12},{20,24},{24,20},{28,32},{32,28}... | collective-permute-start | bytes 147464 | tf_op jit(solution)/shard_map/ppermute | solution.py:202
  17.3 7.7 %collective-permute-start.8 = (f32[5,8,128]{2,1,0:T(8,128)S(1)}, f32[5,8,128]{2,1,0:T(8,128)S(1)}, u32[]{:S(2)}, u32[]{:S(2)}) collective-permute-start(f32[5,8,128]{2,1,0:T(8,128)S(1)} %get-tuple-element.49), channel_id=1, source_target_pairs={{0,32},{4,36},{8,40},{12,44},{16,48},{20,52},{24,56},{28,60},{32,0... | collective-permute-start | bytes 61448 | tf_op jit(solution)/shard_map/ppermute | solution.py:462
  20.2 6.2 %collective-permute-start.7 = (f32[5,8,256]{2,1,0:T(8,128)S(1)}, f32[5,8,256]{2,1,0:T(8,128)S(1)}, u32[]{:S(2)}, u32[]{:S(2)}) collective-permute-start(f32[5,8,256]{2,1,0:T(8,128)S(1)} %pair.1), channel_id=1, source_target_pairs={{0,16},{4,52},{8,24},{12,60},{16,32},{20,4},{24,40},{28,12},{32,48... | collective-permute-start | bytes 122888 | tf_op jit(solution)/shard_map/ppermute | solution.py:462
  26.5 1.3 %collective-permute-start.9 = (f32[5,8,384]{2,1,0:T(8,128)S(1)}, f32[5,8,384]{2,1,0:T(8,128)S(1)}, u32[]{:S(2)}, u32[]{:S(2)}) collective-permute-start(f32[5,8,384]{2,1,0:T(8,128)S(1)} %side.1.side_ref), channel_id=1, source_target_pairs={{0,4},{4,0},{8,12},{12,8},{16,20},{20,16},{24,28},{28,24},{32,36},... | collective-permute-start | bytes 184328 | tf_op jit(solution)/shard_map/ppermute | solution.py:205
  28.2 5.3 %collective-permute-start.12 = (f32[8,384]{1,0:T(8,128)S(1)}, f32[8,384]{1,0:T(8,128)S(1)}, u32[]{:S(2)}, u32[]{:S(2)}) collective-permute-start(f32[8,384]{1,0:T(8,128)S(1)} %get-tuple-element.54.own_ref), channel_id=1, source_target_pairs={{0,2},{1,3},{2,0},{3,1},{4,6},{5,7},{6,4},{7,5},{8,10},{9,11},{10,... | collective-permute-start | bytes 36872 | tf_op jit(solution)/shard_map/ppermute | solution.py:498
  29.3 4.9 %collective-permute-start.11 = (f32[8,384]{1,0:T(8,128)S(1)}, f32[8,384]{1,0:T(8,128)S(1)}, u32[]{:S(2)}, u32[]{:S(2)}) collective-permute-start(f32[8,384]{1,0:T(8,128)S(1)} %get-tuple-element.54.own_ref), channel_id=1, source_target_pairs={{0,3},{1,2},{2,1},{3,0},{4,7},{5,6},{6,5},{7,4},{8,11},{9,10},{10,... | collective-permute-start | bytes 36872 | tf_op jit(solution)/shard_map/ppermute | solution.py:498
  30.5 3.7 %collective-permute-start.10 = (f32[8,384]{1,0:T(8,128)S(1)}, f32[8,384]{1,0:T(8,128)S(1)}, u32[]{:S(2)}, u32[]{:S(2)}) collective-permute-start(f32[8,384]{1,0:T(8,128)S(1)} %get-tuple-element.54.own_ref), channel_id=1, source_target_pairs={{0,1},{1,0},{2,3},{3,2},{4,5},{5,4},{6,7},{7,6},{8,9},{9,8},{10,11... | collective-permute-start | bytes 36872 | tf_op jit(solution)/shard_map/ppermute | solution.py:498
  34.6 4.1 %collective-permute-start.13 = (f32[32,256]{1,0:T(8,128)S(1)}, f32[32,256]{1,0:T(8,128)S(1)}, u32[]{:S(2)}, u32[]{:S(2)}) collective-permute-start(f32[32,256]{1,0:T(8,128)S(1)} %get-tuple-element.67), channel_id=1, source_target_pairs={{0,64},{4,12},{8,72},{12,4},{16,80},{20,28},{24,88},{28,20},{32,96... | collective-permute-start | bytes 98312 | tf_op jit(solution)/shard_map/ppermute | solution.py:195
  35.8 3.9 %collective-permute-start.14 = (f32[32,256]{1,0:T(8,128)S(1)}, f32[32,256]{1,0:T(8,128)S(1)}, u32[]{:S(2)}, u32[]{:S(2)}) collective-permute-start(f32[32,256]{1,0:T(8,128)S(1)} %get-tuple-element.68), channel_id=1, source_target_pairs={{0,8},{4,68},{8,0},{12,76},{16,24},{20,84},{24,16},{28,92},{32,40}... | collective-permute-start | bytes 98312 | tf_op jit(solution)/shard_map/ppermute | solution.py:195
